TPU v7x, 128 devices: a whole 4x4x4 slice. The times are simulated.
128 devices in a mesh: head: 8 (over x, core), inner: 8 (over z, y_lo), outer: 2 (over y_hi).
Axes of the slice: x: 4, y: 4 (y_hi: 2, y_lo: 2; y = y_hi * 2 + y_lo), z: 4, core: 2. Of those that a mesh axis runs over, the one named last changes fastest.
Arguments:
- queries: bfloat16 [4096, 64, 128], P(('head', 'inner', 'outer')), may hold values from -162 to 162
- keys: bfloat16 [4096, 8, 128], P(('head', 'inner', 'outer')), may hold values from -6 to 6
- values: bfloat16 [4096, 8, 128], P(('head', 'inner', 'outer')), may hold values from -6 to 6
- out_states: bfloat16 [4096, 64, 128], P(('head', 'inner', 'outer')), may hold values from -6 to 6
- out_grads: bfloat16 [4096, 64, 128], P(('head', 'inner', 'outer')), may hold values from -6 to 6
- segment_ids: int32 [4096], replicated, may hold values from 0 to 7, never falling along the last dimension, each value on 1 to 2048 neighbouring positions
- span_position: int32 [128], replicated, may hold values from 0 to 127, each once
Outputs:
- query_grad: bfloat16 [4096, 64, 128], P(('head', 'inner', 'outer'))
- key_grad: bfloat16 [4096, 8, 128], P(('head', 'inner', 'outer'))
- value_grad: bfloat16 [4096, 8, 128], P(('head', 'inner', 'outer'))
All inputs are finite; a program needn't handle non-finite values.
Results may differ from a plain program's by a relative error of at most 0.005.
Values may be sent and summed in bfloat16 or wider, within the bound.
No kernel may reach another device: no remote copies, remote signals or barrier semaphores. Data moves between devices by JAX's collectives and lax.ppermute only.
A program may use at most 64 MiB of HBM per device.

v0:
```python
import math

import jax
import jax.numpy as jnp
from jax import lax
from jax.sharding import PartitionSpec as P

TOK_DEV = 32


def blocks_of(arrays, count):
    width = 512
    return tuple((item.reshape((count // width, width) + item.shape[1:]) for item in arrays))


def shards(queries, keys, values, out_states, out_grads, segment_ids, span_position):
    ctx_count = lax.axis_size(("inner", "outer"))
    ctx_index = lax.axis_index(("inner", "outer"))
    query_rows, key_rows, value_rows, state_rows, grad_rows = (
        lax.all_to_all(queries, "head", split_axis=1, concat_axis=0, tiled=True),
        lax.all_to_all(keys, "head", split_axis=1, concat_axis=0, tiled=True),
        lax.all_to_all(values, "head", split_axis=1, concat_axis=0, tiled=True),
        lax.all_to_all(out_states, "head", split_axis=1, concat_axis=0, tiled=True),
        lax.all_to_all(out_grads, "head", split_axis=1, concat_axis=0, tiled=True),
    )
    row_count = query_rows.shape[0]
    kv_local = key_rows.shape[1]
    group = query_rows.shape[1] // kv_local
    width = query_rows.shape[2]
    scale = 1.0 / math.sqrt(width)
    query_four = query_rows.reshape(row_count, kv_local, group, width)
    grad_four = grad_rows.reshape(row_count, kv_local, group, width)
    state_four = state_rows.reshape(row_count, kv_local, group, width)
    delta = jnp.transpose(
        jnp.sum(grad_four.astype(jnp.float32) * state_four.astype(jnp.float32), axis=-1), (1, 2, 0)
    )

    def places(start, count):
        index = start + jnp.arange(count, dtype=jnp.int32)
        owner = index // row_count
        within = index % row_count
        stored = within // TOK_DEV * ctx_count + owner
        place = span_position[stored] * TOK_DEV + within % TOK_DEV
        return (place, segment_ids[place])

    query_pos, query_doc = places(ctx_index * row_count, row_count)

    def seen(key_pos, key_doc):
        return (query_doc[:, None] == key_doc[None, :]) & (query_pos[:, None] >= key_pos[None, :])

    def stats_block(carry, items):
        key_blk, key_pos, key_doc = items
        visible = seen(key_pos, key_doc)
        top, total = carry
        scores = (
            jnp.einsum("rkgd,lkd->kgrl", query_four, key_blk, preferred_element_type=jnp.float32)
            * scale
        )
        block_top = jnp.max(jnp.where(visible, scores, -1e30), axis=-1)
        new_top = jnp.maximum(top, block_top)
        total = total * jnp.exp(top - new_top) + jnp.sum(
            jnp.where(visible, jnp.exp(scores - new_top[..., None]), 0.0), axis=-1
        )
        return ((new_top, total), None)

    stats_init = (
        jnp.full((kv_local, group, row_count), -1e30, jnp.float32),
        jnp.zeros((kv_local, group, row_count), jnp.float32),
    )
    carry = stats_init
    piece = lax.all_gather(key_rows, ("inner", "outer"), axis=0, tiled=True)
    count = piece.shape[0]
    key_pos, key_doc = places(jnp.int32(0), count)
    carry, unused = lax.scan(stats_block, carry, blocks_of((piece, key_pos, key_doc), count))
    top, total = carry
    lse = top + jnp.log(total)

    def grad_block(query_acc, items):
        key_blk, value_blk, key_pos, key_doc = items
        visible = seen(key_pos, key_doc)
        scores = (
            jnp.einsum("rkgd,lkd->kgrl", query_four, key_blk, preferred_element_type=jnp.float32)
            * scale
        )
        probs = jnp.where(visible, jnp.exp(scores - lse[..., None]), 0.0)
        dprobs = jnp.einsum(
            "rkgd,lkd->kgrl", grad_four, value_blk, preferred_element_type=jnp.float32
        )
        dscore = (probs * (dprobs - delta[..., None])).astype(jnp.bfloat16)
        query_acc = query_acc + jnp.einsum(
            "kgrl,lkd->rkgd", dscore, key_blk, preferred_element_type=jnp.float32
        )
        key_part = jnp.einsum(
            "kgrl,rkgd->lkd", dscore, query_four, preferred_element_type=jnp.float32
        )
        value_part = jnp.einsum(
            "kgrl,rkgd->lkd",
            probs.astype(jnp.bfloat16),
            grad_four,
            preferred_element_type=jnp.float32,
        )
        return (query_acc, (key_part, value_part))

    query_zero = jnp.zeros((row_count, kv_local, group, width), jnp.float32)
    query_acc = query_zero
    sweep_query_acc = query_acc
    key_piece = lax.all_gather(key_rows, ("inner", "outer"), axis=0, tiled=True)
    value_piece = lax.all_gather(value_rows, ("inner", "outer"), axis=0, tiled=True)
    count = key_piece.shape[0]
    key_pos, key_doc = places(jnp.int32(0), count)
    sweep_query_acc, parts = lax.scan(
        grad_block, sweep_query_acc, blocks_of((key_piece, value_piece, key_pos, key_doc), count)
    )
    key_part = parts[0].reshape(key_piece.shape)
    value_part = parts[1].reshape(value_piece.shape)
    query_acc, key_part, value_part = (sweep_query_acc, key_part, value_part)
    key_all = key_part
    value_all = value_part
    query_acc, key_all, value_all = (query_acc, key_all, value_all)
    key_sum, value_sum = (
        lax.psum_scatter(key_all, ("inner", "outer"), scatter_dimension=0, tiled=True),
        lax.psum_scatter(value_all, ("inner", "outer"), scatter_dimension=0, tiled=True),
    )
    query_out = (scale * query_acc).astype(jnp.bfloat16).reshape(row_count, kv_local * group, width)
    key_out = (scale * key_sum).astype(jnp.bfloat16)
    value_out = value_sum.astype(jnp.bfloat16)
    return (
        lax.all_to_all(query_out, "head", split_axis=0, concat_axis=1, tiled=True),
        lax.all_to_all(key_out, "head", split_axis=0, concat_axis=1, tiled=True),
        lax.all_to_all(value_out, "head", split_axis=0, concat_axis=1, tiled=True),
    )


def solution(mesh):
    return jax.shard_map(
        shards,
        mesh=mesh,
        in_specs=(
            P(("head", "inner", "outer"), None, None),
            P(("head", "inner", "outer"), None, None),
            P(("head", "inner", "outer"), None, None),
            P(("head", "inner", "outer"), None, None),
            P(("head", "inner", "outer"), None, None),
            P(),
            P(),
        ),
        out_specs=(
            P(("head", "inner", "outer"), None, None),
            P(("head", "inner", "outer"), None, None),
            P(("head", "inner", "outer"), None, None),
        ),
        check_vma=False,
    )
```

profile of v0, /device:TPU:0, one launch (start us, length us, event | category | flops | bytes accessed | tf_op | source)
XLA Modules:
  0.0 493.7 jit_solution(18366192911536608141)
XLA Ops:
  8.7 4.4 all-to-all-start
  14.6 24.7 %gather_fusion.2 = s32[4096]{0:T(1024)S(1)} fusion(s32[128]{0:T(128)S(1)} %copy-done.1, s32[4096]{0:T(1024)S(1)} %broadcast_clamp_fusion.1), kind=kCustom, calls=%fused_computation.2 | custom fusion | bytes 49152 | tf_op jit(solution)/shard_map/gather | solution.py:43
  39.4 4.9 %all-to-all-start.2 = ((bf16[32,8,128]{2,0,1:T(8,128)(2,1)}), bf16[32,8,128]{2,0,1:T(8,128)(2,1)S(1)}, u32[]{:S(2)}, u32[]{:S(2)}) async-start(bf16[32,8,128]{2,0,1:T(8,128)(2,1)} %copy.81), calls=%async_computation.2 | async-start | bytes 131072 | tf_op jit(solution)/shard_map/all_to_all | solution.py:22
  45.5 4.4 all-to-all-done.2
  49.9 3.5 all-to-all-start.1
  54.7 9.0 %all-to-all-done.1 = bf16[32,64,128]{2,0,1:T(8,128)(2,1)S(1)} async-done(((bf16[32,64,128]{2,0,1:T(8,128)(2,1)}), bf16[32,64,128]{2,0,1:T(8,128)(2,1)S(1)}, u32[]{:S(2)}, u32[]{:S(2)}) %all-to-all-start.1) | async-done | bytes 524320 | tf_op jit(solution)/shard_map/all_to_all | solution.py:20
  63.7 3.5 all-to-all-start.3
  67.2 1.9 gather_fusion
  70.3 7.2 %all-to-all-done.3 = bf16[32,64,128]{2,0,1:T(8,128)(2,1)S(1)} async-done(((bf16[32,64,128]{2,0,1:T(8,128)(2,1)}), bf16[32,64,128]{2,0,1:T(8,128)(2,1)S(1)}, u32[]{:S(2)}, u32[]{:S(2)}) %all-to-all-start.3) | async-done | bytes 524320 | tf_op jit(solution)/shard_map/all_to_all | solution.py:24
  77.5 3.5 all-to-all-start.4
  81.1 1.7 gather_fusion.1
  82.9 23.0 %gather_fusion.3 = s32[4096]{0:T(1024)S(1)} fusion(s32[4096]{0:T(1024)S(1)} %copy-done, s32[4096]{0:T(1024)S(1)} %broadcast_clamp_fusion), kind=kCustom, calls=%fused_computation.3 | custom fusion | bytes 49152 | tf_op jit(solution)/shard_map/gather | solution.py:44
  106.6 18.9 %all-gather.3.cloned.1.call-done = bf16[4096,1,128]{2,0,1:T(8,128)(2,1)} async-done(((bf16[256,1,128]{2,0,1:T(8,128)(2,1)}), bf16[4096,1,128]{2,0,1:T(8,128)(2,1)}) %all-gather.3.cloned.1.call-update) | async-done | bytes 1048592 | tf_op jit(solution)/shard_map/all_gather | solution.py:107
  125.5 55.6 %while.28 = (s32[]{:T(128)}, f32[1,8,256]{2,1,0:T(8,128)S(1)}, f32[1,8,256]{2,1,0:T(8,128)S(1)}, s32[256]{0:T(256)S(1)}, s32[8,512]{1,0:T(8,128)S(1)}, /*index=5...) while((s32[]{:T(128)}, f32[1,8,256]{2,1,0:T(8,128)S(1)}, ...), condition=%wide.region_3.4_spmd.clone, body=%wide.region_0.3_spmd.clone.sunk | while | flops 276178944 | bytes 9558652 | solution.py:74
  125.7 3.6 fusion.85
  129.4 3.0 fusion.86
  132.7 3.6 fusion.85
  136.3 3.1 fusion.86
  139.7 3.6 fusion.85
  143.3 3.1 fusion.86
  146.6 3.6 fusion.85
  150.2 3.1 fusion.86
  153.6 3.6 fusion.85
  157.2 3.0 fusion.86
  160.5 3.6 fusion.85
  164.1 3.0 fusion.86
  167.5 3.6 fusion.85
  171.1 3.1 fusion.86
  174.4 3.6 fusion.85
  178.0 3.0 fusion.86
  181.1 22.4 %all-gather.5.cloned.1.call-done = bf16[4096,1,128]{2,0,1:T(8,128)(2,1)} async-done(((bf16[256,1,128]{2,0,1:T(8,128)(2,1)}), bf16[4096,1,128]{2,0,1:T(8,128)(2,1)}) %all-gather.5.cloned.1.call-update) | async-done | bytes 1048592 | tf_op jit(solution)/shard_map/all_gather | solution.py:108
  203.5 95.4 %while.29 = (s32[]{:T(128)}, f32[256,1,8,128]{0,3,2,1:T(8,128)}, f32[8,512,1,128]{3,1,2,0:T(8,128)}, f32[8,512,1,128]{3,1,2,0:T(8,128)}, bf16[8,512,1,128]{3,1,2...) while((s32[]{:T(128)}, f32[256,1,8,128]{0,3,2,1:T(8,128)}, ...), condition=%wide.region_6.7_spmd.clone, body=%wide.region_5.6_spmd.clone.sunk | while | flops 1353580544 | bytes 57975516 | solution.py:111
  205.4 1.9 copy-done.2
  207.3 2.3 fusion.98
  211.0 2.5 fusion.99
  217.0 1.9 copy-done.2
  218.9 2.3 fusion.98
  222.7 2.9 fusion.99
  229.0 1.9 copy-done.2
  230.9 2.3 fusion.98
  234.6 2.9 fusion.99
  240.9 1.9 copy-done.2
  242.9 2.3 fusion.98
  246.6 2.9 fusion.99
  252.9 1.9 copy-done.2
  254.8 2.3 fusion.98
  258.5 2.9 fusion.99
  264.8 1.9 copy-done.2
  266.8 2.3 fusion.98
  270.5 2.9 fusion.99
  276.8 1.9 copy-done.2
  278.7 2.3 fusion.98
  282.4 2.9 fusion.99
  285.3 1.6 fusion.101
  287.1 1.6 fusion.97
  288.8 1.9 copy-done.2
  290.7 2.3 fusion.98
  294.4 2.9 fusion.99
  301.4 4.3 all-to-all-start.5
  305.7 81.6 %reduce-scatter.3.cloned.1.call-done = f32[256,1,128]{2,1,0:T(1,128)} async-done(((f32[4096,1,128]{2,1,0:T(1,128)}), f32[256,1,128]{2,1,0:T(1,128)}) %reduce-scatter.3.cloned.1.call-update) | async-done | bytes 131088 | tf_op jit(solution)/shard_map/reduce_scatter | solution.py:121
  390.5 4.4 all-to-all-start.6
  394.9 79.1 %reduce-scatter.5.cloned.1.call-done = f32[256,1,128]{2,1,0:T(1,128)} async-done(((f32[4096,1,128]{2,1,0:T(1,128)}), f32[256,1,128]{2,1,0:T(1,128)}) %reduce-scatter.5.cloned.1.call-update) | async-done | bytes 131088 | tf_op jit(solution)/shard_map/reduce_scatter | solution.py:122
  476.7 4.1 all-to-all-start.7
  482.5 3.9 all-to-all-done.7
  (175 shorter events, 55.3 us)
Async XLA Ops:
  7.2 73.9 %copy-start = (s32[4096]{0:T(1024)S(1)}, s32[4096]{0:T(1024)}, u32[]{:S(2)}) copy-start(s32[4096]{0:T(1024)} %param.16) | copy-start | bytes 49156
  7.2 7.4 %copy-start.1 = (s32[128]{0:T(128)S(1)}, s32[128]{0:T(128)}, u32[]{:S(2)}) copy-start(s32[128]{0:T(128)} %param.17) | copy-start | bytes 1540
  8.7 30.7 %all-to-all-start = ((bf16[32,8,128]{2,0,1:T(8,128)(2,1)}), bf16[32,8,128]{2,0,1:T(8,128)(2,1)S(1)}, u32[]{:S(2)}, u32[]{:S(2)}) async-start(bf16[32,8,128]{2,0,1:T(8,128)(2,1)} %copy.77), calls=%async_computation | async-start | bytes 131072 | tf_op jit(solution)/shard_map/all_to_all | solution.py:21
  14.6 29.7 %copy-start.5 = (bf16[32,64,128]{2,1,0:T(8,128)(2,1)S(1)}, bf16[32,64,128]{2,1,0:T(8,128)(2,1)}, u32[]{:S(2)}) copy-start(bf16[32,64,128]{2,1,0:T(8,128)(2,1)} %param.11) | copy-start | bytes 1572868
  14.6 38.9 %copy-start.6 = (bf16[32,64,128]{2,1,0:T(8,128)(2,1)S(1)}, bf16[32,64,128]{2,1,0:T(8,128)(2,1)}, u32[]{:S(2)}) copy-start(bf16[32,64,128]{2,1,0:T(8,128)(2,1)} %param.15) | copy-start | bytes 1572868
  39.3 29.8 %copy-start.7 = (bf16[32,64,128]{2,1,0:T(8,128)(2,1)S(1)}, bf16[32,64,128]{2,1,0:T(8,128)(2,1)}, u32[]{:S(2)}) copy-start(bf16[32,64,128]{2,1,0:T(8,128)(2,1)} %param.14) | copy-start | bytes 1572868
  39.4 6.2 %copy-start.9 = (bf16[32,8,128]{2,0,1:T(8,128)(2,1)}, bf16[32,8,128]{2,0,1:T(8,128)(2,1)S(1)}, u32[]{:S(2)}) copy-start(bf16[32,8,128]{2,0,1:T(8,128)(2,1)S(1)} %all-to-all-done) | copy-start | bytes 196612
  39.4 10.6 %all-to-all-start.2 = ((bf16[32,8,128]{2,0,1:T(8,128)(2,1)}), bf16[32,8,128]{2,0,1:T(8,128)(2,1)S(1)}, u32[]{:S(2)}, u32[]{:S(2)}) async-start(bf16[32,8,128]{2,0,1:T(8,128)(2,1)} %copy.81), calls=%async_computation.2 | async-start | bytes 131072 | tf_op jit(solution)/shard_map/all_to_all | solution.py:22
  44.3 81.2 %all-gather.3.cloned.1.call-start = ((), (), s32[]{:S(2)}) async-start(), calls=%async_computation.10 | async-start | bytes 1114112 | tf_op jit(solution)/shard_map/all_gather | solution.py:107
  49.9 56.0 %copy-start.8 = (bf16[32,8,128]{2,0,1:T(8,128)(2,1)}, bf16[32,8,128]{2,0,1:T(8,128)(2,1)S(1)}, u32[]{:S(2)}) copy-start(bf16[32,8,128]{2,0,1:T(8,128)(2,1)S(1)} %all-to-all-done.2) | copy-start | bytes 196612
  49.9 13.8 %all-to-all-start.1 = ((bf16[32,64,128]{2,0,1:T(8,128)(2,1)}), bf16[32,64,128]{2,0,1:T(8,128)(2,1)S(1)}, u32[]{:S(2)}, u32[]{:S(2)}) async-start(bf16[32,64,128]{2,0,1:T(8,128)(2,1)} %copy.78), calls=%async_computation.1 | async-start | bytes 1048576 | tf_op jit(solution)/shard_map/all_to_all | solution.py:20
  63.7 13.8 %all-to-all-start.3 = ((bf16[32,64,128]{2,0,1:T(8,128)(2,1)}), bf16[32,64,128]{2,0,1:T(8,128)(2,1)S(1)}, u32[]{:S(2)}, u32[]{:S(2)}) async-start(bf16[32,64,128]{2,0,1:T(8,128)(2,1)} %copy.82), calls=%async_computation.3 | async-start | bytes 1048576 | tf_op jit(solution)/shard_map/all_to_all | solution.py:24
  77.5 28.6 %all-to-all-start.4 = ((bf16[32,64,128]{2,0,1:T(8,128)(2,1)}), bf16[32,64,128]{2,0,1:T(8,128)(2,1)S(1)}, u32[]{:S(2)}, u32[]{:S(2)}) async-start(bf16[32,64,128]{2,0,1:T(8,128)(2,1)} %copy.84), calls=%async_computation.4 | async-start | bytes 1048576 | tf_op jit(solution)/shard_map/all_to_all | solution.py:23
  81.0 122.6 %all-gather.5.cloned.1.call-start = ((), (), s32[]{:S(2)}) async-start(), calls=%async_computation.11 | async-start | bytes 1114112 | tf_op jit(solution)/shard_map/all_gather | solution.py:108
  106.0 281.3 %reduce-scatter.3.cloned.1.call-start = ((), (), s32[]{:S(2)}) async-start(), calls=%async_computation.12 | async-start | bytes 2228224 | tf_op jit(solution)/shard_map/reduce_scatter | solution.py:121
  205.4 1.9 copy-start.2
  211.0 2.5 copy-start.3
  217.0 1.9 copy-start.2
  222.6 2.9 copy-start.3
  229.0 1.9 copy-start.2
  234.6 2.9 copy-start.3
  240.9 1.9 copy-start.2
  246.6 2.9 copy-start.3
  252.9 1.9 copy-start.2
  258.5 2.9 copy-start.3
  264.8 1.9 copy-start.2
  270.5 2.9 copy-start.3
  276.8 1.9 copy-start.2
  282.4 2.9 copy-start.3
  288.8 1.9 copy-start.2
  294.4 2.9 copy-start.3
  298.9 1.2 copy-start.4
  298.9 175.1 %reduce-scatter.5.cloned.1.call-start = ((), (), s32[]{:S(2)}) async-start(), calls=%async_computation.13 | async-start | bytes 2228224 | tf_op jit(solution)/shard_map/reduce_scatter | solution.py:122
  301.4 89.1 %all-to-all-start.5 = ((bf16[256,8,128]{2,1,0:T(8,128)(2,1)}), bf16[256,8,128]{2,1,0:T(8,128)(2,1)S(1)}, u32[]{:S(2)}, u32[]{:S(2)}) async-start(bf16[256,8,128]{2,1,0:T(8,128)(2,1)} %fusion.58), calls=%async_computation.5 | async-start | bytes 1048576 | tf_op jit(solution)/shard_map/all_to_all | solution.py:128
  390.5 86.1 %all-to-all-start.6 = ((bf16[8,2,2048]{2,1,0:T(2,128)(2,1)}), bf16[8,2,2048]{2,1,0:T(2,128)(2,1)S(1)}, u32[]{:S(2)}, u32[]{:S(2)}) async-start(bf16[8,2,2048]{2,1,0:T(2,128)(2,1)} %reshape.486), calls=%async_computation.7 | async-start | bytes 131072 | tf_op jit(solution)/shard_map/all_to_all | solution.py:129
  476.7 9.8 %all-to-all-start.7 = ((bf16[8,2,2048]{2,1,0:T(2,128)(2,1)}), bf16[8,2,2048]{2,1,0:T(2,128)(2,1)S(1)}, u32[]{:S(2)}, u32[]{:S(2)}) async-start(bf16[8,2,2048]{2,1,0:T(2,128)(2,1)} %reshape.488), calls=%async_computation.9 | async-start | bytes 131072 | tf_op jit(solution)/shard_map/all_to_all | solution.py:130
Sparse Core Ops, SparseCore 0:
  47.4 78.0 all-gather.2
  127.7 75.7 all-gather.4
  299.0 88.2 reduce-scatter.2
  389.5 84.4 reduce-scatter.4
where the time goes:
time: 496 us; the launch traced here: 494 us
  waiting for transfers between devices  227 us (46%)
  matrix products  107 us (22%)
  local copies, waits for them, and re-layouts  78.7 us (16%)
  other arithmetic  33.4 us (7%)
  starting transfers between devices  32.8 us (7%)
  between operations  14.1 us (3%)
    reduce_scatter x1, waiting for transfers between devices, shards(): lax.psum_scatter(key_all, ('inner', 'outer'), scatter_dimension=0, tiled=...  81.6 us
    reduce_scatter x1, waiting for transfers between devices, shards(): lax.psum_scatter(value_all, ('inner', 'outer'), scatter_dimension=0, tile...  79.1 us
    dot_general x8, matrix products, stats_block(): jnp.einsum('rkgd,lkd->kgrl', query_four, key_blk, preferred_element_type=...  28.9 us
    gather x2, local copies, waits for them, and re-layouts, places(): place = span_position[stored] * TOK_DEV + within % TOK_DEV  26.6 us
    gather x2, local copies, waits for them, and re-layouts, places(): return (place, segment_ids[place])  24.8 us
    reduce_sum x8, other arithmetic, stats_block(): jnp.sum(jnp.where(visible, jnp.exp(scores - new_top[..., None]), 0.0), ax...  24.4 us
    dot_general x8, matrix products, grad_block(): jnp.einsum('kgrl,lkd->rkgd', dscore, key_blk, preferred_element_type=jnp....  22.7 us
    all_gather x1, waiting for transfers between devices, shards(): lax.all_gather(value_rows, ('inner', 'outer'), axis=0, tiled=True)  22.4 us
  transfers between devices with their start and end apart: 12, of which 8 were waited for; matrix products, arithmetic and copies ran while one was open for 25% of the time, Pallas kernels for 0%

commit v1 on v0

v1 whole, which is shorter than its diff:
```python
import functools
import math

import jax
import jax.numpy as jnp
from jax import lax
from jax.experimental import pallas as pl
from jax.experimental.pallas import tpu as pltpu
from jax.sharding import PartitionSpec as P

AXES = ("head", "inner", "outer")
F32 = jnp.float32
BF16 = jnp.bfloat16
TOK = 32
GROUP = 8
ROWS = TOK * GROUP
KV0 = 2 * ROWS
DEL0 = KV0 + 2 * TOK
MSG = DEL0 + 16
TK = 256
LENGTH = 4096
PAD = LENGTH + TK
SPAN = 2048 + TOK + 128 + 2 * TK
LOW = -1e30
NT = (((1,), (1,)), ((), ()))


def linear(x, core, z, y_lo, y_hi):
    return (x * 2 + core) * 16 + (z * 2 + y_lo) * 2 + y_hi


def head_groups():
    return [
        [linear(g >> 1, core, z, (g & 1) ^ y_hi, y_hi) for g in range(8)]
        for core in range(2)
        for z in range(4)
        for y_hi in range(2)
    ]


def seq_groups():
    return [
        [linear(x, core, c >> 1, side ^ (c & 1), c & 1) for c in range(8)]
        for x in range(4)
        for core in range(2)
        for side in range(2)
    ]


def core_pairs():
    return [(i, i ^ 16) for i in range(128)]


def exchange(array, groups):
    return lax.all_to_all(
        array, AXES, split_axis=0, concat_axis=0, axis_index_groups=groups, tiled=True
    )


def dot(a, b):
    return jnp.dot(a, b, preferred_element_type=F32)


def pack_kernel(q_ref, g_ref, o_ref, k_ref, v_ref, out_ref):
    ones = jnp.ones((8, 128), BF16)
    for pair in range(4):
        cols = pl.ds(16 * pair, 16)
        q = q_ref[:, cols, :].astype(F32)
        g = g_ref[:, cols, :].astype(F32)
        prod = g * o_ref[:, cols, :].astype(F32)
        for half in range(2):
            j = 2 * pair + half
            sub = slice(8 * half, 8 * half + 8)
            out_ref[j, 0:ROWS, :] = q[:, sub, :].reshape(ROWS, 128).astype(BF16)
            out_ref[j, ROWS:KV0, :] = g[:, sub, :].reshape(ROWS, 128).astype(BF16)
            part = prod[:, sub, :].reshape(ROWS, 128)
            top = part.astype(BF16)
            rest = (part - top.astype(F32)).astype(BF16)
            delta = lax.dot_general(ones, top, NT, preferred_element_type=F32)
            delta = delta + lax.dot_general(ones, rest, NT, preferred_element_type=F32)
            delta = jnp.concatenate([delta[:, :128], delta[:, 128:]], axis=0)
            first = delta.astype(BF16).astype(F32)
            second = (delta - first).astype(BF16).astype(F32)
            third = delta - first - second
            row = lax.broadcasted_iota(jnp.int32, (16, 128), 0)
            packed = jnp.where(row % 8 == 0, first, jnp.where(row % 8 == 1, second, third))
            out_ref[j, DEL0:MSG, :] = packed.astype(BF16)
            out_ref[j, KV0 : KV0 + TOK, :] = k_ref[j]
            out_ref[j, KV0 + TOK : DEL0, :] = v_ref[j]


def stored_block(core, c, i):
    y_hi = c % 2
    return linear(i // 2, core, c // 2, (i + c) % 2, y_hi)


def attn_kernel(
    span_ref, start_ref, me_ref, msg_ref, kv0_ref, kv1_ref,
    dq_ref, part0_ref, part1_ref,
    k_s, kt_s, v_s, dk_s, dv_s, s_s,
):
    core = me_ref[0]
    mine = me_ref[1]
    scale = 1.0 / math.sqrt(128)
    factor = scale * math.log2(math.e)

    k_s[LENGTH:, :] = jnp.zeros((TK, 128), BF16)
    v_s[LENGTH:, :] = jnp.zeros((TK, 128), BF16)

    def place(n, _):
        c = n // 8
        i = n % 8
        for other, ref in ((0, kv0_ref), (1, kv1_ref)):
            who = (core + other) % 2
            at = pl.multiple_of(span_ref[stored_block(who, c, i)] * TOK, TOK)
            k_s[pl.ds(at, TOK), :] = ref[c, i, 0:TOK, :]
            v_s[pl.ds(at, TOK), :] = ref[c, i, TOK : 2 * TOK, :]
        return 0

    lax.fori_loop(0, 64, place, 0)

    def clear(n, _):
        at = pl.multiple_of(n * TK, TK)
        zero = jnp.zeros((TK, 128), F32)
        dk_s[pl.ds(at, TK), :] = zero
        dv_s[pl.ds(at, TK), :] = zero
        kt_s[:, pl.ds(at, TK)] = k_s[pl.ds(at, TK), :].T
        return 0

    lax.fori_loop(0, PAD // TK, clear, 0)

    def block(i, _):
        base = span_ref[stored_block(core, mine, i)] * TOK
        lane = lax.broadcasted_iota(jnp.int32, (1, ROWS), 1)
        place_q = base + lane // GROUP
        begin = jnp.zeros((1, ROWS), jnp.int32)
        low = jnp.int32(0)
        for s in range(1, 8):
            edge = start_ref[s]
            begin = jnp.where(place_q >= edge, jnp.maximum(begin, edge), begin)
            low = jnp.where(base >= edge, jnp.maximum(low, edge), low)
        first = low // 128 * 128
        tiles = (base + TOK - first + TK - 1) // TK
        q = msg_ref[i, 0:ROWS, :]
        grad = msg_ref[i, ROWS:KV0, :]
        tail = msg_ref[i, DEL0:MSG, :].astype(F32)
        halves = [tail[n : n + 1] + tail[n + 1 : n + 2] + tail[n + 2 : n + 3] for n in (0, 8)]
        delta = jnp.concatenate(halves, axis=1)

        def stats(t, carry):
            top, total = carry
            at = pl.multiple_of(first + t * TK, 128)
            keys = k_s[pl.ds(at, TK), :]
            s = lax.dot_general(keys, q, NT, preferred_element_type=F32) * factor
            pos = at + lax.broadcasted_iota(jnp.int32, (TK, ROWS), 0)
            s = jnp.where((pos <= place_q) & (pos >= begin), s, LOW)
            s_s[pl.ds(pl.multiple_of(t * TK, TK), TK), :] = s
            split = s.reshape(TK // 8, 8, ROWS)
            new = jnp.maximum(top, jnp.max(split, axis=0))
            total = total * jnp.exp2(top - new) + jnp.sum(jnp.exp2(split - new[None]), axis=0)
            return new, total

        top, total = lax.fori_loop(
            0, tiles, stats, (jnp.full((8, ROWS), LOW, F32), jnp.zeros((8, ROWS), F32))
        )
        peak = jnp.max(top, axis=0, keepdims=True)
        total = jnp.sum(total * jnp.exp2(top - peak), axis=0, keepdims=True)
        lse = peak + jnp.log2(total)

        def grads(t, acc):
            at = pl.multiple_of(first + t * TK, 128)
            p = jnp.exp2(s_s[pl.ds(pl.multiple_of(t * TK, TK), TK), :] - lse)
            dp = lax.dot_general(
                v_s[pl.ds(at, TK), :], grad, NT, preferred_element_type=F32
            )
            ds = (p * (dp - delta)).astype(BF16)
            dv_s[pl.ds(at, TK), :] += dot(p.astype(BF16), grad)
            dk_s[pl.ds(at, TK), :] += dot(ds, q)
            return acc + dot(kt_s[:, pl.ds(at, TK)], ds)

        acc = lax.fori_loop(0, tiles, grads, jnp.zeros((128, ROWS), F32))
        dq_ref[i, :, :] = (acc * scale).T.astype(BF16)
        return 0

    lax.fori_loop(0, 8, block, 0)

    def collect(n, _):
        c = n // 8
        i = n % 8
        for other, ref in ((0, part0_ref), (1, part1_ref)):
            who = (core + other) % 2
            at = pl.multiple_of(span_ref[stored_block(who, c, i)] * TOK, TOK)
            ref[c, i, 0:TOK, :] = (dk_s[pl.ds(at, TOK), :] * scale).astype(BF16)
            ref[c, i, TOK : 2 * TOK, :] = dv_s[pl.ds(at, TOK), :].astype(BF16)
        return 0

    lax.fori_loop(0, 64, collect, 0)


def vmem():
    return pl.BlockSpec(memory_space=pltpu.VMEM)


def smem():
    return pl.BlockSpec(memory_space=pltpu.SMEM)


def shards(queries, keys, values, out_states, out_grads, segment_ids, span_position):
    head = lax.axis_index("head")
    inner = lax.axis_index("inner")
    outer = lax.axis_index("outer")
    me = jnp.stack([head % 2, inner // 2 * 2 + outer]).astype(jnp.int32)
    starts = jnp.sum(
        segment_ids[None, :] < jnp.arange(8, dtype=jnp.int32)[:, None], axis=1, dtype=jnp.int32
    )
    message = pl.pallas_call(
        pack_kernel,
        out_shape=jax.ShapeDtypeStruct((8, MSG, 128), BF16),
        in_specs=[vmem()] * 5,
        out_specs=vmem(),
        compiler_params=pltpu.CompilerParams(vmem_limit_bytes=32 << 20),
        name="pack",
    )(queries, out_grads, out_states, keys.transpose(1, 0, 2), values.transpose(1, 0, 2))
    message = exchange(message, head_groups())
    kv_part = message[:, KV0:DEL0, :]
    kv_mine = exchange(
        jnp.broadcast_to(kv_part[None], (8, 8, 2 * TOK, 128)), seq_groups()
    )
    kv_other = lax.ppermute(kv_mine, AXES, core_pairs())
    kv_shape = jax.ShapeDtypeStruct((8, 8, 2 * TOK, 128), BF16)
    dq, part_mine, part_other = pl.pallas_call(
        attn_kernel,
        out_shape=(jax.ShapeDtypeStruct((8, ROWS, 128), BF16), kv_shape, kv_shape),
        in_specs=[smem()] * 3 + [vmem()] * 3,
        out_specs=(vmem(),) * 3,
        scratch_shapes=[
            pltpu.VMEM((PAD, 128), BF16),
            pltpu.VMEM((128, PAD), BF16),
            pltpu.VMEM((PAD, 128), BF16),
            pltpu.VMEM((PAD, 128), F32),
            pltpu.VMEM((PAD, 128), F32),
            pltpu.VMEM((SPAN, ROWS), F32),
        ],
        compiler_params=pltpu.CompilerParams(vmem_limit_bytes=48 << 20),
        name="attention",
    )(span_position, starts, me, message, kv_mine, kv_other)
    theirs = lax.ppermute(part_other, AXES, core_pairs())
    part = (part_mine.astype(F32) + theirs.astype(F32)).astype(BF16)
    part = exchange(part, seq_groups())
    total = jnp.sum(part.astype(F32), axis=0).astype(BF16)
    back = exchange(jnp.concatenate([dq, total], axis=1), head_groups())
    query_grad = back[:, :ROWS].reshape(8, TOK, GROUP, 128).transpose(1, 0, 2, 3)
    return (
        query_grad.reshape(TOK, 64, 128),
        back[:, ROWS : ROWS + TOK].transpose(1, 0, 2),
        back[:, ROWS + TOK :].transpose(1, 0, 2),
    )


def solution(mesh):
    spec = P(AXES, None, None)
    return jax.shard_map(
        shards,
        mesh=mesh,
        in_specs=(spec,) * 5 + (P(), P()),
        out_specs=(spec,) * 3,
        check_vma=False,
    )
```

time: 496 us -> 124 us (0.25)
  waiting for transfers between devices: 227 us -> 4.72 us
  matrix products: 107 us -> 0 us
  blocking collectives: 0 us -> 86 us
  local copies, waits for them, and re-layouts: 78.7 us -> 7.4 us
  other arithmetic: 33.4 us -> 0.87 us
  starting transfers between devices: 32.8 us -> 2.8 us
  Pallas kernels: 0 us -> 21.6 us
  between operations: 14.1 us -> 0.73 us
    reduce_scatter x2 -> x0, waiting for transfers between devices: 161 us -> none  [the longest x1 81.6 us: shards(): lax.psum_scatter(key_all, ('inner', 'outer'), scatter_dimension=0, tiled=...]
    dot_general x48 -> x0, matrix products: 107 us -> none  [the longest x8 28.9 us: stats_block(): jnp.einsum('rkgd,lkd->kgrl', query_four, key_blk, preferred_element_type=...]
    all_to_all x0 -> x4, blocking collectives: none -> 86 us  [exchange(): lax.all_to_all(array, AXES, split_axis=0, concat_axis=0, axis_index_group...]
    gather x4 -> x0, local copies, waits for them, and re-layouts: 51.3 us -> none  [the longest x2 26.6 us: places(): place = span_position[stored] * TOK_DEV + within % TOK_DEV]
    all_gather x2 -> x0, waiting for transfers between devices: 41.3 us -> none  [the longest x1 22.4 us: shards(): lax.all_gather(value_rows, ('inner', 'outer'), axis=0, tiled=True)]
    all_to_all x8 -> x0, starting transfers between devices: 32.7 us -> none  [the longest x1 4.95 us: shards(): lax.all_to_all(values, 'head', split_axis=1, concat_axis=0, tiled=True)]
    all_to_all x8 -> x0, waiting for transfers between devices: 24.6 us -> none  [the longest x1 9.04 us: shards(): lax.all_to_all(queries, 'head', split_axis=1, concat_axis=0, tiled=True)]
    reduce_sum x9 -> x2, other arithmetic: 24.8 us -> 0.33 us  [the longest x1 0.18 us: shards(): total = jnp.sum(part.astype(F32), axis=0).astype(BF16)]
  transfers between devices with their start and end apart: 12 -> 2, of which waited for: 8 -> 2; matrix products, arithmetic and copies ran while one was open for 25% -> 0% of each run, Pallas kernels for 0% -> 0%
where the time goes in v1:
time: 124 us
  blocking collectives  86 us (69%)
  Pallas kernels  21.6 us (17%)
  local copies, waits for them, and re-layouts  7.4 us (6%)
  waiting for transfers between devices  4.72 us (4%)
  starting transfers between devices  2.8 us (2%)
    all_to_all x4, blocking collectives, exchange(): lax.all_to_all(array, AXES, split_axis=0, concat_axis=0, axis_index_group...  86 us
    pallas_call x1, Pallas kernels, shards(): pl.pallas_call(attn_kernel, out_shape=(jax.ShapeDtypeStruct((8, ROWS, 128...  21.1 us
    unnamed x16, local copies, waits for them, and re-layouts  5.31 us
    ppermute x1, starting transfers between devices, shards(): theirs = lax.ppermute(part_other, AXES, core_pairs())  2.8 us
  transfers between devices with their start and end apart: 2, of which 2 were waited for; matrix products, arithmetic and copies ran while one was open for 0% of the time, Pallas kernels for 0%

profile of v1, /device:TPU:0, one launch (start us, length us, event | category | flops | bytes accessed | tf_op | source)
XLA Modules:
  0.0 124.1 jit_solution(10064083673048431073)
XLA Ops:
  0.6 0.9 copy_bitcast_fusion.1
  1.5 0.0 copy-start.2
  1.5 1.0 copy-done.2
  2.6 0.0 copy-start.3
  2.6 1.0 copy-done.3
  3.6 0.0 copy-start.4
  3.6 1.0 copy-done.4
  4.7 0.5 pack.1
  5.1 22.4 %all_to_all.20.msg_ref = bf16[8,592,128]{2,1,0:T(8,128)(2,1)S(1)} all-to-all(bf16[8,592,128]{2,1,0:T(8,128)(2,1)S(1)} %pack.1), channel_id=1, replica_groups={{0,2,32,34,64,66,96,98},{3,1,35,33,67,65,99,97},{4,6,36,38,68,70,100,10..., dimensions={0} | all-to-all | bytes 2424832 | tf_op jit(solution)/shard_map/all_to_all | solution.py:55
  27.6 0.2 broadcast_in_dim.2
  27.8 0.0 copy-start.6
  27.9 0.0 copy-start.5
  27.9 22.3 %all_to_all.21.kv0_ref = bf16[8,8,64,128]{3,2,1,0:T(8,128)(2,1)S(1)} all-to-all(bf16[8,8,64,128]{3,2,1,0:T(8,128)(2,1)S(1)} %broadcast_in_dim.2), channel_id=1, replica_groups={{0,3,4,7,8,11,12,15},{2,1,6,5,10,9,14,13},{16,19,20,23,24,27,28,31},{18..., dimensions={0} | all-to-all | bytes 2097152 | tf_op jit(solution)/shard_map/all_to_all | solution.py:55
  50.2 0.0 collective-permute-start
  50.2 0.1 pad_add_fusion.me_ref
  50.2 0.0 copy-done.6
  50.2 0.1 convert_reduce_fusion.start_ref
  50.4 2.4 %collective-permute-done.kv1_ref = bf16[8,8,64,128]{3,2,1,0:T(8,128)(2,1)S(1)} collective-permute-done((bf16[8,8,64,128]{3,2,1,0:T(8,128)(2,1)S(1)}, bf16[8,8,64,128]{3,2,1,0:T(8,128)(2,1)S(1)}, u32[]{:S(2)}, u32[]{:S(2)}) %collective-permute-start) | collective-permute-done | bytes 1048608 | tf_op jit(solution)/shard_map/ppermute | solution.py:229
  52.8 0.0 copy-done.5
  52.8 21.1 %attention.1 = (bf16[8,256,128]{2,1,0:T(8,128)(2,1)S(1)}, bf16[8,8,64,128]{3,2,1,0:T(8,128)(2,1)S(1)}, bf16[8,8,64,128]{3,2,1,0:T(8,128)(2,1)S(1)}) custom-call(s32[128]{0:T(128)S(1)} %copy-done.5, s32[8]{0:T(128)S(1)} %convert_reduce_fusion.start_ref, s32[2]{0:T(128)S(1)} %pad_add_fusion.me_ref, bf16[8,592,128]{2,1,0:T(8,128)(2,1)S(1)} %all_to_all.20.msg_ref, ...), custom_call_target="tpu_custom_call" | custom-call | tf_op jit(solution)/shard_map/attention/pallas_call | solution.py:231
  73.9 0.0 copy-start
  73.9 2.8 %collective-permute-start.1 = (bf16[8,8,64,128]{3,2,1,0:T(8,128)(2,1)S(1)}, bf16[8,8,64,128]{3,2,1,0:T(8,128)(2,1)S(1)}, u32[]{:S(2)}, u32[]{:S(2)}) collective-permute-start(bf16[8,8,64,128]{3,2,1,0:T(8,128)(2,1)S(1)} %get-tuple-element.8), channel_id=1, source_target_pairs={{0,16},{1,17},{2,18},{3,19},{4,20},{5,21},{6,22},{7,23},{8,24},{9,... | collective-permute-start | bytes 3145736 | tf_op jit(solution)/shard_map/ppermute | solution.py:247
  76.7 2.3 %collective-permute-done.1 = bf16[8,8,64,128]{3,2,1,0:T(8,128)(2,1)S(1)} collective-permute-done((bf16[8,8,64,128]{3,2,1,0:T(8,128)(2,1)S(1)}, bf16[8,8,64,128]{3,2,1,0:T(8,128)(2,1)S(1)}, u32[]{:S(2)}, u32[]{:S(2)}) %collective-permute-start.1) | collective-permute-done | bytes 1048608 | tf_op jit(solution)/shard_map/ppermute | solution.py:247
  79.0 0.4 add_convert_fusion
  79.5 0.0 copy-done
  79.5 27.8 %all_to_all.22 = bf16[8,8,64,128]{3,2,1,0:T(8,128)(2,1)S(1)} all-to-all(bf16[8,8,64,128]{3,2,1,0:T(8,128)(2,1)S(1)} %add_convert_fusion), channel_id=1, replica_groups={{0,3,4,7,8,11,12,15},{2,1,6,5,10,9,14,13},{16,19,20,23,24,27,28,31},{18..., dimensions={0} | all-to-all | bytes 2097152 | tf_op jit(solution)/shard_map/all_to_all | solution.py:55
  107.2 0.0 copy-start.1
  107.2 0.2 reduce_sum.22
  107.4 0.9 copy-done.1
  108.3 13.5 %all_to_all.23 = bf16[8,320,128]{2,1,0:T(8,128)(2,1)S(1)} all-to-all(bf16[8,320,128]{2,1,0:T(8,128)(2,1)S(1)} %pad_maximum_fusion), channel_id=1, replica_groups={{0,2,32,34,64,66,96,98},{3,1,35,33,67,65,99,97},{4,6,36,38,68,70,100,10..., dimensions={0} | all-to-all | bytes 1310720 | tf_op jit(solution)/shard_map/all_to_all | solution.py:55
  121.8 0.7 copy.19
  122.5 0.7 copy.18
  123.1 0.9 copy_bitcast_fusion
  (3 shorter events, 0.1 us)
Async XLA Ops:
  1.5 1.0 copy-start.2
  2.6 1.0 copy-start.3
  3.6 1.0 copy-start.4
  27.8 22.4 %copy-start.6 = (s32[4096]{0:T(1024)S(1)}, s32[4096]{0:T(1024)}, u32[]{:S(2)}) copy-start(s32[4096]{0:T(1024)} %param.12) | copy-start | bytes 49156
  27.9 25.0 %copy-start.5 = (s32[128]{0:T(128)S(1)}, s32[128]{0:T(128)}, u32[]{:S(2)}) copy-start(s32[128]{0:T(128)} %span_ref.1) | copy-start | bytes 1540
  50.2 2.7 %collective-permute-start = (bf16[8,8,64,128]{3,2,1,0:T(8,128)(2,1)S(1)}, bf16[8,8,64,128]{3,2,1,0:T(8,128)(2,1)S(1)}, u32[]{:S(2)}, u32[]{:S(2)}) collective-permute-start(bf16[8,8,64,128]{3,2,1,0:T(8,128)(2,1)S(1)} %all_to_all.21.kv0_ref), channel_id=1, source_target_pairs={{0,16},{1,17},{2,18},{3,19},{4,20},{5,21},{6,22},{7,23},{8,24},{9,... | collective-permute-start | bytes 3145736 | tf_op jit(solution)/shard_map/ppermute | solution.py:229
  73.9 5.5 %copy-start = (bf16[8,256,128]{2,1,0:T(8,128)(2,1)}, bf16[8,256,128]{2,1,0:T(8,128)(2,1)S(1)}, u32[]{:S(2)}) copy-start(bf16[8,256,128]{2,1,0:T(8,128)(2,1)S(1)} %get-tuple-element.6) | copy-start | bytes 1572868
  73.9 5.1 %collective-permute-start.1 = (bf16[8,8,64,128]{3,2,1,0:T(8,128)(2,1)S(1)}, bf16[8,8,64,128]{3,2,1,0:T(8,128)(2,1)S(1)}, u32[]{:S(2)}, u32[]{:S(2)}) collective-permute-start(bf16[8,8,64,128]{3,2,1,0:T(8,128)(2,1)S(1)} %get-tuple-element.8), channel_id=1, source_target_pairs={{0,16},{1,17},{2,18},{3,19},{4,20},{5,21},{6,22},{7,23},{8,24},{9,... | collective-permute-start | bytes 3145736 | tf_op jit(solution)/shard_map/ppermute | solution.py:247
  107.2 1.0 copy-start.1

commit v2 on v1

v2 whole, which is shorter than its diff:
```python
import math

import jax
import jax.numpy as jnp
from jax import lax
from jax.experimental import pallas as pl
from jax.experimental.pallas import tpu as pltpu
from jax.sharding import PartitionSpec as P

AXES = ("head", "inner", "outer")
F32 = jnp.float32
BF16 = jnp.bfloat16
I32 = jnp.int32
TOK = 32
HEADS = 64
MSG = 4 * TOK + 8
BACK = 3 * TOK
TK = 256
TQ = 256
BLOCKS = TQ // TOK
LENGTH = 4096
PAD = LENGTH + TK
LOW = -1e30
NT = (((1,), (1,)), ((), ()))


def linear(x, core, z, y_lo, y_hi):
    return (x * 2 + core) * 16 + (z * 2 + y_lo) * 2 + y_hi


def owner(core, rank):
    g = rank // 8
    c = rank % 8
    return linear(g // 2, core, c // 2, (g + c) % 2, c % 2)


def chip_groups():
    return [[owner(core, rank) for rank in range(64)] for core in range(2)]


def core_pairs():
    return [(i, i ^ 16) for i in range(128)]


def exchange(array):
    return lax.all_to_all(
        array, AXES, split_axis=0, concat_axis=0, axis_index_groups=chip_groups(), tiled=True
    )


def dot(a, b):
    return jnp.dot(a, b, preferred_element_type=F32)


def pack_kernel(q_hbm, g_hbm, o_hbm, k_hbm, v_hbm, out_ref, q_v, g_v, o_v, k_v, v_v, wide, sem):
    copies = []
    for n, (src, dst) in enumerate(
        ((g_hbm, g_v), (o_hbm, o_v), (q_hbm, q_v), (k_hbm, k_v), (v_hbm, v_v))
    ):
        copy = pltpu.make_async_copy(src, dst, sem.at[n])
        copy.start()
        copies.append(copy)
    copies[0].wait()
    copies[1].wait()
    lane = lax.broadcasted_iota(I32, (HEADS, 128), 1) % TOK
    ones = jnp.ones((128, 128), BF16)

    def token(t, delta):
        prod = g_v[t].astype(F32) * o_v[t].astype(F32)
        top = prod.astype(BF16)
        rest = (prod - top.astype(F32)).astype(BF16)
        return jnp.where(lane == t, dot(top, ones) + dot(rest, ones), delta)

    delta = lax.fori_loop(0, TOK, token, jnp.zeros((HEADS, 128), F32))
    first = delta.astype(BF16).astype(F32)
    second = (delta - first).astype(BF16).astype(F32)
    third = delta - first - second
    row = lax.broadcasted_iota(I32, (8, 128), 0)
    for h in range(HEADS):
        at = slice(h, h + 1)
        tile = jnp.where(row == 0, first[at], jnp.where(row == 1, second[at], third[at]))
        out_ref[h, 4 * TOK :, :] = tile.astype(BF16)
    for n, ref in ((1, g_v), (0, q_v)):
        if n == 0:
            copies[2].wait()
        wide[...] = ref[...].reshape(TOK * HEADS, 128).astype(F32)
        for h in range(HEADS):
            out_ref[h, n * TOK : n * TOK + TOK, :] = wide[pl.ds(h, TOK, HEADS), :].astype(BF16)
    for n, ref in ((2, k_v), (3, v_v)):
        copies[n + 1].wait()
        wide[0 : TOK * 8, :] = ref[...].reshape(TOK * 8, 128).astype(F32)
        for g in range(8):
            part = wide[pl.ds(g, TOK, 8), :].astype(BF16)
            for c in range(8):
                out_ref[g * 8 + c, n * TOK : n * TOK + TOK, :] = part


def attn_kernel(
    span_ref, start_ref, rank_ref, me_ref, msg_ref, kv_ref,
    dq_ref, mine_ref, other_ref,
    q_s, g_s, d_s, pos_s, from_s, k_s, kt_s, v_s, dk_s, dv_s, s_s,
):
    core = me_ref[0]
    scale = 1.0 / math.sqrt(128)
    factor = scale * math.log2(math.e)

    k_s[LENGTH:, :] = jnp.zeros((TK, 128), BF16)
    v_s[LENGTH:, :] = jnp.zeros((TK, 128), BF16)

    def place(r, _):
        block = owner(core, r)
        at = pl.multiple_of(span_ref[block] * TOK, TOK)
        k_s[pl.ds(at, TOK), :] = msg_ref[r, 2 * TOK : 3 * TOK, :]
        v_s[pl.ds(at, TOK), :] = msg_ref[r, 3 * TOK : 4 * TOK, :]
        slot = rank_ref[block // 32 * 16 + block % 16]
        pos_s[slot] = span_ref[block] * TOK
        from_s[slot] = r
        row = pl.multiple_of(slot * TOK, TOK)
        q_s[pl.ds(row, TOK), :] = msg_ref[r, 0:TOK, :]
        g_s[pl.ds(row, TOK), :] = msg_ref[r, TOK : 2 * TOK, :]
        d_s[pl.ds(pl.multiple_of(slot * 8, 8), 8), :] = msg_ref[r, 4 * TOK :, :].astype(F32)
        at = pl.multiple_of(span_ref[owner(1 - core, r)] * TOK, TOK)
        k_s[pl.ds(at, TOK), :] = kv_ref[r, 0:TOK, :]
        v_s[pl.ds(at, TOK), :] = kv_ref[r, TOK : 2 * TOK, :]
        return 0

    lax.fori_loop(0, 64, place, 0)

    def clear(n, _):
        at = pl.multiple_of(n * TK, TK)
        zero = jnp.zeros((TK, 128), F32)
        dk_s[pl.ds(at, TK), :] = zero
        dv_s[pl.ds(at, TK), :] = zero
        kt_s[:, pl.ds(at, TK)] = k_s[pl.ds(at, TK), :].T
        return 0

    lax.fori_loop(0, PAD // TK, clear, 0)

    lane = lax.broadcasted_iota(I32, (1, TQ), 1)
    sub = lax.broadcasted_iota(I32, (8, TQ), 0)
    step = lax.broadcasted_iota(I32, (TK // 8, 8, TQ), 0) * 8

    def tile(i, _):
        slot = i * BLOCKS
        lead = jnp.zeros((1, TQ), I32)
        parts = []
        for j in range(BLOCKS):
            lead = jnp.where(lane // TOK == j, pos_s[slot + j], lead)
            d = d_s[pl.ds(pl.multiple_of((slot + j) * 8, 8), 8), :]
            parts.append(d[0:1] + d[1:2] + d[2:3])
        small = lane[:, :128] // TOK
        sides = []
        for n in range(0, BLOCKS, 4):
            side = parts[n]
            for j in range(1, 4):
                side = jnp.where(small == j, parts[n + j], side)
            sides.append(side)
        delta = jnp.concatenate(sides, axis=1)
        place_q = lead + lane % TOK
        begin = jnp.zeros((1, TQ), I32)
        low = jnp.int32(0)
        base = pos_s[slot]
        for s in range(1, 8):
            edge = start_ref[s]
            begin = jnp.where(place_q >= edge, jnp.maximum(begin, edge), begin)
            low = jnp.where(base >= edge, jnp.maximum(low, edge), low)
        first = low // 128 * 128
        tiles = (pos_s[slot + BLOCKS - 1] + TOK - first + TK - 1) // TK
        rows = pl.ds(pl.multiple_of(slot * TOK, TQ), TQ)
        q = q_s[rows, :]
        grad = g_s[rows, :]

        def stats(t, carry):
            top, total = carry
            at = pl.multiple_of(first + t * TK, 128)
            s = lax.dot_general(k_s[pl.ds(at, TK), :], q, NT, preferred_element_type=F32)
            s = (s * factor).reshape(TK // 8, 8, TQ)
            upper = place_q - at - sub
            lower = begin - at - sub
            s = jnp.where((step <= upper[None]) & (step >= lower[None]), s, LOW)
            s_s[pl.ds(pl.multiple_of(t * TK, TK), TK), :] = s.reshape(TK, TQ)
            new = jnp.maximum(top, jnp.max(s, axis=0))
            total = total * jnp.exp2(top - new) + jnp.sum(jnp.exp2(s - new[None]), axis=0)
            return new, total

        top, total = lax.fori_loop(
            0, tiles, stats, (jnp.full((8, TQ), LOW, F32), jnp.zeros((8, TQ), F32))
        )
        peak = jnp.max(top, axis=0, keepdims=True)
        total = jnp.sum(total * jnp.exp2(top - peak), axis=0, keepdims=True)
        lse = peak + jnp.log2(total)

        def grads(t, acc):
            at = pl.multiple_of(first + t * TK, 128)
            p = jnp.exp2(s_s[pl.ds(pl.multiple_of(t * TK, TK), TK), :] - lse)
            dp = lax.dot_general(v_s[pl.ds(at, TK), :], grad, NT, preferred_element_type=F32)
            ds = (p * (dp - delta)).astype(BF16)
            dv_s[pl.ds(at, TK), :] += dot(p.astype(BF16), grad)
            dk_s[pl.ds(at, TK), :] += dot(ds, q)
            return acc + dot(kt_s[:, pl.ds(at, TK)], ds)

        acc = lax.fori_loop(0, tiles, grads, jnp.zeros((128, TQ), F32))
        out = (acc * scale).T.astype(BF16)
        for j in range(BLOCKS):
            dq_ref[from_s[slot + j], :, :] = out[j * TOK : j * TOK + TOK]
        return 0

    lax.fori_loop(0, 64 // BLOCKS, tile, 0)

    def collect(r, _):
        at = pl.multiple_of(span_ref[owner(core, r)] * TOK, TOK)
        mine_ref[r, 0:TOK, :] = dk_s[pl.ds(at, TOK), :] * scale
        mine_ref[r, TOK : 2 * TOK, :] = dv_s[pl.ds(at, TOK), :]
        at = pl.multiple_of(span_ref[owner(1 - core, r)] * TOK, TOK)
        other_ref[r, 0:TOK, :] = (dk_s[pl.ds(at, TOK), :] * scale).astype(BF16)
        other_ref[r, TOK : 2 * TOK, :] = dv_s[pl.ds(at, TOK), :].astype(BF16)
        return 0

    lax.fori_loop(0, 64, collect, 0)


def vmem():
    return pl.BlockSpec(memory_space=pltpu.VMEM)


def smem():
    return pl.BlockSpec(memory_space=pltpu.SMEM)


def hbm():
    return pl.BlockSpec(memory_space=pl.ANY)


def pack(queries, out_grads, out_states, keys, values):
    return pl.pallas_call(
        pack_kernel,
        out_shape=jax.ShapeDtypeStruct((HEADS, MSG, 128), BF16),
        in_specs=[hbm()] * 5,
        out_specs=vmem(),
        scratch_shapes=[pltpu.VMEM((TOK, HEADS, 128), BF16)] * 3
        + [pltpu.VMEM((TOK, 8, 128), BF16)] * 2
        + [pltpu.VMEM((TOK * HEADS, 128), F32), pltpu.SemaphoreType.DMA((5,))],
        compiler_params=pltpu.CompilerParams(vmem_limit_bytes=32 << 20),
        name="pack",
    )(queries, out_grads, out_states, keys, values)


def attention(span_position, starts, rank, me, message, kv_other):
    return pl.pallas_call(
        attn_kernel,
        out_shape=(
            jax.ShapeDtypeStruct((HEADS, TOK, 128), BF16),
            jax.ShapeDtypeStruct((HEADS, 2 * TOK, 128), F32),
            jax.ShapeDtypeStruct((HEADS, 2 * TOK, 128), BF16),
        ),
        in_specs=[smem()] * 4 + [vmem()] * 2,
        out_specs=(vmem(),) * 3,
        scratch_shapes=[
            pltpu.VMEM((64 * TOK, 128), BF16),
            pltpu.VMEM((64 * TOK, 128), BF16),
            pltpu.VMEM((64 * 8, 128), F32),
            pltpu.SMEM((64,), I32),
            pltpu.SMEM((64,), I32),
            pltpu.VMEM((PAD, 128), BF16),
            pltpu.VMEM((128, PAD), BF16),
            pltpu.VMEM((PAD, 128), BF16),
            pltpu.VMEM((PAD, 128), F32),
            pltpu.VMEM((PAD, 128), F32),
            pltpu.VMEM((PAD, TQ), F32),
        ],
        compiler_params=pltpu.CompilerParams(vmem_limit_bytes=48 << 20),
        name="attention",
    )(span_position, starts, rank, me, message, kv_other)


def shards(queries, keys, values, out_states, out_grads, segment_ids, span_position):
    core = lax.axis_index("head") % 2
    starts = jnp.sum(
        segment_ids[None, :] < jnp.arange(8, dtype=I32)[:, None], axis=1, dtype=I32
    )
    own = lax.dynamic_index_in_dim(span_position.reshape(4, 2, 16), core, 1, False).reshape(64)
    rank = jnp.sum(own[None, :] < own[:, None], axis=1, dtype=I32)
    message = exchange(pack(queries, out_grads, out_states, keys, values))
    kv_other = lax.ppermute(message[:, 2 * TOK : 4 * TOK, :], AXES, core_pairs())
    dq, mine, other = attention(
        span_position, starts, rank, core.astype(I32).reshape(1), message, kv_other
    )
    theirs = lax.ppermute(other, AXES, core_pairs())
    part = (mine + theirs.astype(F32)).astype(BF16)
    back = exchange(jnp.concatenate([dq, part], axis=1))
    sums = jnp.sum(back[:, TOK:].reshape(8, 8, 2, TOK, 128).astype(F32), axis=1).astype(BF16)
    return (
        back[:, :TOK].transpose(1, 0, 2),
        sums[:, 0].transpose(1, 0, 2),
        sums[:, 1].transpose(1, 0, 2),
    )


def solution(mesh):
    spec = P(AXES, None, None)
    return jax.shard_map(
        shards,
        mesh=mesh,
        in_specs=(spec,) * 5 + (P(), P()),
        out_specs=(spec,) * 3,
        check_vma=False,
    )
```

time: 124 us -> 127 us (1.024)
  Pallas kernels: 21.6 us -> 37.2 us
  blocking collectives: 86 us -> 72.7 us
  local copies, waits for them, and re-layouts: 7.4 us -> 8.75 us
  starting transfers between devices: 2.8 us -> 1.51 us
    pallas_call x2, Pallas kernels: 21.6 us -> 37.2 us  [the longest x1 31 us: attention(): pl.pallas_call(attn_kernel, out_shape=(jax.ShapeDtypeStruct((HEADS, TOK,...]
    all_to_all x4 -> x2, blocking collectives: 86 us -> 72.7 us  [exchange(): lax.all_to_all(array, AXES, split_axis=0, concat_axis=0, axis_index_group...]
    unnamed x16 -> x19, local copies, waits for them, and re-layouts: 5.31 us -> 7.12 us
    slice x1 -> x2, local copies, waits for them, and re-layouts: 0.01 us -> 1.39 us  [the longest x1 1.25 us: shards(): kv_other = lax.ppermute(message[:, 2 * TOK:4 * TOK, :], AXES, core_pairs())]
    ppermute x2, starting transfers between devices: 2.8 us -> 1.51 us  [the longest x1 1.51 us: shards(): theirs = lax.ppermute(other, AXES, core_pairs())]
where the time goes in v2:
time: 127 us
  blocking collectives  72.7 us (57%)
  Pallas kernels  37.2 us (29%)
  local copies, waits for them, and re-layouts  8.75 us (7%)
  waiting for transfers between devices  4.62 us (4%)
  starting transfers between devices  1.51 us (1%)
    all_to_all x2, blocking collectives, exchange(): lax.all_to_all(array, AXES, split_axis=0, concat_axis=0, axis_index_group...  72.7 us
    pallas_call x1, Pallas kernels, attention(): pl.pallas_call(attn_kernel, out_shape=(jax.ShapeDtypeStruct((HEADS, TOK,...  31 us
    unnamed x19, local copies, waits for them, and re-layouts  7.12 us
    pallas_call x1, Pallas kernels, pack(): pl.pallas_call(pack_kernel, out_shape=jax.ShapeDtypeStruct((HEADS, MSG, 1...  6.21 us
  transfers between devices with their start and end apart: 2, of which 2 were waited for; matrix products, arithmetic and copies ran while one was open for 0% of the time, Pallas kernels for 0%

profile of v2, /device:TPU:0, one launch (start us, length us, event | category | flops | bytes accessed | tf_op | source)
XLA Modules:
  0.0 126.5 jit_solution(4484204498610547375)
XLA Ops:
  0.6 0.0 copy-start
  0.6 1.0 copy-done
  1.7 0.0 copy-start.1
  1.7 1.0 copy-done.1
  2.7 0.0 copy-start.2
  2.7 1.0 copy-done.2
  3.8 0.0 copy-start.3
  3.8 0.8 copy-done.3
  4.6 0.0 copy-start.4
  4.6 0.8 copy-done.4
  5.4 6.2 %pack.1 = bf16[64,136,128]{2,1,0:T(8,128)(2,1)S(1)} custom-call(bf16[32,64,128]{2,1,0:T(8,128)(2,1)S(1)} %copy-done, bf16[32,64,128]{2,1,0:T(8,128)(2,1)S(1)} %copy-done.1, bf16[32,64,128]{2,1,0:T(8,128)(2,1)S(1)} %copy-done.2, bf16[32,8,128]{2,1,0:T(8,128)(2,1)S(1)} %copy-done.3, bf16[32,8,128]{2,1,0:T(8,128)(2,1)S(1)} %copy-done.4), custom_call_target="tpu_custom_call" | custom-call | tf_op jit(solution)/shard_map/pack/pallas_call | solution.py:235
  11.7 43.2 %all_to_all.10.msg_ref = bf16[64,136,128]{2,1,0:T(8,128)(2,1)S(1)} all-to-all(bf16[64,136,128]{2,1,0:T(8,128)(2,1)S(1)} %pack.1), channel_id=1, replica_groups={{0,3,4,7,8,11,12,15,2,1,6,5,10,9,14,13,32,35,36,39,40,43,44,47,34,33,38..., dimensions={0} | all-to-all | bytes 4456448 | tf_op jit(solution)/shard_map/all_to_all | solution.py:46
  54.8 0.0 copy-start.6
  54.8 0.0 copy-start.5
  54.9 0.0 copy-start.7
  54.9 1.3 slice.20
  56.1 0.0 collective-permute-start
  56.1 0.0 copy-done.5
  56.1 0.1 reshape.20
  56.2 0.1 lt.43
  56.3 0.2 convert_reduce_fusion.1.rank_ref
  56.5 0.0 copy-done.7
  56.5 0.1 convert_reduce_fusion.start_ref
  56.6 2.3 %collective-permute-done.kv_ref = bf16[64,64,128]{2,1,0:T(8,128)(2,1)S(1)} collective-permute-done((bf16[64,64,128]{2,1,0:T(8,128)(2,1)}, bf16[64,64,128]{2,1,0:T(8,128)(2,1)S(1)}, u32[]{:S(2)}, u32[]{:S(2)}) %collective-permute-start) | collective-permute-done | bytes 1048608 | tf_op jit(solution)/shard_map/ppermute | solution.py:284
  59.0 0.0 copy-done.6
  59.0 31.0 %attention.1 = (bf16[64,32,128]{2,1,0:T(8,128)(2,1)S(1)}, f32[64,64,128]{2,1,0:T(8,128)S(1)}, bf16[64,64,128]{2,1,0:T(8,128)(2,1)S(1)}) custom-call(s32[128]{0:T(128)S(1)} %copy-done.5, s32[8]{0:T(128)S(1)} %convert_reduce_fusion.start_ref, s32[64]{0:T(128)S(1)} %convert_reduce_fusion.1.rank_ref, s32[1]{0:T(128)} %bitcast.me_ref, ...), custom_call_target="tpu_custom_call" | custom-call | tf_op jit(solution)/shard_map/attention/pallas_call | solution.py:249
  90.0 1.5 %collective-permute-start.1 = (bf16[64,64,128]{2,1,0:T(8,128)(2,1)S(1)}, bf16[64,64,128]{2,1,0:T(8,128)(2,1)S(1)}, u32[]{:S(2)}, u32[]{:S(2)}) collective-permute-start(bf16[64,64,128]{2,1,0:T(8,128)(2,1)S(1)} %get-tuple-element.8), channel_id=1, source_target_pairs={{0,16},{1,17},{2,18},{3,19},{4,20},{5,21},{6,22},{7,23},{8,24},{9,... | collective-permute-start | bytes 3145736 | tf_op jit(solution)/shard_map/ppermute | solution.py:288
  91.5 2.3 %collective-permute-done.1 = bf16[64,64,128]{2,1,0:T(8,128)(2,1)S(1)} collective-permute-done((bf16[64,64,128]{2,1,0:T(8,128)(2,1)S(1)}, bf16[64,64,128]{2,1,0:T(8,128)(2,1)S(1)}, u32[]{:S(2)}, u32[]{:S(2)}) %collective-permute-start.1) | collective-permute-done | bytes 1048608 | tf_op jit(solution)/shard_map/ppermute | solution.py:288
  93.8 0.4 add_convert_fusion
  94.2 0.1 pad_maximum_fusion
  94.3 29.5 %all_to_all.11 = bf16[64,96,128]{2,1,0:T(8,128)(2,1)S(1)} all-to-all(bf16[64,96,128]{2,1,0:T(8,128)(2,1)S(1)} %pad_maximum_fusion), channel_id=1, replica_groups={{0,3,4,7,8,11,12,15,2,1,6,5,10,9,14,13,32,35,36,39,40,43,44,47,34,33,38..., dimensions={0} | all-to-all | bytes 3145728 | tf_op jit(solution)/shard_map/all_to_all | solution.py:46
  123.8 1.0 copy.14
  124.8 0.1 slice.22
  125.0 0.2 reduce_sum.32
  125.2 0.7 copy.16
  125.9 0.7 copy.15
  (3 shorter events, 0.1 us)
Async XLA Ops:
  0.6 1.0 copy-start
  1.7 1.0 copy-start.1
  2.7 1.0 copy-start.2
  3.8 0.8 copy-start.3
  4.6 0.8 copy-start.4
  54.8 4.1 %copy-start.6 = (bf16[64,136,128]{2,1,0:T(8,128)(2,1)}, bf16[64,136,128]{2,1,0:T(8,128)(2,1)S(1)}, u32[]{:S(2)}) copy-start(bf16[64,136,128]{2,1,0:T(8,128)(2,1)S(1)} %all_to_all.10.msg_ref) | copy-start | bytes 6684676
  54.8 1.3 copy-start.5
  54.9 1.6 %copy-start.7 = (s32[4096]{0:T(1024)S(1)}, s32[4096]{0:T(1024)}, u32[]{:S(2)}) copy-start(s32[4096]{0:T(1024)} %param.12) | copy-start | bytes 49156
  56.1 2.9 %collective-permute-start = (bf16[64,64,128]{2,1,0:T(8,128)(2,1)}, bf16[64,64,128]{2,1,0:T(8,128)(2,1)S(1)}, u32[]{:S(2)}, u32[]{:S(2)}) collective-permute-start(bf16[64,64,128]{2,1,0:T(8,128)(2,1)} %slice.20), channel_id=1, source_target_pairs={{0,16},{1,17},{2,18},{3,19},{4,20},{5,21},{6,22},{7,23},{8,24},{9,... | collective-permute-start | bytes 3145736 | tf_op jit(solution)/shard_map/ppermute | solution.py:284
  90.0 3.8 %collective-permute-start.1 = (bf16[64,64,128]{2,1,0:T(8,128)(2,1)S(1)}, bf16[64,64,128]{2,1,0:T(8,128)(2,1)S(1)}, u32[]{:S(2)}, u32[]{:S(2)}) collective-permute-start(bf16[64,64,128]{2,1,0:T(8,128)(2,1)S(1)} %get-tuple-element.8), channel_id=1, source_target_pairs={{0,16},{1,17},{2,18},{3,19},{4,20},{5,21},{6,22},{7,23},{8,24},{9,... | collective-permute-start | bytes 3145736 | tf_op jit(solution)/shard_map/ppermute | solution.py:288

commit v3 on v1

v3 whole, which is shorter than its diff:
```python
import functools
import math

import jax
import jax.numpy as jnp
from jax import lax
from jax.experimental import pallas as pl
from jax.experimental.pallas import tpu as pltpu
from jax.sharding import PartitionSpec as P

AXES = ("head", "inner", "outer")
F32 = jnp.float32
BF16 = jnp.bfloat16
TOK = 32
GROUP = 8
ROWS = TOK * GROUP
KV0 = 2 * ROWS
DEL0 = KV0 + 2 * TOK
MSG = DEL0 + 16
TK = 256
LENGTH = 4096
PAD = LENGTH + 256
WIDE = 4
UNITS = 8 * (-(-(2048 + TOK + 128) // TK)) + WIDE
LOW = -1e30
NT = (((1,), (1,)), ((), ()))


def linear(x, core, z, y_lo, y_hi):
    return (x * 2 + core) * 16 + (z * 2 + y_lo) * 2 + y_hi


def head_groups():
    return [
        [linear(g >> 1, core, z, (g & 1) ^ y_hi, y_hi) for g in range(8)]
        for core in range(2)
        for z in range(4)
        for y_hi in range(2)
    ]


def seq_groups():
    return [
        [linear(x, core, c >> 1, side ^ (c & 1), c & 1) for c in range(8)]
        for x in range(4)
        for core in range(2)
        for side in range(2)
    ]


def core_pairs():
    return [(i, i ^ 16) for i in range(128)]


def exchange(array, groups):
    return lax.all_to_all(
        array, AXES, split_axis=0, concat_axis=0, axis_index_groups=groups, tiled=True
    )


def dot(a, b):
    return jnp.dot(a, b, preferred_element_type=F32)


def pack_kernel(q_ref, g_ref, o_ref, k_ref, v_ref, out_ref):
    ones = jnp.ones((8, 128), BF16)
    for pair in range(4):
        cols = pl.ds(16 * pair, 16)
        q = q_ref[:, cols, :].astype(F32)
        g = g_ref[:, cols, :].astype(F32)
        prod = g * o_ref[:, cols, :].astype(F32)
        for half in range(2):
            j = 2 * pair + half
            sub = slice(8 * half, 8 * half + 8)
            out_ref[j, 0:ROWS, :] = q[:, sub, :].reshape(ROWS, 128).astype(BF16)
            out_ref[j, ROWS:KV0, :] = g[:, sub, :].reshape(ROWS, 128).astype(BF16)
            part = prod[:, sub, :].reshape(ROWS, 128)
            top = part.astype(BF16)
            rest = (part - top.astype(F32)).astype(BF16)
            delta = lax.dot_general(ones, top, NT, preferred_element_type=F32)
            delta = delta + lax.dot_general(ones, rest, NT, preferred_element_type=F32)
            delta = jnp.concatenate([delta[:, :128], delta[:, 128:]], axis=0)
            first = delta.astype(BF16).astype(F32)
            second = (delta - first).astype(BF16).astype(F32)
            third = delta - first - second
            row = lax.broadcasted_iota(jnp.int32, (16, 128), 0)
            packed = jnp.where(row % 8 == 0, first, jnp.where(row % 8 == 1, second, third))
            out_ref[j, DEL0:MSG, :] = packed.astype(BF16)
            out_ref[j, KV0 : KV0 + TOK, :] = k_ref[j]
            out_ref[j, KV0 + TOK : DEL0, :] = v_ref[j]


def stored_block(core, c, i):
    y_hi = c % 2
    return linear(i // 2, core, c // 2, (i + c) % 2, y_hi)


def attn_kernel(
    span_ref, start_ref, me_ref, msg_ref, kv0_ref, kv1_ref,
    dq_ref, part0_ref, part1_ref,
    unit_q, unit_at, k_s, kt_s, v_s, qt_s, gt_s, d_s, hi_s, lo_s, dk_s, dv_s, dq_s, m_s, l_s, s_s,
):
    core = me_ref[0]
    mine = me_ref[1]
    scale = 1.0 / math.sqrt(128)
    factor = scale * math.log2(math.e)

    k_s[LENGTH:, :] = jnp.zeros((PAD - LENGTH, 128), BF16)
    v_s[LENGTH:, :] = jnp.zeros((PAD - LENGTH, 128), BF16)

    for c in range(8):
        for i in range(8):
            for other, ref in ((0, kv0_ref), (1, kv1_ref)):
                who = core if other == 0 else 1 - core
                at = pl.multiple_of(span_ref[stored_block(who, c, i)] * TOK, TOK)
                k_s[pl.ds(at, TOK), :] = ref[c, i, 0:TOK, :]
                v_s[pl.ds(at, TOK), :] = ref[c, i, TOK : 2 * TOK, :]
    zero = jnp.zeros((256, 128), F32)
    for at in range(0, PAD, 256):
        dk_s[at : at + 256, :] = zero
        dv_s[at : at + 256, :] = zero
        kt_s[:, at : at + 256] = k_s[at : at + 256, :].T

    lane = lax.broadcasted_iota(jnp.int32, (8, ROWS), 1)
    sub = lax.broadcasted_iota(jnp.int32, (8, ROWS), 0)
    step = lax.broadcasted_iota(jnp.int32, (TK // 8, 8, ROWS), 0) * 8
    count = jnp.int32(0)
    for i in range(8):
        base = span_ref[stored_block(core, mine, i)] * TOK
        place_q = base + lane // GROUP
        begin = jnp.zeros((8, ROWS), jnp.int32)
        low = jnp.int32(0)
        for s in range(1, 8):
            edge = start_ref[s]
            begin = jnp.where(place_q >= edge, jnp.maximum(begin, edge), begin)
            low = jnp.where(base >= edge, jnp.maximum(low, edge), low)
        hi_s[i] = place_q - sub
        lo_s[i] = begin - sub
        first = low // 128 * 128
        tiles = (base + TOK - first + TK - 1) // TK

        def enlist(t, _):
            unit_q[count + t] = i
            unit_at[count + t] = first + t * TK
            return 0

        lax.fori_loop(0, tiles, enlist, 0)
        count = count + tiles
        qt_s[i] = msg_ref[i, 0:ROWS, :].T
        gt_s[i] = msg_ref[i, ROWS:KV0, :].T
        tail = msg_ref[i, DEL0:MSG, :].astype(F32)
        halves = [tail[n : n + 1] + tail[n + 1 : n + 2] + tail[n + 2 : n + 3] for n in (0, 8)]
        d_s[i] = jnp.broadcast_to(jnp.concatenate(halves, axis=1), (8, ROWS))
        m_s[i] = jnp.full((8, ROWS), LOW, F32)
        l_s[i] = jnp.zeros((8, ROWS), F32)
        dq_s[i] = jnp.zeros((128, ROWS), F32)
    for n in range(WIDE - 1):
        unit_q[count + n] = 0
        unit_at[count + n] = LENGTH
    rounds = (count + WIDE - 1) // WIDE

    def stats(n, _):
        units = []
        for u in range(WIDE):
            i = unit_q[n * WIDE + u]
            at = pl.multiple_of(unit_at[n * WIDE + u], 128)
            units.append((i, at, dot(k_s[pl.ds(at, TK), :], qt_s[i])))
        results = []
        for u, (i, at, s) in enumerate(units):
            s = (s * factor).reshape(TK // 8, 8, ROWS)
            upper = hi_s[i] - at
            lower = lo_s[i] - at
            s = jnp.where((step <= upper[None]) & (step >= lower[None]), s, LOW)
            s_s[n * WIDE + u] = s.reshape(TK, ROWS)
            top = jnp.max(s, axis=0)
            results.append((i, top, jnp.sum(jnp.exp2(s - top[None]), axis=0)))
        for i, top, total in results:
            old = m_s[i]
            new = jnp.maximum(old, top)
            m_s[i] = new
            l_s[i] = l_s[i] * jnp.exp2(old - new) + total * jnp.exp2(top - new)
        return 0

    lax.fori_loop(0, rounds, stats, 0)
    for i in range(8):
        top = m_s[i]
        peak = jnp.max(top, axis=0, keepdims=True)
        total = jnp.sum(l_s[i] * jnp.exp2(top - peak), axis=0, keepdims=True)
        m_s[i] = jnp.broadcast_to(peak + jnp.log2(total), (8, ROWS))

    def grads(n, _):
        units = []
        for u in range(WIDE):
            i = unit_q[n * WIDE + u]
            at = pl.multiple_of(unit_at[n * WIDE + u], 128)
            units.append((i, at, dot(v_s[pl.ds(at, TK), :], gt_s[i])))
        results = []
        for u, (i, at, dp) in enumerate(units):
            s = s_s[n * WIDE + u].reshape(TK // 8, 8, ROWS)
            p = jnp.exp2(s - m_s[i][None])
            ds = p * (dp.reshape(TK // 8, 8, ROWS) - d_s[i][None])
            p = p.reshape(TK, ROWS).astype(BF16)
            ds = ds.reshape(TK, ROWS).astype(BF16)
            results.append((i, at, p, ds))
        for i, at, p, ds in results:
            dv_s[pl.ds(at, TK), :] += dot(p, msg_ref[i, ROWS:KV0, :])
            dk_s[pl.ds(at, TK), :] += dot(ds, msg_ref[i, 0:ROWS, :])
            dq_s[i] += dot(kt_s[:, pl.ds(at, TK)], ds)
        return 0

    lax.fori_loop(0, rounds, grads, 0)
    for i in range(8):
        dq_ref[i, :, :] = (dq_s[i] * scale).T.astype(BF16)

    for c in range(8):
        for i in range(8):
            for other, ref in ((0, part0_ref), (1, part1_ref)):
                who = core if other == 0 else 1 - core
                at = pl.multiple_of(span_ref[stored_block(who, c, i)] * TOK, TOK)
                ref[c, i, 0:TOK, :] = (dk_s[pl.ds(at, TOK), :] * scale).astype(BF16)
                ref[c, i, TOK : 2 * TOK, :] = dv_s[pl.ds(at, TOK), :].astype(BF16)


def vmem():
    return pl.BlockSpec(memory_space=pltpu.VMEM)


def smem():
    return pl.BlockSpec(memory_space=pltpu.SMEM)


def attention(span_position, starts, me, message, kv_mine, kv_other):
    kv_shape = jax.ShapeDtypeStruct((8, 8, 2 * TOK, 128), BF16)
    return pl.pallas_call(
        attn_kernel,
        out_shape=(jax.ShapeDtypeStruct((8, ROWS, 128), BF16), kv_shape, kv_shape),
        in_specs=[smem()] * 3 + [vmem()] * 3,
        out_specs=(vmem(),) * 3,
        scratch_shapes=[
            pltpu.SMEM((UNITS,), jnp.int32),
            pltpu.SMEM((UNITS,), jnp.int32),
            pltpu.VMEM((PAD, 128), BF16),
            pltpu.VMEM((128, PAD), BF16),
            pltpu.VMEM((PAD, 128), BF16),
            pltpu.VMEM((8, 128, ROWS), BF16),
            pltpu.VMEM((8, 128, ROWS), BF16),
            pltpu.VMEM((8, 8, ROWS), F32),
            pltpu.VMEM((8, 8, ROWS), jnp.int32),
            pltpu.VMEM((8, 8, ROWS), jnp.int32),
            pltpu.VMEM((PAD, 128), F32),
            pltpu.VMEM((PAD, 128), F32),
            pltpu.VMEM((8, 128, ROWS), F32),
            pltpu.VMEM((8, 8, ROWS), F32),
            pltpu.VMEM((8, 8, ROWS), F32),
            pltpu.VMEM((UNITS, TK, ROWS), F32),
        ],
        compiler_params=pltpu.CompilerParams(vmem_limit_bytes=56 << 20),
        name="attention",
    )(span_position, starts, me, message, kv_mine, kv_other)


def shards(queries, keys, values, out_states, out_grads, segment_ids, span_position):
    head = lax.axis_index("head")
    inner = lax.axis_index("inner")
    outer = lax.axis_index("outer")
    me = jnp.stack([head % 2, inner // 2 * 2 + outer]).astype(jnp.int32)
    starts = jnp.sum(
        segment_ids[None, :] < jnp.arange(8, dtype=jnp.int32)[:, None], axis=1, dtype=jnp.int32
    )
    message = pl.pallas_call(
        pack_kernel,
        out_shape=jax.ShapeDtypeStruct((8, MSG, 128), BF16),
        in_specs=[vmem()] * 5,
        out_specs=vmem(),
        compiler_params=pltpu.CompilerParams(vmem_limit_bytes=32 << 20),
        name="pack",
    )(queries, out_grads, out_states, keys.transpose(1, 0, 2), values.transpose(1, 0, 2))
    message = exchange(message, head_groups())
    kv_part = message[:, KV0:DEL0, :]
    kv_mine = exchange(
        jnp.broadcast_to(kv_part[None], (8, 8, 2 * TOK, 128)), seq_groups()
    )
    kv_other = lax.ppermute(kv_mine, AXES, core_pairs())
    dq, part_mine, part_other = attention(span_position, starts, me, message, kv_mine, kv_other)
    theirs = lax.ppermute(part_other, AXES, core_pairs())
    part = (part_mine.astype(F32) + theirs.astype(F32)).astype(BF16)
    part = exchange(part, seq_groups())
    total = jnp.sum(part.astype(F32), axis=0).astype(BF16)
    back = exchange(jnp.concatenate([dq, total], axis=1), head_groups())
    query_grad = back[:, :ROWS].reshape(8, TOK, GROUP, 128).transpose(1, 0, 2, 3)
    return (
        query_grad.reshape(TOK, 64, 128),
        back[:, ROWS : ROWS + TOK].transpose(1, 0, 2),
        back[:, ROWS + TOK :].transpose(1, 0, 2),
    )


def solution(mesh):
    spec = P(AXES, None, None)
    return jax.shard_map(
        shards,
        mesh=mesh,
        in_specs=(spec,) * 5 + (P(), P()),
        out_specs=(spec,) * 3,
        check_vma=False,
    )
```

time: 124 us -> 112 us (0.903)
  Pallas kernels: 21.6 us -> 15.5 us
  blocking collectives: 86 us -> 80.7 us
  starting transfers between devices: 2.8 us -> 0.01 us
  other arithmetic: 0.87 us -> 3.18 us
    pallas_call x1, Pallas kernels: 21.1 us -> 15 us  [attention(): pl.pallas_call(attn_kernel, out_shape=(jax.ShapeDtypeStruct((8, ROWS, 128...]
    all_to_all x4, blocking collectives: 86 us -> 80.7 us  [exchange(): lax.all_to_all(array, AXES, split_axis=0, concat_axis=0, axis_index_group...]
    ppermute x1, starting transfers between devices: 2.8 us -> 0.01 us  [shards(): theirs = lax.ppermute(part_other, AXES, core_pairs())]
    unnamed x16 -> x18, local copies, waits for them, and re-layouts: 5.31 us -> 5.41 us
  transfers between devices with their start and end apart: 2 -> 2, of which waited for: 2 -> 2; matrix products, arithmetic and copies ran while one was open for 0% -> 1% of each run, Pallas kernels for 0% -> 0%
where the time goes in v3:
time: 112 us
  blocking collectives  80.7 us (72%)
  Pallas kernels  15.5 us (14%)
  local copies, waits for them, and re-layouts  7.5 us (7%)
  waiting for transfers between devices  4.16 us (4%)
  other arithmetic  3.18 us (3%)
    all_to_all x4, blocking collectives, exchange(): lax.all_to_all(array, AXES, split_axis=0, concat_axis=0, axis_index_group...  80.7 us
    pallas_call x1, Pallas kernels, attention(): pl.pallas_call(attn_kernel, out_shape=(jax.ShapeDtypeStruct((8, ROWS, 128...  15 us
    unnamed x18, local copies, waits for them, and re-layouts  5.41 us
    ppermute x1, waiting for transfers between devices, shards(): theirs = lax.ppermute(part_other, AXES, core_pairs())  2.87 us
  transfers between devices with their start and end apart: 2, of which 2 were waited for; matrix products, arithmetic and copies ran while one was open for 1% of the time, Pallas kernels for 0%

profile of v3, /device:TPU:0, one launch (start us, length us, event | category | flops | bytes accessed | tf_op | source)
XLA Modules:
  0.0 111.8 jit_solution(8437932274851789182)
XLA Ops:
  0.6 0.9 copy_bitcast_fusion.1
  1.5 0.0 copy-start
  1.5 1.0 copy-done
  2.6 0.0 copy-start.1
  2.6 1.0 copy-done.1
  3.6 0.0 copy-start.2
  3.6 1.0 copy-done.2
  4.7 0.5 pack.1
  5.1 22.4 %all_to_all.20.msg_ref = bf16[8,592,128]{2,1,0:T(8,128)(2,1)S(1)} all-to-all(bf16[8,592,128]{2,1,0:T(8,128)(2,1)S(1)} %pack.1), channel_id=1, replica_groups={{0,2,32,34,64,66,96,98},{3,1,35,33,67,65,99,97},{4,6,36,38,68,70,100,10..., dimensions={0} | all-to-all | bytes 2424832 | tf_op jit(solution)/shard_map/all_to_all | solution.py:56
  27.6 0.0 copy-start.3
  27.6 0.2 broadcast_in_dim.2
  27.8 0.0 copy-start.7
  27.9 22.3 %all_to_all.21.kv0_ref = bf16[8,8,64,128]{3,2,1,0:T(8,128)(2,1)S(1)} all-to-all(bf16[8,8,64,128]{3,2,1,0:T(8,128)(2,1)S(1)} %broadcast_in_dim.2), channel_id=1, replica_groups={{0,3,4,7,8,11,12,15},{2,1,6,5,10,9,14,13},{16,19,20,23,24,27,28,31},{18..., dimensions={0} | all-to-all | bytes 2097152 | tf_op jit(solution)/shard_map/all_to_all | solution.py:56
  50.2 0.0 copy-done.3
  50.2 0.0 copy-start.4
  50.2 0.0 collective-permute-start
  50.2 0.7 pad_add_fusion.me_ref
  50.9 0.0 copy-done.7
  50.9 0.7 convert_reduce_fusion.start_ref
  51.5 1.3 %collective-permute-done.kv1_ref = bf16[8,8,64,128]{3,2,1,0:T(8,128)(2,1)S(1)} collective-permute-done((bf16[8,8,64,128]{3,2,1,0:T(8,128)(2,1)S(1)}, bf16[8,8,64,128]{3,2,1,0:T(8,128)(2,1)S(1)}, u32[]{:S(2)}, u32[]{:S(2)}) %collective-permute-start) | collective-permute-done | bytes 1048608 | tf_op jit(solution)/shard_map/ppermute | solution.py:283
  52.8 0.0 copy-done.4
  52.8 0.0 copy-start.5
  52.8 1.0 copy-done.5
  53.8 15.0 %attention.1 = (bf16[8,256,128]{2,1,0:T(8,128)(2,1)}, bf16[8,8,64,128]{3,2,1,0:T(8,128)(2,1)}, bf16[8,8,64,128]{3,2,1,0:T(8,128)(2,1)}) custom-call(s32[128]{0:T(128)} %span_ref.1, s32[8]{0:T(128)} %convert_reduce_fusion.start_ref, s32[2]{0:T(128)} %pad_add_fusion.me_ref, bf16[8,592,128]{2,1,0:T(8,128)(2,1)} %copy-done.3, bf16[8,8,64,128]{3,2,1,0:T(8,128)(2,1)} %copy-done.4, ...), custom_call_target="tpu_custom_call" | custom-call | tf_op jit(solution)/shard_map/attention/pallas_call | solution.py:234
  68.8 0.0 collective-permute-start.1
  68.8 2.9 %collective-permute-done.1 = bf16[8,8,64,128]{3,2,1,0:T(8,128)(2,1)S(1)} collective-permute-done((bf16[8,8,64,128]{3,2,1,0:T(8,128)(2,1)}, bf16[8,8,64,128]{3,2,1,0:T(8,128)(2,1)S(1)}, u32[]{:S(2)}, u32[]{:S(2)}) %collective-permute-start.1) | collective-permute-done | bytes 1048608 | tf_op jit(solution)/shard_map/ppermute | solution.py:285
  71.7 1.6 %add_convert_fusion = bf16[8,8,64,128]{3,2,1,0:T(8,128)(2,1)S(1)} fusion(bf16[8,8,64,128]{3,2,1,0:T(8,128)(2,1)S(1)} %collective-permute-done.1, bf16[8,8,64,128]{3,2,1,0:T(8,128)(2,1)} %get-tuple-element.7), kind=kLoop, calls=%fused_computation | loop fusion | flops 2097152 | bytes 3145728 | tf_op jit(solution)/shard_map/convert_element_type | solution.py:286
  73.3 0.0 copy-start.6
  73.3 22.4 %all_to_all.22 = bf16[8,8,64,128]{3,2,1,0:T(8,128)(2,1)S(1)} all-to-all(bf16[8,8,64,128]{3,2,1,0:T(8,128)(2,1)S(1)} %add_convert_fusion), channel_id=1, replica_groups={{0,3,4,7,8,11,12,15},{2,1,6,5,10,9,14,13},{16,19,20,23,24,27,28,31},{18..., dimensions={0} | all-to-all | bytes 2097152 | tf_op jit(solution)/shard_map/all_to_all | solution.py:56
  95.8 0.2 reduce_sum.22
  96.0 0.0 copy-done.6
  96.0 13.5 %all_to_all.23 = bf16[8,320,128]{2,1,0:T(8,128)(2,1)S(1)} all-to-all(bf16[8,320,128]{2,1,0:T(8,128)(2,1)S(1)} %pad_maximum_fusion), channel_id=1, replica_groups={{0,2,32,34,64,66,96,98},{3,1,35,33,67,65,99,97},{4,6,36,38,68,70,100,10..., dimensions={0} | all-to-all | bytes 1310720 | tf_op jit(solution)/shard_map/all_to_all | solution.py:56
  109.5 0.7 copy.19
  110.2 0.7 copy.18
  110.9 0.9 copy_bitcast_fusion
  (3 shorter events, 0.1 us)
Async XLA Ops:
  1.5 1.0 copy-start
  2.6 1.0 copy-start.1
  3.6 1.0 copy-start.2
  27.6 22.6 %copy-start.3 = (bf16[8,592,128]{2,1,0:T(8,128)(2,1)}, bf16[8,592,128]{2,1,0:T(8,128)(2,1)S(1)}, u32[]{:S(2)}) copy-start(bf16[8,592,128]{2,1,0:T(8,128)(2,1)S(1)} %all_to_all.20.msg_ref) | copy-start | bytes 3637252
  27.8 23.0 %copy-start.7 = (s32[4096]{0:T(1024)S(1)}, s32[4096]{0:T(1024)}, u32[]{:S(2)}) copy-start(s32[4096]{0:T(1024)} %param.12) | copy-start | bytes 49156
  50.2 2.7 %copy-start.4 = (bf16[8,8,64,128]{3,2,1,0:T(8,128)(2,1)}, bf16[8,8,64,128]{3,2,1,0:T(8,128)(2,1)S(1)}, u32[]{:S(2)}) copy-start(bf16[8,8,64,128]{3,2,1,0:T(8,128)(2,1)S(1)} %all_to_all.21.kv0_ref) | copy-start | bytes 3145732
  50.2 2.7 %collective-permute-start = (bf16[8,8,64,128]{3,2,1,0:T(8,128)(2,1)S(1)}, bf16[8,8,64,128]{3,2,1,0:T(8,128)(2,1)S(1)}, u32[]{:S(2)}, u32[]{:S(2)}) collective-permute-start(bf16[8,8,64,128]{3,2,1,0:T(8,128)(2,1)S(1)} %all_to_all.21.kv0_ref), channel_id=1, source_target_pairs={{0,16},{1,17},{2,18},{3,19},{4,20},{5,21},{6,22},{7,23},{8,24},{9,... | collective-permute-start | bytes 3145736 | tf_op jit(solution)/shard_map/ppermute | solution.py:283
  52.8 1.0 copy-start.5
  68.8 2.9 %collective-permute-start.1 = (bf16[8,8,64,128]{3,2,1,0:T(8,128)(2,1)}, bf16[8,8,64,128]{3,2,1,0:T(8,128)(2,1)S(1)}, u32[]{:S(2)}, u32[]{:S(2)}) collective-permute-start(bf16[8,8,64,128]{3,2,1,0:T(8,128)(2,1)} %get-tuple-element.8), channel_id=1, source_target_pairs={{0,16},{1,17},{2,18},{3,19},{4,20},{5,21},{6,22},{7,23},{8,24},{9,... | collective-permute-start | bytes 3145736 | tf_op jit(solution)/shard_map/ppermute | solution.py:285
  73.3 22.6 %copy-start.6 = (bf16[8,256,128]{2,1,0:T(8,128)(2,1)S(1)}, bf16[8,256,128]{2,1,0:T(8,128)(2,1)}, u32[]{:S(2)}) copy-start(bf16[8,256,128]{2,1,0:T(8,128)(2,1)} %get-tuple-element.6) | copy-start | bytes 1572868

commit v4 on v3

--- a/solution.py
+++ b/solution.py
@@ -21,6 +21,8 @@
 LENGTH = 4096
 PAD = LENGTH + 256
 WIDE = 4
+LAG = 3
+RING = LAG + 1
 UNITS = 8 * (-(-(2048 + TOK + 128) // TK)) + WIDE
 LOW = -1e30
 NT = (((1,), (1,)), ((), ()))
@@ -62,17 +64,23 @@
     return jnp.dot(a, b, preferred_element_type=F32)
 
 
-def pack_kernel(q_ref, g_ref, o_ref, k_ref, v_ref, out_ref):
+def pack_kernel(q_hbm, g_hbm, o_hbm, k_hbm, v_hbm, out_ref, q_v, g_v, o_v, k_v, v_v, wide, sem):
+    copies = []
+    for n, (src, dst) in enumerate(
+        ((g_hbm, g_v), (o_hbm, o_v), (q_hbm, q_v), (k_hbm, k_v), (v_hbm, v_v))
+    ):
+        copies.append(pltpu.make_async_copy(src, dst, sem.at[n]))
+        copies[n].start()
     ones = jnp.ones((8, 128), BF16)
+    copies[0].wait()
+    copies[1].wait()
     for pair in range(4):
         cols = pl.ds(16 * pair, 16)
-        q = q_ref[:, cols, :].astype(F32)
-        g = g_ref[:, cols, :].astype(F32)
-        prod = g * o_ref[:, cols, :].astype(F32)
+        g = g_v[:, cols, :].astype(F32)
+        prod = g * o_v[:, cols, :].astype(F32)
         for half in range(2):
             j = 2 * pair + half
             sub = slice(8 * half, 8 * half + 8)
-            out_ref[j, 0:ROWS, :] = q[:, sub, :].reshape(ROWS, 128).astype(BF16)
             out_ref[j, ROWS:KV0, :] = g[:, sub, :].reshape(ROWS, 128).astype(BF16)
             part = prod[:, sub, :].reshape(ROWS, 128)
             top = part.astype(BF16)
@@ -86,8 +94,42 @@
             row = lax.broadcasted_iota(jnp.int32, (16, 128), 0)
             packed = jnp.where(row % 8 == 0, first, jnp.where(row % 8 == 1, second, third))
             out_ref[j, DEL0:MSG, :] = packed.astype(BF16)
-            out_ref[j, KV0 : KV0 + TOK, :] = k_ref[j]
-            out_ref[j, KV0 + TOK : DEL0, :] = v_ref[j]
+    copies[2].wait()
+    for pair in range(4):
+        q = q_v[:, pl.ds(16 * pair, 16), :].astype(F32)
+        for half in range(2):
+            sub = slice(8 * half, 8 * half + 8)
+            out_ref[2 * pair + half, 0:ROWS, :] = q[:, sub, :].reshape(ROWS, 128).astype(BF16)
+    for n, ref in ((0, k_v), (1, v_v)):
+        copies[3 + n].wait()
+        wide[...] = ref[...].reshape(ROWS, 128).astype(F32)
+        for j in range(8):
+            at = KV0 + n * TOK
+            out_ref[j, at : at + TOK, :] = wide[pl.ds(j, TOK, 8), :].astype(BF16)
+
+
+def unpack_kernel(back_ref, q_hbm, k_hbm, v_hbm, q_v, k_v, v_v, wide, sem):
+    copies = []
+    for n, (src, dst) in enumerate(((k_v, k_hbm), (v_v, v_hbm))):
+        for j in range(8):
+            at = ROWS + n * TOK
+            wide[pl.ds(j, TOK, 8), :] = back_ref[j, at : at + TOK, :].astype(F32)
+        src[...] = wide[...].reshape(TOK, 8, 128).astype(BF16)
+        copies.append(pltpu.make_async_copy(src, dst, sem.at[n]))
+        copies[-1].start()
+    for pair in range(4):
+        cols = pl.ds(16 * pair, 16)
+        sides = [
+            back_ref[2 * pair + half, 0:ROWS, :].astype(F32).reshape(TOK, 8, 128)
+            for half in range(2)
+        ]
+        q_v[:, cols, :] = jnp.concatenate(sides, axis=1).astype(BF16)
+        copies.append(
+            pltpu.make_async_copy(q_v.at[:, cols, :], q_hbm.at[:, cols, :], sem.at[2 + pair])
+        )
+        copies[-1].start()
+    for copy in copies:
+        copy.wait()
 
 
 def stored_block(core, c, i):
@@ -98,7 +140,7 @@
 def attn_kernel(
     span_ref, start_ref, me_ref, msg_ref, kv0_ref, kv1_ref,
     dq_ref, part0_ref, part1_ref,
-    unit_q, unit_at, k_s, kt_s, v_s, qt_s, gt_s, d_s, hi_s, lo_s, dk_s, dv_s, dq_s, m_s, l_s, s_s,
+    unit_q, unit_at, k_s, kt_s, v_s, qt_s, gt_s, d_s, hi_s, lo_s, dk_s, dv_s, dq_s, m_s, l_s, w_s, s_s,
 ):
     core = me_ref[0]
     mine = me_ref[1]
@@ -159,56 +201,73 @@
         unit_at[count + n] = LENGTH
     rounds = (count + WIDE - 1) // WIDE
 
-    def stats(n, _):
+    def units_of(n):
         units = []
         for u in range(WIDE):
             i = unit_q[n * WIDE + u]
-            at = pl.multiple_of(unit_at[n * WIDE + u], 128)
-            units.append((i, at, dot(k_s[pl.ds(at, TK), :], qt_s[i])))
+            units.append((n % RING * WIDE + u, i, pl.multiple_of(unit_at[n * WIDE + u], 128)))
+        return units
+
+    def stats_dots(units):
+        return [dot(k_s[pl.ds(at, TK), :], qt_s[i]) for _, i, at in units]
+
+    def stats_rest(units, scores):
         results = []
-        for u, (i, at, s) in enumerate(units):
+        for (slot, i, at), s in zip(units, scores):
             s = (s * factor).reshape(TK // 8, 8, ROWS)
             upper = hi_s[i] - at
             lower = lo_s[i] - at
             s = jnp.where((step <= upper[None]) & (step >= lower[None]), s, LOW)
-            s_s[n * WIDE + u] = s.reshape(TK, ROWS)
             top = jnp.max(s, axis=0)
-            results.append((i, top, jnp.sum(jnp.exp2(s - top[None]), axis=0)))
+            e = jnp.exp2(s - top[None])
+            s_s[slot] = e.reshape(TK, ROWS)
+            w_s[slot] = top
+            results.append((i, top, jnp.sum(e, axis=0)))
         for i, top, total in results:
             old = m_s[i]
             new = jnp.maximum(old, top)
             m_s[i] = new
             l_s[i] = l_s[i] * jnp.exp2(old - new) + total * jnp.exp2(top - new)
-        return 0
-
-    lax.fori_loop(0, rounds, stats, 0)
-    for i in range(8):
-        top = m_s[i]
-        peak = jnp.max(top, axis=0, keepdims=True)
-        total = jnp.sum(l_s[i] * jnp.exp2(top - peak), axis=0, keepdims=True)
-        m_s[i] = jnp.broadcast_to(peak + jnp.log2(total), (8, ROWS))
-
-    def grads(n, _):
-        units = []
-        for u in range(WIDE):
-            i = unit_q[n * WIDE + u]
-            at = pl.multiple_of(unit_at[n * WIDE + u], 128)
-            units.append((i, at, dot(v_s[pl.ds(at, TK), :], gt_s[i])))
+
+    def grads_dots(units):
+        return [dot(v_s[pl.ds(at, TK), :], gt_s[i]) for _, i, at in units]
+
+    def grads_soft(units, dps):
         results = []
-        for u, (i, at, dp) in enumerate(units):
-            s = s_s[n * WIDE + u].reshape(TK // 8, 8, ROWS)
-            p = jnp.exp2(s - m_s[i][None])
+        for (slot, i, at), dp in zip(units, dps):
+            top = m_s[i]
+            peak = jnp.max(top, axis=0, keepdims=True)
+            total = jnp.sum(l_s[i] * jnp.exp2(top - peak), axis=0, keepdims=True)
+            weight = jnp.exp2(w_s[slot] - peak) / total
+            p = s_s[slot].reshape(TK // 8, 8, ROWS) * weight[None]
             ds = p * (dp.reshape(TK // 8, 8, ROWS) - d_s[i][None])
             p = p.reshape(TK, ROWS).astype(BF16)
-            ds = ds.reshape(TK, ROWS).astype(BF16)
-            results.append((i, at, p, ds))
+            results.append((i, at, p, ds.reshape(TK, ROWS).astype(BF16)))
+        return results
+
+    def grads_rest(results):
         for i, at, p, ds in results:
             dv_s[pl.ds(at, TK), :] += dot(p, msg_ref[i, ROWS:KV0, :])
             dk_s[pl.ds(at, TK), :] += dot(ds, msg_ref[i, 0:ROWS, :])
             dq_s[i] += dot(kt_s[:, pl.ds(at, TK)], ds)
+
+    def ahead(n, _):
+        for unit in units_of(n):
+            stats_rest([unit], stats_dots([unit]))
         return 0
 
-    lax.fori_loop(0, rounds, grads, 0)
+    def behind(n, _):
+        units = units_of(n)
+        grads_rest(grads_soft(units, grads_dots(units)))
+        return 0
+
+    def split(n, _):
+        behind(n - LAG, 0)
+        return ahead(n, 0)
+
+    lax.fori_loop(0, jnp.minimum(rounds, LAG), ahead, 0)
+    lax.fori_loop(LAG, rounds, split, 0)
+    lax.fori_loop(jnp.maximum(rounds - LAG, 0), rounds, behind, 0)
     for i in range(8):
         dq_ref[i, :, :] = (dq_s[i] * scale).T.astype(BF16)
 
@@ -217,7 +276,7 @@
             for other, ref in ((0, part0_ref), (1, part1_ref)):
                 who = core if other == 0 else 1 - core
                 at = pl.multiple_of(span_ref[stored_block(who, c, i)] * TOK, TOK)
-                ref[c, i, 0:TOK, :] = (dk_s[pl.ds(at, TOK), :] * scale).astype(BF16)
+                ref[c, i, 0:TOK, :] = dk_s[pl.ds(at, TOK), :].astype(BF16)
                 ref[c, i, TOK : 2 * TOK, :] = dv_s[pl.ds(at, TOK), :].astype(BF16)
 
 
@@ -227,6 +286,39 @@
 
 def smem():
     return pl.BlockSpec(memory_space=pltpu.SMEM)
+
+
+def hbm():
+    return pl.BlockSpec(memory_space=pl.ANY)
+
+
+def pack(queries, out_grads, out_states, keys, values):
+    return pl.pallas_call(
+        pack_kernel,
+        out_shape=jax.ShapeDtypeStruct((8, MSG, 128), BF16),
+        in_specs=[hbm()] * 5,
+        out_specs=vmem(),
+        scratch_shapes=[pltpu.VMEM((TOK, 64, 128), BF16)] * 3
+        + [pltpu.VMEM((TOK, 8, 128), BF16)] * 2
+        + [pltpu.VMEM((ROWS, 128), F32), pltpu.SemaphoreType.DMA((5,))],
+        compiler_params=pltpu.CompilerParams(vmem_limit_bytes=58 << 20),
+        name="pack",
+    )(queries, out_grads, out_states, keys, values)
+
+
+def unpack(back):
+    small = jax.ShapeDtypeStruct((TOK, 8, 128), BF16)
+    return pl.pallas_call(
+        unpack_kernel,
+        out_shape=(jax.ShapeDtypeStruct((TOK, 64, 128), BF16), small, small),
+        in_specs=[vmem()],
+        out_specs=(hbm(),) * 3,
+        scratch_shapes=[pltpu.VMEM((TOK, 64, 128), BF16)]
+        + [pltpu.VMEM((TOK, 8, 128), BF16)] * 2
+        + [pltpu.VMEM((ROWS, 128), F32), pltpu.SemaphoreType.DMA((6,))],
+        compiler_params=pltpu.CompilerParams(vmem_limit_bytes=58 << 20),
+        name="unpack",
+    )(back)
 
 
 def attention(span_position, starts, me, message, kv_mine, kv_other):
@@ -252,9 +344,10 @@
             pltpu.VMEM((8, 128, ROWS), F32),
             pltpu.VMEM((8, 8, ROWS), F32),
             pltpu.VMEM((8, 8, ROWS), F32),
-            pltpu.VMEM((UNITS, TK, ROWS), F32),
+            pltpu.VMEM((RING * WIDE, 8, ROWS), F32),
+            pltpu.VMEM((RING * WIDE, TK, ROWS), F32),
         ],
-        compiler_params=pltpu.CompilerParams(vmem_limit_bytes=56 << 20),
+        compiler_params=pltpu.CompilerParams(vmem_limit_bytes=32 << 20),
         name="attention",
     )(span_position, starts, me, message, kv_mine, kv_other)
 
@@ -267,14 +360,7 @@
     starts = jnp.sum(
         segment_ids[None, :] < jnp.arange(8, dtype=jnp.int32)[:, None], axis=1, dtype=jnp.int32
     )
-    message = pl.pallas_call(
-        pack_kernel,
-        out_shape=jax.ShapeDtypeStruct((8, MSG, 128), BF16),
-        in_specs=[vmem()] * 5,
-        out_specs=vmem(),
-        compiler_params=pltpu.CompilerParams(vmem_limit_bytes=32 << 20),
-        name="pack",
-    )(queries, out_grads, out_states, keys.transpose(1, 0, 2), values.transpose(1, 0, 2))
+    message = pack(queries, out_grads, out_states, keys, values)
     message = exchange(message, head_groups())
     kv_part = message[:, KV0:DEL0, :]
     kv_mine = exchange(
@@ -285,14 +371,10 @@
     theirs = lax.ppermute(part_other, AXES, core_pairs())
     part = (part_mine.astype(F32) + theirs.astype(F32)).astype(BF16)
     part = exchange(part, seq_groups())
-    total = jnp.sum(part.astype(F32), axis=0).astype(BF16)
-    back = exchange(jnp.concatenate([dq, total], axis=1), head_groups())
-    query_grad = back[:, :ROWS].reshape(8, TOK, GROUP, 128).transpose(1, 0, 2, 3)
-    return (
-        query_grad.reshape(TOK, 64, 128),
-        back[:, ROWS : ROWS + TOK].transpose(1, 0, 2),
-        back[:, ROWS + TOK :].transpose(1, 0, 2),
-    )
+    total = jnp.sum(part.astype(F32), axis=0).reshape(8, 2, TOK, 128)
+    factor = jnp.array([1.0 / math.sqrt(128), 1.0], F32).reshape(1, 2, 1, 1)
+    total = (total * factor).astype(BF16).reshape(8, 2 * TOK, 128)
+    return unpack(exchange(jnp.concatenate([dq, total], axis=1), head_groups()))
 
 
 def solution(mesh):

time: 112 us -> 106 us (0.946)
  blocking collectives: 80.7 us -> 58.8 us
  waiting for transfers between devices: 4.16 us -> 21.8 us
  starting transfers between devices: 0.01 us -> 6.52 us
  local copies, waits for them, and re-layouts: 7.5 us -> 1.22 us
  other arithmetic: 3.18 us -> 1.89 us
  Pallas kernels: 15.5 us -> 14.3 us
    all_to_all x4 -> x3, blocking collectives: 80.7 us -> 58.8 us  [exchange(): lax.all_to_all(array, AXES, split_axis=0, concat_axis=0, axis_index_group...]
    all_to_all x0 -> x1, waiting for transfers between devices: none -> 17.1 us  [exchange(): lax.all_to_all(array, AXES, split_axis=0, concat_axis=0, axis_index_group...]
    pallas_call x1, Pallas kernels: 15 us -> 9.38 us  [attention(): pl.pallas_call(attn_kernel, out_shape=(jax.ShapeDtypeStruct((8, ROWS, 128...]
    all_to_all x0 -> x1, starting transfers between devices: none -> 5.33 us  [exchange(): lax.all_to_all(array, AXES, split_axis=0, concat_axis=0, axis_index_group...]
    unnamed x18 -> x10, local copies, waits for them, and re-layouts: 5.41 us -> 0.81 us
    pallas_call x1 -> x2, Pallas kernels: 0.48 us -> 4.89 us  [the longest x1 2.88 us: pack(): pl.pallas_call(pack_kernel, out_shape=jax.ShapeDtypeStruct((8, MSG, 128),...]
    ppermute x1, starting transfers between devices: 0.01 us -> 1.19 us  [shards(): theirs = lax.ppermute(part_other, AXES, core_pairs())]
    ppermute x1, waiting for transfers between devices: 1.29 us -> 2.43 us  [shards(): kv_other = lax.ppermute(kv_mine, AXES, core_pairs())]
  transfers between devices with their start and end apart: 2 -> 3, of which waited for: 2 -> 3; matrix products, arithmetic and copies ran while one was open for 1% -> 0% of each run, Pallas kernels for 0% -> 0%
where the time goes in v4:
time: 106 us; the launch traced here: 105 us
  blocking collectives  58.8 us (55%)
  waiting for transfers between devices  21.8 us (21%)
  Pallas kernels  14.3 us (13%)
  starting transfers between devices  6.52 us (6%)
  other arithmetic  1.89 us (2%)
  local copies, waits for them, and re-layouts  1.22 us (1%)
    all_to_all x3, blocking collectives, exchange(): lax.all_to_all(array, AXES, split_axis=0, concat_axis=0, axis_index_group...  58.8 us
    all_to_all x1, waiting for transfers between devices, exchange(): lax.all_to_all(array, AXES, split_axis=0, concat_axis=0, axis_index_group...  17.1 us
    pallas_call x1, Pallas kernels, attention(): pl.pallas_call(attn_kernel, out_shape=(jax.ShapeDtypeStruct((8, ROWS, 128...  9.38 us
    all_to_all x1, starting transfers between devices, exchange(): lax.all_to_all(array, AXES, split_axis=0, concat_axis=0, axis_index_group...  5.33 us
    pallas_call x1, Pallas kernels, pack(): pl.pallas_call(pack_kernel, out_shape=jax.ShapeDtypeStruct((8, MSG, 128),...  2.88 us
    ppermute x1, waiting for transfers between devices, shards(): kv_other = lax.ppermute(kv_mine, AXES, core_pairs())  2.43 us
    ppermute x1, waiting for transfers between devices, shards(): theirs = lax.ppermute(part_other, AXES, core_pairs())  2.29 us
  transfers between devices with their start and end apart: 3, of which 3 were waited for; matrix products, arithmetic and copies ran while one was open for 0% of the time, Pallas kernels for 0%

profile of v4, /device:TPU:0, one launch (start us, length us, event | category | flops | bytes accessed | tf_op | source)
XLA Modules:
  0.0 105.2 jit_solution(11403438506576493278)
XLA Ops:
  0.6 2.9 %pack.1 = bf16[8,592,128]{2,1,0:T(8,128)(2,1)} custom-call(bf16[32,64,128]{2,1,0:T(8,128)(2,1)} %q_hbm.1, bf16[32,64,128]{2,1,0:T(8,128)(2,1)} %g_hbm.1, bf16[32,64,128]{2,1,0:T(8,128)(2,1)} %o_hbm.1, bf16[32,8,128]{2,1,0:T(8,128)(2,1)} %k_hbm.1, bf16[32,8,128]{2,1,0:T(8,128)(2,1)} %v_hbm.1), custom_call_target="tpu_custom_call" | custom-call | tf_op jit(solution)/shard_map/pack/pallas_call | solution.py:296
  3.5 22.6 %all_to_all.20.msg_ref = bf16[8,592,128]{2,1,0:T(8,128)(2,1)S(1)} all-to-all(bf16[8,592,128]{2,1,0:T(8,128)(2,1)} %pack.1), channel_id=1, replica_groups={{0,2,32,34,64,66,96,98},{3,1,35,33,67,65,99,97},{4,6,36,38,68,70,100,10..., dimensions={0} | all-to-all | bytes 2424832 | tf_op jit(solution)/shard_map/all_to_all | solution.py:58
  26.2 0.2 broadcast_in_dim.2
  26.4 0.0 copy-start.3
  26.4 0.0 copy-start.2
  26.4 22.3 %all_to_all.21.kv0_ref = bf16[8,8,64,128]{3,2,1,0:T(8,128)(2,1)S(1)} all-to-all(bf16[8,8,64,128]{3,2,1,0:T(8,128)(2,1)S(1)} %broadcast_in_dim.2), channel_id=1, replica_groups={{0,3,4,7,8,11,12,15},{2,1,6,5,10,9,14,13},{16,19,20,23,24,27,28,31},{18..., dimensions={0} | all-to-all | bytes 2097152 | tf_op jit(solution)/shard_map/all_to_all | solution.py:58
  48.7 0.0 collective-permute-start
  48.7 0.1 pad_add_fusion.me_ref
  48.8 0.0 copy-done.3
  48.8 0.1 convert_reduce_fusion.1.start_ref
  49.0 2.4 %collective-permute-done.kv1_ref = bf16[8,8,64,128]{3,2,1,0:T(8,128)(2,1)S(1)} collective-permute-done((bf16[8,8,64,128]{3,2,1,0:T(8,128)(2,1)S(1)}, bf16[8,8,64,128]{3,2,1,0:T(8,128)(2,1)S(1)}, u32[]{:S(2)}, u32[]{:S(2)}) %collective-permute-start) | collective-permute-done | bytes 1048608 | tf_op jit(solution)/shard_map/ppermute | solution.py:369
  51.4 0.0 copy-done.2
  51.4 9.4 %attention.1 = (bf16[8,256,128]{2,1,0:T(8,128)(2,1)S(1)}, bf16[8,8,64,128]{3,2,1,0:T(8,128)(2,1)S(1)}, bf16[8,8,64,128]{3,2,1,0:T(8,128)(2,1)S(1)}) custom-call(s32[128]{0:T(128)S(1)} %copy-done.2, s32[8]{0:T(128)S(1)} %convert_reduce_fusion.1.start_ref, s32[2]{0:T(128)S(1)} %pad_add_fusion.me_ref, bf16[8,592,128]{2,1,0:T(8,128)(2,1)S(1)} %all_to_all.20.msg_ref, ...), custom_call_target="tpu_custom_call" | custom-call | tf_op jit(solution)/shard_map/attention/pallas_call | solution.py:326
  60.8 0.0 copy-start
  60.8 0.8 copy-done
  61.6 1.2 %collective-permute-start.1 = (bf16[8,8,64,128]{3,2,1,0:T(8,128)(2,1)S(1)}, bf16[8,8,64,128]{3,2,1,0:T(8,128)(2,1)S(1)}, u32[]{:S(2)}, u32[]{:S(2)}) collective-permute-start(bf16[8,8,64,128]{3,2,1,0:T(8,128)(2,1)S(1)} %get-tuple-element.8), channel_id=1, source_target_pairs={{0,16},{1,17},{2,18},{3,19},{4,20},{5,21},{6,22},{7,23},{8,24},{9,... | collective-permute-start | bytes 3145736 | tf_op jit(solution)/shard_map/ppermute | solution.py:371
  62.8 2.3 %collective-permute-done.1 = bf16[8,8,64,128]{3,2,1,0:T(8,128)(2,1)S(1)} collective-permute-done((bf16[8,8,64,128]{3,2,1,0:T(8,128)(2,1)S(1)}, bf16[8,8,64,128]{3,2,1,0:T(8,128)(2,1)S(1)}, u32[]{:S(2)}, u32[]{:S(2)}) %collective-permute-start.1) | collective-permute-done | bytes 1048608 | tf_op jit(solution)/shard_map/ppermute | solution.py:371
  65.1 1.4 %add_convert_fusion = bf16[8,8,64,128]{3,2,1,0:T(8,128)(2,1)} fusion(bf16[8,8,64,128]{3,2,1,0:T(8,128)(2,1)S(1)} %collective-permute-done.1, bf16[8,8,64,128]{3,2,1,0:T(8,128)(2,1)S(1)} %get-tuple-element.7), kind=kLoop, calls=%fused_computation.1 | loop fusion | flops 2097152 | bytes 3145728 | tf_op jit(solution)/shard_map/convert_element_type | solution.py:372
  66.4 0.0 copy-start.4
  66.4 5.3 %all-to-all-start.2 = ((bf16[8,8,64,128]{3,2,1,0:T(8,128)(2,1)}), bf16[8,8,64,128]{3,2,1,0:T(8,128)(2,1)S(1)}, u32[]{:S(2)}, u32[]{:S(2)}) async-start(bf16[8,8,64,128]{3,2,1,0:T(8,128)(2,1)} %add_convert_fusion), calls=%async_computation.2 | async-start | bytes 2097152 | tf_op jit(solution)/shard_map/all_to_all | solution.py:58
  71.8 0.0 copy-done.4
  71.8 0.0 copy-start.1
  71.8 0.1 mul.17
  71.9 0.1 mul.18
  71.9 17.1 %all-to-all-done.2 = bf16[8,8,64,128]{3,2,1,0:T(8,128)(2,1)S(1)} async-done(((bf16[8,8,64,128]{3,2,1,0:T(8,128)(2,1)}), bf16[8,8,64,128]{3,2,1,0:T(8,128)(2,1)S(1)}, u32[]{:S(2)}, u32[]{:S(2)}) %all-to-all-start.2) | async-done | bytes 1048608 | tf_op jit(solution)/shard_map/all_to_all | solution.py:58
  89.0 0.2 convert_reduce_fusion
  89.2 0.1 multiply_convert_fusion
  89.3 0.0 copy-done.1
  89.4 13.8 %all_to_all.22.back_ref = bf16[8,320,128]{2,1,0:T(8,128)(2,1)} all-to-all(bf16[8,320,128]{2,1,0:T(8,128)(2,1)S(1)} %pad_maximum_fusion), channel_id=1, replica_groups={{0,2,32,34,64,66,96,98},{3,1,35,33,67,65,99,97},{4,6,36,38,68,70,100,10..., dimensions={0} | all-to-all | bytes 1310720 | tf_op jit(solution)/shard_map/all_to_all | solution.py:58
  103.2 2.0 %unpack.1 = (bf16[32,64,128]{2,1,0:T(8,128)(2,1)}, bf16[32,8,128]{2,1,0:T(8,128)(2,1)}, bf16[32,8,128]{2,1,0:T(8,128)(2,1)}) custom-call(bf16[8,320,128]{2,1,0:T(8,128)(2,1)} %all_to_all.22.back_ref), custom_call_target="tpu_custom_call" | custom-call | tf_op jit(solution)/shard_map/unpack/pallas_call | solution.py:311
  (2 shorter events, 0.1 us)
Async XLA Ops:
  26.4 22.4 %copy-start.3 = (s32[4096]{0:T(1024)S(1)}, s32[4096]{0:T(1024)}, u32[]{:S(2)}) copy-start(s32[4096]{0:T(1024)} %param.13) | copy-start | bytes 49156
  26.4 25.0 %copy-start.2 = (s32[128]{0:T(128)S(1)}, s32[128]{0:T(128)}, u32[]{:S(2)}) copy-start(s32[128]{0:T(128)} %span_ref.1) | copy-start | bytes 1540
  48.7 2.7 %collective-permute-start = (bf16[8,8,64,128]{3,2,1,0:T(8,128)(2,1)S(1)}, bf16[8,8,64,128]{3,2,1,0:T(8,128)(2,1)S(1)}, u32[]{:S(2)}, u32[]{:S(2)}) collective-permute-start(bf16[8,8,64,128]{3,2,1,0:T(8,128)(2,1)S(1)} %all_to_all.21.kv0_ref), channel_id=1, source_target_pairs={{0,16},{1,17},{2,18},{3,19},{4,20},{5,21},{6,22},{7,23},{8,24},{9,... | collective-permute-start | bytes 3145736 | tf_op jit(solution)/shard_map/ppermute | solution.py:369
  60.8 0.8 copy-start
  61.6 3.5 %collective-permute-start.1 = (bf16[8,8,64,128]{3,2,1,0:T(8,128)(2,1)S(1)}, bf16[8,8,64,128]{3,2,1,0:T(8,128)(2,1)S(1)}, u32[]{:S(2)}, u32[]{:S(2)}) collective-permute-start(bf16[8,8,64,128]{3,2,1,0:T(8,128)(2,1)S(1)} %get-tuple-element.8), channel_id=1, source_target_pairs={{0,16},{1,17},{2,18},{3,19},{4,20},{5,21},{6,22},{7,23},{8,24},{9,... | collective-permute-start | bytes 3145736 | tf_op jit(solution)/shard_map/ppermute | solution.py:371
  66.4 5.3 %copy-start.4 = (f32[2]{0:T(128)S(1)}, f32[2]{0:T(128)}, u32[]{:S(2)}) copy-start(f32[2]{0:T(128)} %constant.41.clone) | copy-start | bytes 28
  66.4 22.6 %all-to-all-start.2 = ((bf16[8,8,64,128]{3,2,1,0:T(8,128)(2,1)}), bf16[8,8,64,128]{3,2,1,0:T(8,128)(2,1)S(1)}, u32[]{:S(2)}, u32[]{:S(2)}) async-start(bf16[8,8,64,128]{3,2,1,0:T(8,128)(2,1)} %add_convert_fusion), calls=%async_computation.2 | async-start | bytes 2097152 | tf_op jit(solution)/shard_map/all_to_all | solution.py:58
  71.8 17.5 %copy-start.1 = (bf16[8,256,128]{2,1,0:T(8,128)(2,1)S(1)}, bf16[8,256,128]{2,1,0:T(8,128)(2,1)}, u32[]{:S(2)}) copy-start(bf16[8,256,128]{2,1,0:T(8,128)(2,1)} %copy-done) | copy-start | bytes 1572868

commit v5 on v4

--- a/solution.py
+++ b/solution.py
@@ -14,9 +14,11 @@
 TOK = 32
 GROUP = 8
 ROWS = TOK * GROUP
-KV0 = 2 * ROWS
-DEL0 = KV0 + 2 * TOK
+DEL0 = 2 * ROWS
 MSG = DEL0 + 16
+PART = 2 * TOK
+SHARE = ((3, 1, 6), (5, 4, 2))
+LAST = 7
 TK = 256
 LENGTH = 4096
 PAD = LENGTH + 256
@@ -41,22 +43,33 @@
     ]
 
 
-def seq_groups():
-    return [
-        [linear(x, core, c >> 1, side ^ (c & 1), c & 1) for c in range(8)]
-        for x in range(4)
-        for core in range(2)
-        for side in range(2)
-    ]
-
-
 def core_pairs():
     return [(i, i ^ 16) for i in range(128)]
 
 
-def exchange(array, groups):
+def seq_pairs(flips):
+    pairs = []
+    for x in range(4):
+        for core in range(2):
+            for z in range(4):
+                for y in range(4):
+                    e = flips[core]
+                    pairs.append(
+                        (
+                            linear(x, core, z, y % 2, y // 2),
+                            linear(x, core, z ^ (e >> 1), y % 2 ^ (e & 1), y // 2 ^ (e & 1)),
+                        )
+                    )
+    return pairs
+
+
+def to_core(array):
+    return lax.ppermute(array, AXES, core_pairs())
+
+
+def exchange(array):
     return lax.all_to_all(
-        array, AXES, split_axis=0, concat_axis=0, axis_index_groups=groups, tiled=True
+        array, AXES, split_axis=0, concat_axis=0, axis_index_groups=head_groups(), tiled=True
     )
 
 
@@ -64,11 +77,21 @@
     return jnp.dot(a, b, preferred_element_type=F32)
 
 
-def pack_kernel(q_hbm, g_hbm, o_hbm, k_hbm, v_hbm, out_ref, q_v, g_v, o_v, k_v, v_v, wide, sem):
+def pack_kv_kernel(k_hbm, v_hbm, out_ref, k_v, v_v, wide, sem):
     copies = []
-    for n, (src, dst) in enumerate(
-        ((g_hbm, g_v), (o_hbm, o_v), (q_hbm, q_v), (k_hbm, k_v), (v_hbm, v_v))
-    ):
+    for n, (src, dst) in enumerate(((k_hbm, k_v), (v_hbm, v_v))):
+        copies.append(pltpu.make_async_copy(src, dst, sem.at[n]))
+        copies[n].start()
+    for n, ref in ((0, k_v), (1, v_v)):
+        copies[n].wait()
+        wide[n] = ref[...].reshape(ROWS, 128).astype(F32)
+        for j in range(8):
+            out_ref[j, n * TOK : n * TOK + TOK, :] = wide[n, pl.ds(j, TOK, 8), :].astype(BF16)
+
+
+def pack_q_kernel(q_hbm, g_hbm, o_hbm, out_ref, q_v, g_v, o_v, sem):
+    copies = []
+    for n, (src, dst) in enumerate(((g_hbm, g_v), (o_hbm, o_v), (q_hbm, q_v))):
         copies.append(pltpu.make_async_copy(src, dst, sem.at[n]))
         copies[n].start()
     ones = jnp.ones((8, 128), BF16)
@@ -81,7 +104,7 @@
         for half in range(2):
             j = 2 * pair + half
             sub = slice(8 * half, 8 * half + 8)
-            out_ref[j, ROWS:KV0, :] = g[:, sub, :].reshape(ROWS, 128).astype(BF16)
+            out_ref[j, ROWS:DEL0, :] = g[:, sub, :].reshape(ROWS, 128).astype(BF16)
             part = prod[:, sub, :].reshape(ROWS, 128)
             top = part.astype(BF16)
             rest = (part - top.astype(F32)).astype(BF16)
@@ -100,45 +123,55 @@
         for half in range(2):
             sub = slice(8 * half, 8 * half + 8)
             out_ref[2 * pair + half, 0:ROWS, :] = q[:, sub, :].reshape(ROWS, 128).astype(BF16)
-    for n, ref in ((0, k_v), (1, v_v)):
-        copies[3 + n].wait()
-        wide[...] = ref[...].reshape(ROWS, 128).astype(F32)
-        for j in range(8):
-            at = KV0 + n * TOK
-            out_ref[j, at : at + TOK, :] = wide[pl.ds(j, TOK, 8), :].astype(BF16)
-
-
-def unpack_kernel(back_ref, q_hbm, k_hbm, v_hbm, q_v, k_v, v_v, wide, sem):
+
+
+def unpack_q_kernel(back_ref, q_hbm, q_v, sem):
     copies = []
-    for n, (src, dst) in enumerate(((k_v, k_hbm), (v_v, v_hbm))):
-        for j in range(8):
-            at = ROWS + n * TOK
-            wide[pl.ds(j, TOK, 8), :] = back_ref[j, at : at + TOK, :].astype(F32)
-        src[...] = wide[...].reshape(TOK, 8, 128).astype(BF16)
-        copies.append(pltpu.make_async_copy(src, dst, sem.at[n]))
-        copies[-1].start()
     for pair in range(4):
         cols = pl.ds(16 * pair, 16)
         sides = [
-            back_ref[2 * pair + half, 0:ROWS, :].astype(F32).reshape(TOK, 8, 128)
-            for half in range(2)
+            back_ref[2 * pair + half].astype(F32).reshape(TOK, 8, 128) for half in range(2)
         ]
         q_v[:, cols, :] = jnp.concatenate(sides, axis=1).astype(BF16)
         copies.append(
-            pltpu.make_async_copy(q_v.at[:, cols, :], q_hbm.at[:, cols, :], sem.at[2 + pair])
+            pltpu.make_async_copy(q_v.at[:, cols, :], q_hbm.at[:, cols, :], sem.at[pair])
         )
         copies[-1].start()
     for copy in copies:
         copy.wait()
 
 
+def unpack_kv_kernel(back_ref, k_hbm, v_hbm, k_v, v_v, wide, sem):
+    copies = []
+    for n, (src, dst) in enumerate(((k_v, k_hbm), (v_v, v_hbm))):
+        for j in range(8):
+            wide[n, pl.ds(j, TOK, 8), :] = back_ref[j, n * TOK : n * TOK + TOK, :].astype(F32)
+        src[...] = wide[n].reshape(TOK, 8, 128).astype(BF16)
+        copies.append(pltpu.make_async_copy(src, dst, sem.at[n]))
+        copies[-1].start()
+    for copy in copies:
+        copy.wait()
+
+
 def stored_block(core, c, i):
     y_hi = c % 2
     return linear(i // 2, core, c // 2, (i + c) % 2, y_hi)
 
 
+def chunk_places(span_ref, core, c):
+    first = core * 16 + c // 2 * 4 + c % 2
+    even = first + c % 2 * 2
+    odd = first + 2 - c % 2 * 2
+    return [
+        pl.multiple_of(span_ref[i // 2 * 32 + (odd if i % 2 else even)] * TOK, TOK)
+        for i in range(8)
+    ]
+
+
 def attn_kernel(
-    span_ref, start_ref, me_ref, msg_ref, kv0_ref, kv1_ref,
+    span_ref, start_ref, me_ref, msg_ref,
+    kv0_ref, kv1_ref, mine0_ref, mine1_ref, mine2_ref, mine3_ref,
+    theirs0_ref, theirs1_ref, theirs2_ref, theirs3_ref,
     dq_ref, part0_ref, part1_ref,
     unit_q, unit_at, k_s, kt_s, v_s, qt_s, gt_s, d_s, hi_s, lo_s, dk_s, dv_s, dq_s, m_s, l_s, w_s, s_s,
 ):
@@ -150,13 +183,19 @@
     k_s[LENGTH:, :] = jnp.zeros((PAD - LENGTH, 128), BF16)
     v_s[LENGTH:, :] = jnp.zeros((PAD - LENGTH, 128), BF16)
 
-    for c in range(8):
-        for i in range(8):
-            for other, ref in ((0, kv0_ref), (1, kv1_ref)):
-                who = core if other == 0 else 1 - core
-                at = pl.multiple_of(span_ref[stored_block(who, c, i)] * TOK, TOK)
-                k_s[pl.ds(at, TOK), :] = ref[c, i, 0:TOK, :]
-                v_s[pl.ds(at, TOK), :] = ref[c, i, TOK : 2 * TOK, :]
+    share = [jnp.where(core == 0, a, b) for a, b in zip(*SHARE)]
+    share_other = [jnp.where(core == 0, b, a) for a, b in zip(*SHARE)]
+    chunks = [(kv0_ref, None, core, 0), (kv1_ref, None, 1 - core, 0)]
+    chunks += [(mine3_ref, None, core, LAST), (theirs3_ref, None, 1 - core, LAST)]
+    for n, ref in enumerate((mine0_ref, mine1_ref, mine2_ref)):
+        chunks += [(ref, 0, core, share[n]), (ref, 1, 1 - core, share[n])]
+    for n, ref in enumerate((theirs0_ref, theirs1_ref, theirs2_ref)):
+        chunks += [(ref, 0, 1 - core, share_other[n]), (ref, 1, core, share_other[n])]
+    for ref, side, who, e in chunks:
+        for i, at in enumerate(chunk_places(span_ref, who, mine ^ e)):
+            part = ref[i] if side is None else ref[side, i]
+            k_s[pl.ds(at, TOK), :] = part[0:TOK]
+            v_s[pl.ds(at, TOK), :] = part[TOK:PART]
     zero = jnp.zeros((256, 128), F32)
     for at in range(0, PAD, 256):
         dk_s[at : at + 256, :] = zero
@@ -189,7 +228,7 @@
         lax.fori_loop(0, tiles, enlist, 0)
         count = count + tiles
         qt_s[i] = msg_ref[i, 0:ROWS, :].T
-        gt_s[i] = msg_ref[i, ROWS:KV0, :].T
+        gt_s[i] = msg_ref[i, ROWS:DEL0, :].T
         tail = msg_ref[i, DEL0:MSG, :].astype(F32)
         halves = [tail[n : n + 1] + tail[n + 1 : n + 2] + tail[n + 2 : n + 3] for n in (0, 8)]
         d_s[i] = jnp.broadcast_to(jnp.concatenate(halves, axis=1), (8, ROWS))
@@ -247,7 +286,7 @@
 
     def grads_rest(results):
         for i, at, p, ds in results:
-            dv_s[pl.ds(at, TK), :] += dot(p, msg_ref[i, ROWS:KV0, :])
+            dv_s[pl.ds(at, TK), :] += dot(p, msg_ref[i, ROWS:DEL0, :])
             dk_s[pl.ds(at, TK), :] += dot(ds, msg_ref[i, 0:ROWS, :])
             dq_s[i] += dot(kt_s[:, pl.ds(at, TK)], ds)
 
@@ -271,13 +310,12 @@
     for i in range(8):
         dq_ref[i, :, :] = (dq_s[i] * scale).T.astype(BF16)
 
-    for c in range(8):
-        for i in range(8):
-            for other, ref in ((0, part0_ref), (1, part1_ref)):
-                who = core if other == 0 else 1 - core
-                at = pl.multiple_of(span_ref[stored_block(who, c, i)] * TOK, TOK)
-                ref[c, i, 0:TOK, :] = dk_s[pl.ds(at, TOK), :].astype(BF16)
-                ref[c, i, TOK : 2 * TOK, :] = dv_s[pl.ds(at, TOK), :].astype(BF16)
+    for ref, me, flips in ((part0_ref, core, share), (part1_ref, 1 - core, share_other)):
+        slots = [(who, e) for e in flips for who in (me, 1 - me)] + [(me, LAST), (me, 0)]
+        for slot, (who, e) in enumerate(slots):
+            for i, at in enumerate(chunk_places(span_ref, who, mine ^ e)):
+                ref[slot, i, 0:TOK, :] = dk_s[pl.ds(at, TOK), :].astype(BF16)
+                ref[slot, i, TOK:PART, :] = dv_s[pl.ds(at, TOK), :].astype(BF16)
 
 
 def vmem():
@@ -292,41 +330,69 @@
     return pl.BlockSpec(memory_space=pl.ANY)
 
 
-def pack(queries, out_grads, out_states, keys, values):
+def cost(megabytes):
+    return pl.CostEstimate(flops=0, bytes_accessed=megabytes << 20, transcendentals=0)
+
+
+def pack_kv(keys, values):
     return pl.pallas_call(
-        pack_kernel,
+        pack_kv_kernel,
+        out_shape=jax.ShapeDtypeStruct((8, PART, 128), BF16),
+        in_specs=[hbm()] * 2,
+        out_specs=vmem(),
+        scratch_shapes=[pltpu.VMEM((TOK, 8, 128), BF16)] * 2
+        + [pltpu.VMEM((2, ROWS, 128), F32), pltpu.SemaphoreType.DMA((2,))],
+        compiler_params=pltpu.CompilerParams(vmem_limit_bytes=58 << 20),
+        name="pack_kv",
+    )(keys, values)
+
+
+def pack_q(queries, out_grads, out_states):
+    return pl.pallas_call(
+        pack_q_kernel,
         out_shape=jax.ShapeDtypeStruct((8, MSG, 128), BF16),
-        in_specs=[hbm()] * 5,
+        in_specs=[hbm()] * 3,
         out_specs=vmem(),
-        scratch_shapes=[pltpu.VMEM((TOK, 64, 128), BF16)] * 3
-        + [pltpu.VMEM((TOK, 8, 128), BF16)] * 2
-        + [pltpu.VMEM((ROWS, 128), F32), pltpu.SemaphoreType.DMA((5,))],
+        scratch_shapes=[pltpu.VMEM((TOK, 64, 128), BF16)] * 3 + [pltpu.SemaphoreType.DMA((3,))],
         compiler_params=pltpu.CompilerParams(vmem_limit_bytes=58 << 20),
-        name="pack",
-    )(queries, out_grads, out_states, keys, values)
-
-
-def unpack(back):
+        cost_estimate=cost(8),
+        name="pack_q",
+    )(queries, out_grads, out_states)
+
+
+def unpack_q(back):
+    return pl.pallas_call(
+        unpack_q_kernel,
+        out_shape=jax.ShapeDtypeStruct((TOK, 64, 128), BF16),
+        in_specs=[vmem()],
+        out_specs=hbm(),
+        scratch_shapes=[pltpu.VMEM((TOK, 64, 128), BF16), pltpu.SemaphoreType.DMA((4,))],
+        compiler_params=pltpu.CompilerParams(vmem_limit_bytes=58 << 20),
+        cost_estimate=cost(6),
+        name="unpack_q",
+    )(back)
+
+
+def unpack_kv(back):
     small = jax.ShapeDtypeStruct((TOK, 8, 128), BF16)
     return pl.pallas_call(
-        unpack_kernel,
-        out_shape=(jax.ShapeDtypeStruct((TOK, 64, 128), BF16), small, small),
+        unpack_kv_kernel,
+        out_shape=(small, small),
         in_specs=[vmem()],
-        out_specs=(hbm(),) * 3,
-        scratch_shapes=[pltpu.VMEM((TOK, 64, 128), BF16)]
-        + [pltpu.VMEM((TOK, 8, 128), BF16)] * 2
-        + [pltpu.VMEM((ROWS, 128), F32), pltpu.SemaphoreType.DMA((6,))],
+        out_specs=(hbm(),) * 2,
+        scratch_shapes=[pltpu.VMEM((TOK, 8, 128), BF16)] * 2
+        + [pltpu.VMEM((2, ROWS, 128), F32), pltpu.SemaphoreType.DMA((2,))],
         compiler_params=pltpu.CompilerParams(vmem_limit_bytes=58 << 20),
-        name="unpack",
+        name="unpack_kv",
     )(back)
 
 
-def attention(span_position, starts, me, message, kv_mine, kv_other):
-    kv_shape = jax.ShapeDtypeStruct((8, 8, 2 * TOK, 128), BF16)
+def attention(span_position, starts, me, message, parts):
+    kv_shape = jax.ShapeDtypeStruct((8, 8, PART, 128), BF16)
     return pl.pallas_call(
         attn_kernel,
         out_shape=(jax.ShapeDtypeStruct((8, ROWS, 128), BF16), kv_shape, kv_shape),
-        in_specs=[smem()] * 3 + [vmem()] * 3,
+        in_specs=[smem()] * 3 + [vmem()] * 11,
         out_specs=(vmem(),) * 3,
         scratch_shapes=[
             pltpu.SMEM((UNITS,), jnp.int32),
@@ -349,7 +415,7 @@
         ],
         compiler_params=pltpu.CompilerParams(vmem_limit_bytes=32 << 20),
         name="attention",
-    )(span_position, starts, me, message, kv_mine, kv_other)
+    )(span_position, starts, me, message, *parts)
 
 
 def shards(queries, keys, values, out_states, out_grads, segment_ids, span_position):
@@ -360,21 +426,32 @@
     starts = jnp.sum(
         segment_ids[None, :] < jnp.arange(8, dtype=jnp.int32)[:, None], axis=1, dtype=jnp.int32
     )
-    message = pack(queries, out_grads, out_states, keys, values)
-    message = exchange(message, head_groups())
-    kv_part = message[:, KV0:DEL0, :]
-    kv_mine = exchange(
-        jnp.broadcast_to(kv_part[None], (8, 8, 2 * TOK, 128)), seq_groups()
-    )
-    kv_other = lax.ppermute(kv_mine, AXES, core_pairs())
-    dq, part_mine, part_other = attention(span_position, starts, me, message, kv_mine, kv_other)
-    theirs = lax.ppermute(part_other, AXES, core_pairs())
-    part = (part_mine.astype(F32) + theirs.astype(F32)).astype(BF16)
-    part = exchange(part, seq_groups())
-    total = jnp.sum(part.astype(F32), axis=0).reshape(8, 2, TOK, 128)
+    kv = exchange(pack_kv(keys, values))
+    message = pack_q(queries, out_grads, out_states)
+    kv, message = lax.optimization_barrier((kv, message))
+    kv_theirs = to_core(kv)
+    kv_theirs, message = lax.optimization_barrier((kv_theirs, message))
+    message = exchange(message)
+    both = jnp.stack([kv, kv_theirs])
+    got = [lax.ppermute(both, AXES, seq_pairs(flips)) for flips in zip(*SHARE)]
+    got.append(lax.ppermute(kv, AXES, seq_pairs((LAST, LAST))))
+    parts = [kv, kv_theirs] + got + [to_core(part) for part in got]
+    dq, mine, other = attention(span_position, starts, me, message, parts)
+    part = (mine.astype(F32) + to_core(other).astype(F32)).astype(BF16)
+    part, dq = lax.optimization_barrier((part, dq))
+    dq = exchange(dq)
+    got = [
+        lax.ppermute(part[2 * n : 2 * n + 2], AXES, seq_pairs(flips)).astype(F32)
+        for n, flips in enumerate(zip(*SHARE))
+    ]
+    last = lax.ppermute(part[6], AXES, seq_pairs((LAST, LAST)))
+    total = part[7].astype(F32) + last.astype(F32) + got[0][0] + got[1][0] + got[2][0]
+    give = got[0][1] + got[1][1] + got[2][1]
+    total, give, dq = lax.optimization_barrier((total, give, dq))
     factor = jnp.array([1.0 / math.sqrt(128), 1.0], F32).reshape(1, 2, 1, 1)
-    total = (total * factor).astype(BF16).reshape(8, 2 * TOK, 128)
-    return unpack(exchange(jnp.concatenate([dq, total], axis=1), head_groups()))
+    total = ((total + to_core(give)).reshape(8, 2, TOK, 128) * factor).astype(BF16)
+    back = exchange(total.reshape(8, PART, 128))
+    return (unpack_q(dq),) + tuple(unpack_kv(back))
 
 
 def solution(mesh):

time: 106 us -> 94.4 us (0.89)
  blocking collectives: 58.8 us -> 0 us
  starting transfers between devices: 6.52 us -> 47.1 us
  waiting for transfers between devices: 21.8 us -> 29 us
    all_to_all x3 -> x0, blocking collectives: 58.8 us -> none  [exchange(): lax.all_to_all(array, AXES, split_axis=0, concat_axis=0, axis_index_group...]
    ppermute x2 -> x15, starting transfers between devices: 1.2 us -> 30.3 us  [the longest x7 10.6 us: to_core(): return lax.ppermute(array, AXES, core_pairs())]
    ppermute x2 -> x15, waiting for transfers between devices: 4.72 us -> 17.2 us  [the longest x3 6.9 us: shards(): got = [lax.ppermute(both, AXES, seq_pairs(flips)) for flips in zip(*SHARE)]]
    all_to_all x1 -> x4, starting transfers between devices: 5.33 us -> 16.7 us  [exchange(): lax.all_to_all(array, AXES, split_axis=0, concat_axis=0, axis_index_group...]
    all_to_all x1 -> x4, waiting for transfers between devices: 17.1 us -> 11.8 us  [exchange(): lax.all_to_all(array, AXES, split_axis=0, concat_axis=0, axis_index_group...]
    pallas_call x2 -> x4, Pallas kernels: 4.89 us -> 7.84 us  [the longest x1 2.76 us: pack_q(): pl.pallas_call(pack_q_kernel, out_shape=jax.ShapeDtypeStruct((8, MSG, 128...]
    pallas_call x1, Pallas kernels: 9.38 us -> 6.99 us  [attention(): pl.pallas_call(attn_kernel, out_shape=(jax.ShapeDtypeStruct((8, ROWS, 128...]
  transfers between devices with their start and end apart: 3 -> 19, of which waited for: 3 -> 11; matrix products, arithmetic and copies ran while one was open for 0% -> 1% of each run, Pallas kernels for 0% -> 5%
where the time goes in v5:
time: 94.4 us; the launch traced here: 94.3 us
  starting transfers between devices  47.1 us (50%)
  waiting for transfers between devices  29 us (31%)
  Pallas kernels  14.8 us (16%)
  other arithmetic  1.64 us (2%)
    all_to_all x4, starting transfers between devices, exchange(): lax.all_to_all(array, AXES, split_axis=0, concat_axis=0, axis_index_group...  16.7 us
    all_to_all x4, waiting for transfers between devices, exchange(): lax.all_to_all(array, AXES, split_axis=0, concat_axis=0, axis_index_group...  11.8 us
    ppermute x7, starting transfers between devices, to_core(): return lax.ppermute(array, AXES, core_pairs())  10.6 us
    ppermute x3, starting transfers between devices, shards(): got = [lax.ppermute(both, AXES, seq_pairs(flips)) for flips in zip(*SHARE)]  7.19 us
    pallas_call x1, Pallas kernels, attention(): pl.pallas_call(attn_kernel, out_shape=(jax.ShapeDtypeStruct((8, ROWS, 128...  6.99 us
    ppermute x3, waiting for transfers between devices, shards(): got = [lax.ppermute(both, AXES, seq_pairs(flips)) for flips in zip(*SHARE)]  6.9 us
    ppermute x3, starting transfers between devices, shards(): lax.ppermute(part[2 * n:2 * n + 2], AXES, seq_pairs(flips)).astype(F32)  6.65 us
    ppermute x7, waiting for transfers between devices, to_core(): return lax.ppermute(array, AXES, core_pairs())  6 us
  transfers between devices with their start and end apart: 19, of which 11 were waited for; matrix products, arithmetic and copies ran while one was open for 1% of the time, Pallas kernels for 5%

profile of v5, /device:TPU:0, one launch (start us, length us, event | category | flops | bytes accessed | tf_op | source)
XLA Modules:
  0.0 94.3 jit_solution(7954984233506797662)
XLA Ops:
  0.6 1.6 %pack_kv.1 = bf16[8,64,128]{2,1,0:T(8,128)(2,1)} custom-call(bf16[32,8,128]{2,1,0:T(8,128)(2,1)} %k_hbm.1, bf16[32,8,128]{2,1,0:T(8,128)(2,1)} %v_hbm.1), custom_call_target="tpu_custom_call" | custom-call | tf_op jit(solution)/shard_map/pack_kv/pallas_call | solution.py:338
  2.2 5.4 %all-to-all-start = ((bf16[8,64,128]{2,1,0:T(8,128)(2,1)}), bf16[8,64,128]{2,1,0:T(8,128)(2,1)S(1)}, u32[]{:S(2)}, u32[]{:S(2)}) async-start(bf16[8,64,128]{2,1,0:T(8,128)(2,1)} %pack_kv.1), calls=%async_computation | async-start | bytes 262144 | tf_op jit(solution)/shard_map/all_to_all | solution.py:71
  7.6 2.8 %pack_q.1 = bf16[8,528,128]{2,1,0:T(8,128)(2,1)} custom-call(bf16[32,64,128]{2,1,0:T(8,128)(2,1)} %q_hbm.1, bf16[32,64,128]{2,1,0:T(8,128)(2,1)} %g_hbm.1, bf16[32,64,128]{2,1,0:T(8,128)(2,1)} %o_hbm.1), custom_call_target="tpu_custom_call" | custom-call | bytes 8388608 | tf_op jit(solution)/shard_map/pack_q/pallas_call | solution.py:351
  10.4 0.0 copy-start.3
  10.4 0.0 copy-start
  10.4 3.6 %all-to-all-done.kv0_ref = bf16[8,64,128]{2,1,0:T(8,128)(2,1)S(1)} async-done(((bf16[8,64,128]{2,1,0:T(8,128)(2,1)}), bf16[8,64,128]{2,1,0:T(8,128)(2,1)S(1)}, u32[]{:S(2)}, u32[]{:S(2)}) %all-to-all-start) | async-done | bytes 131104 | tf_op jit(solution)/shard_map/all_to_all | solution.py:71
  14.0 0.0 collective-permute-start
  14.0 1.3 %collective-permute-done.kv1_ref = bf16[8,64,128]{2,1,0:T(8,128)(2,1)S(1)} collective-permute-done((bf16[8,64,128]{2,1,0:T(8,128)(2,1)S(1)}, bf16[8,64,128]{2,1,0:T(8,128)(2,1)S(1)}, u32[]{:S(2)}, u32[]{:S(2)}) %collective-permute-start) | collective-permute-done | bytes 131104 | tf_op jit(solution)/shard_map/ppermute | solution.py:67
  15.4 3.6 %all-to-all-start.1 = ((bf16[8,528,128]{2,1,0:T(8,128)(2,1)}), bf16[8,528,128]{2,1,0:T(8,128)(2,1)S(1)}, u32[]{:S(2)}, u32[]{:S(2)}) async-start(bf16[8,528,128]{2,1,0:T(8,128)(2,1)} %pack_q.1), calls=%async_computation.1 | async-start | bytes 2162688 | tf_op jit(solution)/shard_map/all_to_all | solution.py:71
  19.0 3.6 %collective-permute-start.1 = (bf16[2,8,64,128]{3,2,1,0:T(8,128)(2,1)S(1)}, bf16[2,8,64,128]{3,2,1,0:T(8,128)(2,1)S(1)}, u32[]{:S(2)}, u32[]{:S(2)}) collective-permute-start(bf16[2,8,64,128]{3,2,1,0:T(8,128)(2,1)S(1)} %pad_maximum_fusion), channel_id=1, source_target_pairs={{0,7},{2,5},{1,6},{3,4},{4,3},{6,1},{5,2},{7,0},{8,15},{10,13},{9,... | collective-permute-start | bytes 786440 | tf_op jit(solution)/shard_map/ppermute | solution.py:436
  22.6 1.1 %collective-permute-start.2 = (bf16[2,8,64,128]{3,2,1,0:T(8,128)(2,1)S(1)}, bf16[2,8,64,128]{3,2,1,0:T(8,128)(2,1)S(1)}, u32[]{:S(2)}, u32[]{:S(2)}) collective-permute-start(bf16[2,8,64,128]{3,2,1,0:T(8,128)(2,1)S(1)} %pad_maximum_fusion), channel_id=1, source_target_pairs={{0,3},{2,1},{1,2},{3,0},{4,7},{6,5},{5,6},{7,4},{8,11},{10,9},{9,1... | collective-permute-start | bytes 786440 | tf_op jit(solution)/shard_map/ppermute | solution.py:436
  23.7 2.5 %collective-permute-start.3 = (bf16[2,8,64,128]{3,2,1,0:T(8,128)(2,1)S(1)}, bf16[2,8,64,128]{3,2,1,0:T(8,128)(2,1)S(1)}, u32[]{:S(2)}, u32[]{:S(2)}) collective-permute-start(bf16[2,8,64,128]{3,2,1,0:T(8,128)(2,1)S(1)} %pad_maximum_fusion), channel_id=1, source_target_pairs={{0,12},{2,14},{1,13},{3,15},{4,8},{6,10},{5,9},{7,11},{8,4},{10,6}... | collective-permute-start | bytes 786440 | tf_op jit(solution)/shard_map/ppermute | solution.py:436
  26.2 2.3 %collective-permute-start.4 = (bf16[8,64,128]{2,1,0:T(8,128)(2,1)S(1)}, bf16[8,64,128]{2,1,0:T(8,128)(2,1)S(1)}, u32[]{:S(2)}, u32[]{:S(2)}) collective-permute-start(bf16[8,64,128]{2,1,0:T(8,128)(2,1)S(1)} %all-to-all-done.kv0_ref), channel_id=1, source_target_pairs={{0,15},{2,13},{1,14},{3,12},{4,11},{6,9},{5,10},{7,8},{8,7},{10,5}... | collective-permute-start | bytes 393224 | tf_op jit(solution)/shard_map/ppermute | solution.py:437
  28.5 0.0 collective-permute-done.1.mine0_ref
  28.5 2.1 %collective-permute-start.5 = (bf16[2,8,64,128]{3,2,1,0:T(8,128)(2,1)S(1)}, bf16[2,8,64,128]{3,2,1,0:T(8,128)(2,1)S(1)}, u32[]{:S(2)}, u32[]{:S(2)}) collective-permute-start(bf16[2,8,64,128]{3,2,1,0:T(8,128)(2,1)S(1)} %collective-permute-done.1.mine0_ref), channel_id=1, source_target_pairs={{0,16},{1,17},{2,18},{3,19},{4,20},{5,21},{6,22},{7,23},{8,24},{9,... | collective-permute-start | bytes 786440 | tf_op jit(solution)/shard_map/ppermute | solution.py:67
  30.6 4.5 %collective-permute-done.2.mine1_ref = bf16[2,8,64,128]{3,2,1,0:T(8,128)(2,1)S(1)} collective-permute-done((bf16[2,8,64,128]{3,2,1,0:T(8,128)(2,1)S(1)}, bf16[2,8,64,128]{3,2,1,0:T(8,128)(2,1)S(1)}, u32[]{:S(2)}, u32[]{:S(2)}) %collective-permute-start.2) | collective-permute-done | bytes 262176 | tf_op jit(solution)/shard_map/ppermute | solution.py:436
  35.1 0.2 collective-permute-start.6
  35.3 2.4 %collective-permute-done.3.mine2_ref = bf16[2,8,64,128]{3,2,1,0:T(8,128)(2,1)S(1)} collective-permute-done((bf16[2,8,64,128]{3,2,1,0:T(8,128)(2,1)S(1)}, bf16[2,8,64,128]{3,2,1,0:T(8,128)(2,1)S(1)}, u32[]{:S(2)}, u32[]{:S(2)}) %collective-permute-start.3) | collective-permute-done | bytes 262176 | tf_op jit(solution)/shard_map/ppermute | solution.py:436
  37.7 0.0 collective-permute-start.7
  37.7 0.0 collective-permute-done.4.mine3_ref
  37.7 0.5 collective-permute-start.8
  38.3 0.1 pad_add_fusion.me_ref
  38.3 0.0 copy-done.3
  38.3 0.1 convert_reduce_fusion.start_ref
  38.5 1.0 %collective-permute-done.8.theirs3_ref = bf16[8,64,128]{2,1,0:T(8,128)(2,1)S(1)} collective-permute-done((bf16[8,64,128]{2,1,0:T(8,128)(2,1)S(1)}, bf16[8,64,128]{2,1,0:T(8,128)(2,1)S(1)}, u32[]{:S(2)}, u32[]{:S(2)}) %collective-permute-start.8) | collective-permute-done | bytes 131104 | tf_op jit(solution)/shard_map/ppermute | solution.py:67
  39.5 0.0 collective-permute-done.5.theirs0_ref
  39.5 0.0 collective-permute-done.6.theirs1_ref
  39.5 0.0 collective-permute-done.7.theirs2_ref
  39.5 0.0 all-to-all-done.1.msg_ref
  39.5 0.0 copy-done
  39.5 7.0 %attention.1 = (bf16[8,256,128]{2,1,0:T(8,128)(2,1)}, bf16[8,8,64,128]{3,2,1,0:T(8,128)(2,1)S(1)}, bf16[8,8,64,128]{3,2,1,0:T(8,128)(2,1)S(1)}) custom-call(s32[128]{0:T(128)S(1)} %copy-done, s32[8]{0:T(128)S(1)} %convert_reduce_fusion.start_ref, s32[2]{0:T(128)S(1)} %pad_add_fusion.me_ref, bf16[8,528,128]{2,1,0:T(8,128)(2,1)S(1)} %all-to-all-done.1.msg_ref, ...), custom_call_target="tpu_custom_call" | custom-call | tf_op jit(solution)/shard_map/attention/pallas_call | solution.py:392
  46.5 7.7 %collective-permute-start.9 = (bf16[8,8,64,128]{3,2,1,0:T(8,128)(2,1)S(1)}, bf16[8,8,64,128]{3,2,1,0:T(8,128)(2,1)S(1)}, u32[]{:S(2)}, u32[]{:S(2)}) collective-permute-start(bf16[8,8,64,128]{3,2,1,0:T(8,128)(2,1)S(1)} %get-tuple-element.22), channel_id=1, source_target_pairs={{0,16},{1,17},{2,18},{3,19},{4,20},{5,21},{6,22},{7,23},{8,24},{9,... | collective-permute-start | bytes 3145736 | tf_op jit(solution)/shard_map/ppermute | solution.py:67
  54.2 2.3 %collective-permute-done.9 = bf16[8,8,64,128]{3,2,1,0:T(8,128)(2,1)S(1)} collective-permute-done((bf16[8,8,64,128]{3,2,1,0:T(8,128)(2,1)S(1)}, bf16[8,8,64,128]{3,2,1,0:T(8,128)(2,1)S(1)}, u32[]{:S(2)}, u32[]{:S(2)}) %collective-permute-start.9) | collective-permute-done | bytes 1048608 | tf_op jit(solution)/shard_map/ppermute | solution.py:67
  56.5 0.4 add_convert_fusion
  56.9 0.1 fusion.4
  57.0 4.3 %collective-permute-start.11 = (bf16[2,8,64,128]{3,2,1,0:T(8,128)(2,1)S(1)}, bf16[2,8,64,128]{3,2,1,0:T(8,128)(2,1)S(1)}, u32[]{:S(2)}, u32[]{:S(2)}) collective-permute-start(bf16[2,8,64,128]{3,2,1,0:T(8,128)(2,1)S(1)} %get-tuple-element.31), channel_id=1, source_target_pairs={{0,7},{2,5},{1,6},{3,4},{4,3},{6,1},{5,2},{7,0},{8,15},{10,13},{9,... | collective-permute-start | bytes 786440 | tf_op jit(solution)/shard_map/ppermute | solution.py:444
  61.2 0.0 collective-permute-start.12
  61.2 2.4 %collective-permute-start.13 = (bf16[2,8,64,128]{3,2,1,0:T(8,128)(2,1)S(1)}, bf16[2,8,64,128]{3,2,1,0:T(8,128)(2,1)S(1)}, u32[]{:S(2)}, u32[]{:S(2)}) collective-permute-start(bf16[2,8,64,128]{3,2,1,0:T(8,128)(2,1)S(1)} %get-tuple-element.32), channel_id=1, source_target_pairs={{0,12},{2,14},{1,13},{3,15},{4,8},{6,10},{5,9},{7,11},{8,4},{10,6}... | collective-permute-start | bytes 786440 | tf_op jit(solution)/shard_map/ppermute | solution.py:444
  63.6 3.6 %collective-permute-start.10 = (bf16[8,64,128]{2,1,0:T(8,128)(2,1)S(1)}, bf16[8,64,128]{2,1,0:T(8,128)(2,1)S(1)}, u32[]{:S(2)}, u32[]{:S(2)}) collective-permute-start(bf16[8,64,128]{2,1,0:T(8,128)(2,1)S(1)} %slice_bitcast_fusion.3), channel_id=1, source_target_pairs={{0,15},{2,13},{1,14},{3,12},{4,11},{6,9},{5,10},{7,8},{8,7},{10,5}... | collective-permute-start | bytes 393224 | tf_op jit(solution)/shard_map/ppermute | solution.py:447
  67.2 4.4 %all-to-all-start.2 = ((bf16[8,256,128]{2,1,0:T(8,128)(2,1)}), bf16[8,256,128]{2,1,0:T(8,128)(2,1)S(1)}, u32[]{:S(2)}, u32[]{:S(2)}) async-start(bf16[8,256,128]{2,1,0:T(8,128)(2,1)} %get-tuple-element.25), calls=%async_computation.2 | async-start | bytes 1048576 | tf_op jit(solution)/shard_map/all_to_all | solution.py:71
  71.6 0.0 collective-permute-done.11
  71.7 0.5 collective-permute-done.12
  72.2 3.8 %collective-permute-done.13 = bf16[2,8,64,128]{3,2,1,0:T(8,128)(2,1)S(1)} collective-permute-done((bf16[2,8,64,128]{3,2,1,0:T(8,128)(2,1)S(1)}, bf16[2,8,64,128]{3,2,1,0:T(8,128)(2,1)S(1)}, u32[]{:S(2)}, u32[]{:S(2)}) %collective-permute-start.13) | collective-permute-done | bytes 262176 | tf_op jit(solution)/shard_map/ppermute | solution.py:444
  76.1 0.0 copy-start.4
  76.1 0.0 collective-permute-done.10
  76.1 0.1 fusion.1
  76.2 3.6 %all-to-all-done.2.back_ref = bf16[8,256,128]{2,1,0:T(8,128)(2,1)S(1)} async-done(((bf16[8,256,128]{2,1,0:T(8,128)(2,1)}), bf16[8,256,128]{2,1,0:T(8,128)(2,1)S(1)}, u32[]{:S(2)}, u32[]{:S(2)}) %all-to-all-start.2) | async-done | bytes 524320 | tf_op jit(solution)/shard_map/all_to_all | solution.py:71
  79.8 0.0 copy-start.1
  79.8 0.0 collective-permute-start.14
  79.8 0.0 copy-done.4
  79.8 0.1 mul.17
  79.9 0.1 mul.18
  80.0 1.4 %collective-permute-done.14 = f32[8,64,128]{2,1,0:T(8,128)S(1)} collective-permute-done((f32[8,64,128]{2,1,0:T(8,128)S(1)}, f32[8,64,128]{2,1,0:T(8,128)S(1)}, u32[]{:S(2)}, u32[]{:S(2)}) %collective-permute-start.14) | collective-permute-done | bytes 262176 | tf_op jit(solution)/shard_map/ppermute | solution.py:67
  81.4 0.7 multiply_convert_fusion
  82.1 3.4 %all-to-all-start.3 = ((bf16[8,64,128]{2,1,0:T(8,128)(2,1)}), bf16[8,64,128]{2,1,0:T(8,128)(2,1)S(1)}, u32[]{:S(2)}, u32[]{:S(2)}) async-start(bf16[8,64,128]{2,1,0:T(8,128)(2,1)} %multiply_convert_fusion), calls=%async_computation.3 | async-start | bytes 262144 | tf_op jit(solution)/shard_map/all_to_all | solution.py:71
  85.5 0.0 copy-done.1
  85.5 1.9 %unpack_q.1 = bf16[32,64,128]{2,1,0:T(8,128)(2,1)} custom-call(bf16[8,256,128]{2,1,0:T(8,128)(2,1)} %copy-done.1), custom_call_target="tpu_custom_call" | custom-call | bytes 6291456 | tf_op jit(solution)/shard_map/unpack_q/pallas_call | solution.py:364
  87.4 4.6 %all-to-all-done.3.back_ref = bf16[8,64,128]{2,1,0:T(8,128)(2,1)S(1)} async-done(((bf16[8,64,128]{2,1,0:T(8,128)(2,1)}), bf16[8,64,128]{2,1,0:T(8,128)(2,1)S(1)}, u32[]{:S(2)}, u32[]{:S(2)}) %all-to-all-start.3) | async-done | bytes 131104 | tf_op jit(solution)/shard_map/all_to_all | solution.py:71
  92.0 0.0 copy-start.2
  92.0 0.7 copy-done.2
  92.6 1.6 %unpack_kv.1 = (bf16[32,8,128]{2,1,0:T(8,128)(2,1)}, bf16[32,8,128]{2,1,0:T(8,128)(2,1)}) custom-call(bf16[8,64,128]{2,1,0:T(8,128)(2,1)} %copy-done.2), custom_call_target="tpu_custom_call" | custom-call | tf_op jit(solution)/shard_map/unpack_kv/pallas_call | solution.py:378
  (6 shorter events, 0.2 us)
Async XLA Ops:
  2.2 11.8 %all-to-all-start = ((bf16[8,64,128]{2,1,0:T(8,128)(2,1)}), bf16[8,64,128]{2,1,0:T(8,128)(2,1)S(1)}, u32[]{:S(2)}, u32[]{:S(2)}) async-start(bf16[8,64,128]{2,1,0:T(8,128)(2,1)} %pack_kv.1), calls=%async_computation | async-start | bytes 262144 | tf_op jit(solution)/shard_map/all_to_all | solution.py:71
  10.4 27.9 %copy-start.3 = (s32[4096]{0:T(1024)S(1)}, s32[4096]{0:T(1024)}, u32[]{:S(2)}) copy-start(s32[4096]{0:T(1024)} %param.13) | copy-start | bytes 49156
  10.4 29.1 %copy-start = (s32[128]{0:T(128)S(1)}, s32[128]{0:T(128)}, u32[]{:S(2)}) copy-start(s32[128]{0:T(128)} %span_ref.1) | copy-start | bytes 1540
  14.0 1.3 %collective-permute-start = (bf16[8,64,128]{2,1,0:T(8,128)(2,1)S(1)}, bf16[8,64,128]{2,1,0:T(8,128)(2,1)S(1)}, u32[]{:S(2)}, u32[]{:S(2)}) collective-permute-start(bf16[8,64,128]{2,1,0:T(8,128)(2,1)S(1)} %all-to-all-done.kv0_ref), channel_id=1, source_target_pairs={{0,16},{1,17},{2,18},{3,19},{4,20},{5,21},{6,22},{7,23},{8,24},{9,... | collective-permute-start | bytes 393224 | tf_op jit(solution)/shard_map/ppermute | solution.py:67
  15.4 24.1 %all-to-all-start.1 = ((bf16[8,528,128]{2,1,0:T(8,128)(2,1)}), bf16[8,528,128]{2,1,0:T(8,128)(2,1)S(1)}, u32[]{:S(2)}, u32[]{:S(2)}) async-start(bf16[8,528,128]{2,1,0:T(8,128)(2,1)} %pack_q.1), calls=%async_computation.1 | async-start | bytes 2162688 | tf_op jit(solution)/shard_map/all_to_all | solution.py:71
  19.0 9.5 %collective-permute-start.1 = (bf16[2,8,64,128]{3,2,1,0:T(8,128)(2,1)S(1)}, bf16[2,8,64,128]{3,2,1,0:T(8,128)(2,1)S(1)}, u32[]{:S(2)}, u32[]{:S(2)}) collective-permute-start(bf16[2,8,64,128]{3,2,1,0:T(8,128)(2,1)S(1)} %pad_maximum_fusion), channel_id=1, source_target_pairs={{0,7},{2,5},{1,6},{3,4},{4,3},{6,1},{5,2},{7,0},{8,15},{10,13},{9,... | collective-permute-start | bytes 786440 | tf_op jit(solution)/shard_map/ppermute | solution.py:436
  22.6 12.5 %collective-permute-start.2 = (bf16[2,8,64,128]{3,2,1,0:T(8,128)(2,1)S(1)}, bf16[2,8,64,128]{3,2,1,0:T(8,128)(2,1)S(1)}, u32[]{:S(2)}, u32[]{:S(2)}) collective-permute-start(bf16[2,8,64,128]{3,2,1,0:T(8,128)(2,1)S(1)} %pad_maximum_fusion), channel_id=1, source_target_pairs={{0,3},{2,1},{1,2},{3,0},{4,7},{6,5},{5,6},{7,4},{8,11},{10,9},{9,1... | collective-permute-start | bytes 786440 | tf_op jit(solution)/shard_map/ppermute | solution.py:436
  23.7 14.1 %collective-permute-start.3 = (bf16[2,8,64,128]{3,2,1,0:T(8,128)(2,1)S(1)}, bf16[2,8,64,128]{3,2,1,0:T(8,128)(2,1)S(1)}, u32[]{:S(2)}, u32[]{:S(2)}) collective-permute-start(bf16[2,8,64,128]{3,2,1,0:T(8,128)(2,1)S(1)} %pad_maximum_fusion), channel_id=1, source_target_pairs={{0,12},{2,14},{1,13},{3,15},{4,8},{6,10},{5,9},{7,11},{8,4},{10,6}... | collective-permute-start | bytes 786440 | tf_op jit(solution)/shard_map/ppermute | solution.py:436
  26.2 11.6 %collective-permute-start.4 = (bf16[8,64,128]{2,1,0:T(8,128)(2,1)S(1)}, bf16[8,64,128]{2,1,0:T(8,128)(2,1)S(1)}, u32[]{:S(2)}, u32[]{:S(2)}) collective-permute-start(bf16[8,64,128]{2,1,0:T(8,128)(2,1)S(1)} %all-to-all-done.kv0_ref), channel_id=1, source_target_pairs={{0,15},{2,13},{1,14},{3,12},{4,11},{6,9},{5,10},{7,8},{8,7},{10,5}... | collective-permute-start | bytes 393224 | tf_op jit(solution)/shard_map/ppermute | solution.py:437
  28.5 10.9 %collective-permute-start.5 = (bf16[2,8,64,128]{3,2,1,0:T(8,128)(2,1)S(1)}, bf16[2,8,64,128]{3,2,1,0:T(8,128)(2,1)S(1)}, u32[]{:S(2)}, u32[]{:S(2)}) collective-permute-start(bf16[2,8,64,128]{3,2,1,0:T(8,128)(2,1)S(1)} %collective-permute-done.1.mine0_ref), channel_id=1, source_target_pairs={{0,16},{1,17},{2,18},{3,19},{4,20},{5,21},{6,22},{7,23},{8,24},{9,... | collective-permute-start | bytes 786440 | tf_op jit(solution)/shard_map/ppermute | solution.py:67
  35.1 4.4 %collective-permute-start.6 = (bf16[2,8,64,128]{3,2,1,0:T(8,128)(2,1)S(1)}, bf16[2,8,64,128]{3,2,1,0:T(8,128)(2,1)S(1)}, u32[]{:S(2)}, u32[]{:S(2)}) collective-permute-start(bf16[2,8,64,128]{3,2,1,0:T(8,128)(2,1)S(1)} %collective-permute-done.2.mine1_ref), channel_id=1, source_target_pairs={{0,16},{1,17},{2,18},{3,19},{4,20},{5,21},{6,22},{7,23},{8,24},{9,... | collective-permute-start | bytes 786440 | tf_op jit(solution)/shard_map/ppermute | solution.py:67
  37.7 1.7 %collective-permute-start.7 = (bf16[2,8,64,128]{3,2,1,0:T(8,128)(2,1)S(1)}, bf16[2,8,64,128]{3,2,1,0:T(8,128)(2,1)S(1)}, u32[]{:S(2)}, u32[]{:S(2)}) collective-permute-start(bf16[2,8,64,128]{3,2,1,0:T(8,128)(2,1)S(1)} %collective-permute-done.3.mine2_ref), channel_id=1, source_target_pairs={{0,16},{1,17},{2,18},{3,19},{4,20},{5,21},{6,22},{7,23},{8,24},{9,... | collective-permute-start | bytes 786440 | tf_op jit(solution)/shard_map/ppermute | solution.py:67
  37.7 1.7 %collective-permute-start.8 = (bf16[8,64,128]{2,1,0:T(8,128)(2,1)S(1)}, bf16[8,64,128]{2,1,0:T(8,128)(2,1)S(1)}, u32[]{:S(2)}, u32[]{:S(2)}) collective-permute-start(bf16[8,64,128]{2,1,0:T(8,128)(2,1)S(1)} %collective-permute-done.4.mine3_ref), channel_id=1, source_target_pairs={{0,16},{1,17},{2,18},{3,19},{4,20},{5,21},{6,22},{7,23},{8,24},{9,... | collective-permute-start | bytes 393224 | tf_op jit(solution)/shard_map/ppermute | solution.py:67
  46.5 10.0 %collective-permute-start.9 = (bf16[8,8,64,128]{3,2,1,0:T(8,128)(2,1)S(1)}, bf16[8,8,64,128]{3,2,1,0:T(8,128)(2,1)S(1)}, u32[]{:S(2)}, u32[]{:S(2)}) collective-permute-start(bf16[8,8,64,128]{3,2,1,0:T(8,128)(2,1)S(1)} %get-tuple-element.22), channel_id=1, source_target_pairs={{0,16},{1,17},{2,18},{3,19},{4,20},{5,21},{6,22},{7,23},{8,24},{9,... | collective-permute-start | bytes 3145736 | tf_op jit(solution)/shard_map/ppermute | solution.py:67
  57.0 14.7 %collective-permute-start.11 = (bf16[2,8,64,128]{3,2,1,0:T(8,128)(2,1)S(1)}, bf16[2,8,64,128]{3,2,1,0:T(8,128)(2,1)S(1)}, u32[]{:S(2)}, u32[]{:S(2)}) collective-permute-start(bf16[2,8,64,128]{3,2,1,0:T(8,128)(2,1)S(1)} %get-tuple-element.31), channel_id=1, source_target_pairs={{0,7},{2,5},{1,6},{3,4},{4,3},{6,1},{5,2},{7,0},{8,15},{10,13},{9,... | collective-permute-start | bytes 786440 | tf_op jit(solution)/shard_map/ppermute | solution.py:444
  61.2 11.0 %collective-permute-start.12 = (bf16[2,8,64,128]{3,2,1,0:T(8,128)(2,1)S(1)}, bf16[2,8,64,128]{3,2,1,0:T(8,128)(2,1)S(1)}, u32[]{:S(2)}, u32[]{:S(2)}) collective-permute-start(bf16[2,8,64,128]{3,2,1,0:T(8,128)(2,1)S(1)} %get-tuple-element.33), channel_id=1, source_target_pairs={{0,3},{2,1},{1,2},{3,0},{4,7},{6,5},{5,6},{7,4},{8,11},{10,9},{9,1... | collective-permute-start | bytes 786440 | tf_op jit(solution)/shard_map/ppermute | solution.py:444
  61.2 14.8 %collective-permute-start.13 = (bf16[2,8,64,128]{3,2,1,0:T(8,128)(2,1)S(1)}, bf16[2,8,64,128]{3,2,1,0:T(8,128)(2,1)S(1)}, u32[]{:S(2)}, u32[]{:S(2)}) collective-permute-start(bf16[2,8,64,128]{3,2,1,0:T(8,128)(2,1)S(1)} %get-tuple-element.32), channel_id=1, source_target_pairs={{0,12},{2,14},{1,13},{3,15},{4,8},{6,10},{5,9},{7,11},{8,4},{10,6}... | collective-permute-start | bytes 786440 | tf_op jit(solution)/shard_map/ppermute | solution.py:444
  63.6 12.5 %collective-permute-start.10 = (bf16[8,64,128]{2,1,0:T(8,128)(2,1)S(1)}, bf16[8,64,128]{2,1,0:T(8,128)(2,1)S(1)}, u32[]{:S(2)}, u32[]{:S(2)}) collective-permute-start(bf16[8,64,128]{2,1,0:T(8,128)(2,1)S(1)} %slice_bitcast_fusion.3), channel_id=1, source_target_pairs={{0,15},{2,13},{1,14},{3,12},{4,11},{6,9},{5,10},{7,8},{8,7},{10,5}... | collective-permute-start | bytes 393224 | tf_op jit(solution)/shard_map/ppermute | solution.py:447
  67.2 12.6 %all-to-all-start.2 = ((bf16[8,256,128]{2,1,0:T(8,128)(2,1)}), bf16[8,256,128]{2,1,0:T(8,128)(2,1)S(1)}, u32[]{:S(2)}, u32[]{:S(2)}) async-start(bf16[8,256,128]{2,1,0:T(8,128)(2,1)} %get-tuple-element.25), calls=%async_computation.2 | async-start | bytes 1048576 | tf_op jit(solution)/shard_map/all_to_all | solution.py:71
  76.1 3.8 %copy-start.4 = (f32[2]{0:T(128)S(1)}, f32[2]{0:T(128)}, u32[]{:S(2)}) copy-start(f32[2]{0:T(128)} %constant.39.clone) | copy-start | bytes 28
  79.8 5.7 %copy-start.1 = (bf16[8,256,128]{2,1,0:T(8,128)(2,1)}, bf16[8,256,128]{2,1,0:T(8,128)(2,1)S(1)}, u32[]{:S(2)}) copy-start(bf16[8,256,128]{2,1,0:T(8,128)(2,1)S(1)} %all-to-all-done.2.back_ref) | copy-start | bytes 1572868
  79.8 1.5 %collective-permute-start.14 = (f32[8,64,128]{2,1,0:T(8,128)S(1)}, f32[8,64,128]{2,1,0:T(8,128)S(1)}, u32[]{:S(2)}, u32[]{:S(2)}) collective-permute-start(f32[8,64,128]{2,1,0:T(8,128)S(1)} %fusion), channel_id=1, source_target_pairs={{0,16},{1,17},{2,18},{3,19},{4,20},{5,21},{6,22},{7,23},{8,24},{9,... | collective-permute-start | bytes 786440 | tf_op jit(solution)/shard_map/ppermute | solution.py:67
  82.1 9.9 %all-to-all-start.3 = ((bf16[8,64,128]{2,1,0:T(8,128)(2,1)}), bf16[8,64,128]{2,1,0:T(8,128)(2,1)S(1)}, u32[]{:S(2)}, u32[]{:S(2)}) async-start(bf16[8,64,128]{2,1,0:T(8,128)(2,1)} %multiply_convert_fusion), calls=%async_computation.3 | async-start | bytes 262144 | tf_op jit(solution)/shard_map/all_to_all | solution.py:71
  92.0 0.7 copy-start.2

commit v6 on v5

--- a/solution.py
+++ b/solution.py
@@ -255,8 +255,9 @@
         for (slot, i, at), s in zip(units, scores):
             s = (s * factor).reshape(TK // 8, 8, ROWS)
             upper = hi_s[i] - at
-            lower = lo_s[i] - at
-            s = jnp.where((step <= upper[None]) & (step >= lower[None]), s, LOW)
+            span = (hi_s[i] - lo_s[i]).astype(jnp.uint32)
+            back = (upper[None] - step).astype(jnp.uint32)
+            s = jnp.where(back <= span[None], s, LOW)
             top = jnp.max(s, axis=0)
             e = jnp.exp2(s - top[None])
             s_s[slot] = e.reshape(TK, ROWS)
@@ -314,7 +315,7 @@
         slots = [(who, e) for e in flips for who in (me, 1 - me)] + [(me, LAST), (me, 0)]
         for slot, (who, e) in enumerate(slots):
             for i, at in enumerate(chunk_places(span_ref, who, mine ^ e)):
-                ref[slot, i, 0:TOK, :] = dk_s[pl.ds(at, TOK), :].astype(BF16)
+                ref[slot, i, 0:TOK, :] = (dk_s[pl.ds(at, TOK), :] * scale).astype(BF16)
                 ref[slot, i, TOK:PART, :] = dv_s[pl.ds(at, TOK), :].astype(BF16)
 
 
@@ -426,7 +427,9 @@
     starts = jnp.sum(
         segment_ids[None, :] < jnp.arange(8, dtype=jnp.int32)[:, None], axis=1, dtype=jnp.int32
     )
-    kv = exchange(pack_kv(keys, values))
+    kv = exchange(
+        jnp.concatenate([keys.transpose(1, 0, 2), values.transpose(1, 0, 2)], axis=1)
+    )
     message = pack_q(queries, out_grads, out_states)
     kv, message = lax.optimization_barrier((kv, message))
     kv_theirs = to_core(kv)
@@ -438,7 +441,6 @@
     parts = [kv, kv_theirs] + got + [to_core(part) for part in got]
     dq, mine, other = attention(span_position, starts, me, message, parts)
     part = (mine.astype(F32) + to_core(other).astype(F32)).astype(BF16)
-    part, dq = lax.optimization_barrier((part, dq))
     dq = exchange(dq)
     got = [
         lax.ppermute(part[2 * n : 2 * n + 2], AXES, seq_pairs(flips)).astype(F32)
@@ -448,10 +450,12 @@
     total = part[7].astype(F32) + last.astype(F32) + got[0][0] + got[1][0] + got[2][0]
     give = got[0][1] + got[1][1] + got[2][1]
     total, give, dq = lax.optimization_barrier((total, give, dq))
-    factor = jnp.array([1.0 / math.sqrt(128), 1.0], F32).reshape(1, 2, 1, 1)
-    total = ((total + to_core(give)).reshape(8, 2, TOK, 128) * factor).astype(BF16)
-    back = exchange(total.reshape(8, PART, 128))
-    return (unpack_q(dq),) + tuple(unpack_kv(back))
+    back = exchange((total + to_core(give)).astype(BF16))
+    return (
+        unpack_q(dq),
+        back[:, :TOK].transpose(1, 0, 2),
+        back[:, TOK:].transpose(1, 0, 2),
+    )
 
 
 def solution(mesh):

time: 94.4 us -> 91.4 us (0.968); the launches traced: 94.3 us -> 90.2 us
  starting transfers between devices: 47.1 us -> 42.8 us
  waiting for transfers between devices: 29 us -> 27.3 us
  local copies, waits for them, and re-layouts: 0.91 us -> 2.32 us
    ppermute x7, starting transfers between devices: 10.6 us -> 4.88 us  [to_core(): return lax.ppermute(array, AXES, core_pairs())]
    ppermute x1, waiting for transfers between devices: 0.01 us -> 4.86 us  [shards(): last = lax.ppermute(part[6], AXES, seq_pairs((LAST, LAST)))]
    ppermute x3, waiting for transfers between devices: 4.27 us -> 0.14 us  [shards(): lax.ppermute(part[2 * n:2 * n + 2], AXES, seq_pairs(flips)).astype(F32)]
    pallas_call x2 -> x0, Pallas kernels: 3.2 us -> none  [the longest x1 1.62 us: unpack_kv(): pl.pallas_call(unpack_kv_kernel, out_shape=(small, small), in_specs=[vmem...]
    pallas_call x1, Pallas kernels: 6.99 us -> 10.1 us  [attention(): pl.pallas_call(attn_kernel, out_shape=(jax.ShapeDtypeStruct((8, ROWS, 128...]
    all_to_all x4, waiting for transfers between devices: 11.8 us -> 8.73 us  [exchange(): lax.all_to_all(array, AXES, split_axis=0, concat_axis=0, axis_index_group...]
    ppermute x1, waiting for transfers between devices: 0.01 us -> 1.8 us  [shards(): got.append(lax.ppermute(kv, AXES, seq_pairs((LAST, LAST))))]
    ppermute x3, waiting for transfers between devices: 6.9 us -> 5.89 us  [shards(): got = [lax.ppermute(both, AXES, seq_pairs(flips)) for flips in zip(*SHARE)]]
  transfers between devices with their start and end apart: 19 -> 19, of which waited for: 11 -> 13; matrix products, arithmetic and copies ran while one was open for 1% -> 1% of each run, Pallas kernels for 5% -> 5%
where the time goes in v6:
time: 91.4 us; the launch traced here: 90.2 us
  starting transfers between devices  42.8 us (47%)
  waiting for transfers between devices  27.3 us (30%)
  Pallas kernels  14.7 us (16%)
  local copies, waits for them, and re-layouts  2.32 us (3%)
  other arithmetic  2.24 us (2%)
    all_to_all x4, starting transfers between devices, exchange(): lax.all_to_all(array, AXES, split_axis=0, concat_axis=0, axis_index_group...  17.6 us
    pallas_call x1, Pallas kernels, attention(): pl.pallas_call(attn_kernel, out_shape=(jax.ShapeDtypeStruct((8, ROWS, 128...  10.1 us
    all_to_all x4, waiting for transfers between devices, exchange(): lax.all_to_all(array, AXES, split_axis=0, concat_axis=0, axis_index_group...  8.73 us
    ppermute x3, starting transfers between devices, shards(): lax.ppermute(part[2 * n:2 * n + 2], AXES, seq_pairs(flips)).astype(F32)  7.07 us
    ppermute x3, starting transfers between devices, shards(): got = [lax.ppermute(both, AXES, seq_pairs(flips)) for flips in zip(*SHARE)]  6.59 us
    ppermute x7, waiting for transfers between devices, to_core(): return lax.ppermute(array, AXES, core_pairs())  5.92 us
    ppermute x3, waiting for transfers between devices, shards(): got = [lax.ppermute(both, AXES, seq_pairs(flips)) for flips in zip(*SHARE)]  5.89 us
    ppermute x7, starting transfers between devices, to_core(): return lax.ppermute(array, AXES, core_pairs())  4.88 us
  transfers between devices with their start and end apart: 19, of which 13 were waited for; matrix products, arithmetic and copies ran while one was open for 1% of the time, Pallas kernels for 5%

profile of v6, /device:TPU:0, one launch (start us, length us, event | category | flops | bytes accessed | tf_op | source)
XLA Modules:
  0.0 90.2 jit_solution(5223159829330668680)
XLA Ops:
  0.6 0.9 copy_bitcast_fusion
  1.5 0.7 pad_maximum_fusion.1
  2.2 5.4 %all-to-all-start = ((bf16[8,64,128]{2,1,0:T(8,128)(2,1)}), bf16[8,64,128]{2,1,0:T(8,128)(2,1)S(1)}, u32[]{:S(2)}, u32[]{:S(2)}) async-start(bf16[8,64,128]{2,1,0:T(8,128)(2,1)} %pad_maximum_fusion.1), calls=%async_computation | async-start | bytes 262144 | tf_op jit(solution)/shard_map/all_to_all | solution.py:71
  7.6 2.8 %pack_q.1 = bf16[8,528,128]{2,1,0:T(8,128)(2,1)} custom-call(bf16[32,64,128]{2,1,0:T(8,128)(2,1)} %q_hbm.1, bf16[32,64,128]{2,1,0:T(8,128)(2,1)} %g_hbm.1, bf16[32,64,128]{2,1,0:T(8,128)(2,1)} %o_hbm.1), custom_call_target="tpu_custom_call" | custom-call | bytes 8388608 | tf_op jit(solution)/shard_map/pack_q/pallas_call | solution.py:352
  10.4 0.0 copy-start.2
  10.4 0.0 copy-start
  10.4 3.6 %all-to-all-done.kv0_ref = bf16[8,64,128]{2,1,0:T(8,128)(2,1)S(1)} async-done(((bf16[8,64,128]{2,1,0:T(8,128)(2,1)}), bf16[8,64,128]{2,1,0:T(8,128)(2,1)S(1)}, u32[]{:S(2)}, u32[]{:S(2)}) %all-to-all-start) | async-done | bytes 131104 | tf_op jit(solution)/shard_map/all_to_all | solution.py:71
  14.0 0.0 collective-permute-start
  14.0 1.3 %collective-permute-done.kv1_ref = bf16[8,64,128]{2,1,0:T(8,128)(2,1)S(1)} collective-permute-done((bf16[8,64,128]{2,1,0:T(8,128)(2,1)S(1)}, bf16[8,64,128]{2,1,0:T(8,128)(2,1)S(1)}, u32[]{:S(2)}, u32[]{:S(2)}) %collective-permute-start) | collective-permute-done | bytes 131104 | tf_op jit(solution)/shard_map/ppermute | solution.py:67
  15.3 3.6 %all-to-all-start.1 = ((bf16[8,528,128]{2,1,0:T(8,128)(2,1)}), bf16[8,528,128]{2,1,0:T(8,128)(2,1)S(1)}, u32[]{:S(2)}, u32[]{:S(2)}) async-start(bf16[8,528,128]{2,1,0:T(8,128)(2,1)} %pack_q.1), calls=%async_computation.1 | async-start | bytes 2162688 | tf_op jit(solution)/shard_map/all_to_all | solution.py:71
  18.9 4.1 %collective-permute-start.3 = (bf16[2,8,64,128]{3,2,1,0:T(8,128)(2,1)S(1)}, bf16[2,8,64,128]{3,2,1,0:T(8,128)(2,1)S(1)}, u32[]{:S(2)}, u32[]{:S(2)}) collective-permute-start(bf16[2,8,64,128]{3,2,1,0:T(8,128)(2,1)S(1)} %pad_maximum_fusion), channel_id=1, source_target_pairs={{0,12},{2,14},{1,13},{3,15},{4,8},{6,10},{5,9},{7,11},{8,4},{10,6}... | collective-permute-start | bytes 786440 | tf_op jit(solution)/shard_map/ppermute | solution.py:439
  23.1 2.2 %collective-permute-start.2 = (bf16[2,8,64,128]{3,2,1,0:T(8,128)(2,1)S(1)}, bf16[2,8,64,128]{3,2,1,0:T(8,128)(2,1)S(1)}, u32[]{:S(2)}, u32[]{:S(2)}) collective-permute-start(bf16[2,8,64,128]{3,2,1,0:T(8,128)(2,1)S(1)} %pad_maximum_fusion), channel_id=1, source_target_pairs={{0,3},{2,1},{1,2},{3,0},{4,7},{6,5},{5,6},{7,4},{8,11},{10,9},{9,1... | collective-permute-start | bytes 786440 | tf_op jit(solution)/shard_map/ppermute | solution.py:439
  25.2 0.3 collective-permute-start.1
  25.5 2.3 %collective-permute-start.4 = (bf16[8,64,128]{2,1,0:T(8,128)(2,1)S(1)}, bf16[8,64,128]{2,1,0:T(8,128)(2,1)S(1)}, u32[]{:S(2)}, u32[]{:S(2)}) collective-permute-start(bf16[8,64,128]{2,1,0:T(8,128)(2,1)S(1)} %all-to-all-done.kv0_ref), channel_id=1, source_target_pairs={{0,15},{2,13},{1,14},{3,12},{4,11},{6,9},{5,10},{7,8},{8,7},{10,5}... | collective-permute-start | bytes 393224 | tf_op jit(solution)/shard_map/ppermute | solution.py:440
  27.9 4.3 %collective-permute-done.3.mine2_ref = bf16[2,8,64,128]{3,2,1,0:T(8,128)(2,1)S(1)} collective-permute-done((bf16[2,8,64,128]{3,2,1,0:T(8,128)(2,1)S(1)}, bf16[2,8,64,128]{3,2,1,0:T(8,128)(2,1)S(1)}, u32[]{:S(2)}, u32[]{:S(2)}) %collective-permute-start.3) | collective-permute-done | bytes 262176 | tf_op jit(solution)/shard_map/ppermute | solution.py:439
  32.2 0.0 collective-permute-start.7
  32.2 1.2 %collective-permute-done.2.mine1_ref = bf16[2,8,64,128]{3,2,1,0:T(8,128)(2,1)S(1)} collective-permute-done((bf16[2,8,64,128]{3,2,1,0:T(8,128)(2,1)S(1)}, bf16[2,8,64,128]{3,2,1,0:T(8,128)(2,1)S(1)}, u32[]{:S(2)}, u32[]{:S(2)}) %collective-permute-start.2) | collective-permute-done | bytes 262176 | tf_op jit(solution)/shard_map/ppermute | solution.py:439
  33.5 3.1 %collective-permute-start.6 = (bf16[2,8,64,128]{3,2,1,0:T(8,128)(2,1)S(1)}, bf16[2,8,64,128]{3,2,1,0:T(8,128)(2,1)S(1)}, u32[]{:S(2)}, u32[]{:S(2)}) collective-permute-start(bf16[2,8,64,128]{3,2,1,0:T(8,128)(2,1)S(1)} %collective-permute-done.2.mine1_ref), channel_id=1, source_target_pairs={{0,16},{1,17},{2,18},{3,19},{4,20},{5,21},{6,22},{7,23},{8,24},{9,... | collective-permute-start | bytes 786440 | tf_op jit(solution)/shard_map/ppermute | solution.py:67
  36.6 0.3 collective-permute-done.1.mine0_ref
  36.9 0.0 collective-permute-start.5
  36.9 1.8 %collective-permute-done.4.mine3_ref = bf16[8,64,128]{2,1,0:T(8,128)(2,1)S(1)} collective-permute-done((bf16[8,64,128]{2,1,0:T(8,128)(2,1)S(1)}, bf16[8,64,128]{2,1,0:T(8,128)(2,1)S(1)}, u32[]{:S(2)}, u32[]{:S(2)}) %collective-permute-start.4) | collective-permute-done | bytes 131104 | tf_op jit(solution)/shard_map/ppermute | solution.py:440
  38.7 0.0 collective-permute-start.8
  38.7 0.1 pad_add_fusion.me_ref
  38.8 0.0 copy-done.2
  38.8 0.1 convert_reduce_fusion.start_ref
  38.9 1.1 %collective-permute-done.8.theirs3_ref = bf16[8,64,128]{2,1,0:T(8,128)(2,1)S(1)} collective-permute-done((bf16[8,64,128]{2,1,0:T(8,128)(2,1)S(1)}, bf16[8,64,128]{2,1,0:T(8,128)(2,1)S(1)}, u32[]{:S(2)}, u32[]{:S(2)}) %collective-permute-start.8) | collective-permute-done | bytes 131104 | tf_op jit(solution)/shard_map/ppermute | solution.py:67
  40.1 0.0 collective-permute-done.7.theirs2_ref
  40.1 0.0 collective-permute-done.6.theirs1_ref
  40.1 0.0 collective-permute-done.5.theirs0_ref
  40.1 0.0 all-to-all-done.1.msg_ref
  40.1 0.0 copy-done
  40.1 10.1 %attention.1 = (bf16[8,256,128]{2,1,0:T(8,128)(2,1)}, bf16[8,8,64,128]{3,2,1,0:T(8,128)(2,1)S(1)}, bf16[8,8,64,128]{3,2,1,0:T(8,128)(2,1)S(1)}) custom-call(s32[128]{0:T(128)S(1)} %copy-done, s32[8]{0:T(128)S(1)} %convert_reduce_fusion.start_ref, s32[2]{0:T(128)S(1)} %pad_add_fusion.me_ref, bf16[8,528,128]{2,1,0:T(8,128)(2,1)S(1)} %all-to-all-done.1.msg_ref, ...), custom_call_target="tpu_custom_call" | custom-call | tf_op jit(solution)/shard_map/attention/pallas_call | solution.py:393
  50.2 1.2 %collective-permute-start.9 = (bf16[8,8,64,128]{3,2,1,0:T(8,128)(2,1)S(1)}, bf16[8,8,64,128]{3,2,1,0:T(8,128)(2,1)S(1)}, u32[]{:S(2)}, u32[]{:S(2)}) collective-permute-start(bf16[8,8,64,128]{3,2,1,0:T(8,128)(2,1)S(1)} %get-tuple-element.18), channel_id=1, source_target_pairs={{0,16},{1,17},{2,18},{3,19},{4,20},{5,21},{6,22},{7,23},{8,24},{9,... | collective-permute-start | bytes 3145736 | tf_op jit(solution)/shard_map/ppermute | solution.py:67
  51.4 2.3 %collective-permute-done.9 = bf16[8,8,64,128]{3,2,1,0:T(8,128)(2,1)S(1)} collective-permute-done((bf16[8,8,64,128]{3,2,1,0:T(8,128)(2,1)S(1)}, bf16[8,8,64,128]{3,2,1,0:T(8,128)(2,1)S(1)}, u32[]{:S(2)}, u32[]{:S(2)}) %collective-permute-start.9) | collective-permute-done | bytes 1048608 | tf_op jit(solution)/shard_map/ppermute | solution.py:67
  53.7 0.4 add_convert_fusion
  54.1 0.1 fusion.4
  54.2 5.4 %collective-permute-start.11 = (bf16[2,8,64,128]{3,2,1,0:T(8,128)(2,1)S(1)}, bf16[2,8,64,128]{3,2,1,0:T(8,128)(2,1)S(1)}, u32[]{:S(2)}, u32[]{:S(2)}) collective-permute-start(bf16[2,8,64,128]{3,2,1,0:T(8,128)(2,1)S(1)} %get-tuple-element.29), channel_id=1, source_target_pairs={{0,7},{2,5},{1,6},{3,4},{4,3},{6,1},{5,2},{7,0},{8,15},{10,13},{9,... | collective-permute-start | bytes 786440 | tf_op jit(solution)/shard_map/ppermute | solution.py:446
  59.6 1.6 %collective-permute-start.13 = (bf16[2,8,64,128]{3,2,1,0:T(8,128)(2,1)S(1)}, bf16[2,8,64,128]{3,2,1,0:T(8,128)(2,1)S(1)}, u32[]{:S(2)}, u32[]{:S(2)}) collective-permute-start(bf16[2,8,64,128]{3,2,1,0:T(8,128)(2,1)S(1)} %get-tuple-element.30), channel_id=1, source_target_pairs={{0,12},{2,14},{1,13},{3,15},{4,8},{6,10},{5,9},{7,11},{8,4},{10,6}... | collective-permute-start | bytes 786440 | tf_op jit(solution)/shard_map/ppermute | solution.py:446
  61.2 0.0 collective-permute-start.12
  61.3 4.5 %all-to-all-start.2 = ((bf16[8,256,128]{2,1,0:T(8,128)(2,1)}), bf16[8,256,128]{2,1,0:T(8,128)(2,1)S(1)}, u32[]{:S(2)}, u32[]{:S(2)}) async-start(bf16[8,256,128]{2,1,0:T(8,128)(2,1)} %get-tuple-element.19), calls=%async_computation.2 | async-start | bytes 1048576 | tf_op jit(solution)/shard_map/all_to_all | solution.py:71
  65.7 4.3 %collective-permute-start.10 = (bf16[8,64,128]{2,1,0:T(8,128)(2,1)S(1)}, bf16[8,64,128]{2,1,0:T(8,128)(2,1)S(1)}, u32[]{:S(2)}, u32[]{:S(2)}) collective-permute-start(bf16[8,64,128]{2,1,0:T(8,128)(2,1)S(1)} %slice_bitcast_fusion.3), channel_id=1, source_target_pairs={{0,15},{2,13},{1,14},{3,12},{4,11},{6,9},{5,10},{7,8},{8,7},{10,5}... | collective-permute-start | bytes 393224 | tf_op jit(solution)/shard_map/ppermute | solution.py:449
  70.1 0.0 collective-permute-done.11
  70.1 0.0 collective-permute-done.13
  70.2 0.1 collective-permute-done.12
  70.4 4.9 %collective-permute-done.10 = bf16[8,64,128]{2,1,0:T(8,128)(2,1)S(1)} collective-permute-done((bf16[8,64,128]{2,1,0:T(8,128)(2,1)S(1)}, bf16[8,64,128]{2,1,0:T(8,128)(2,1)S(1)}, u32[]{:S(2)}, u32[]{:S(2)}) %collective-permute-start.10) | collective-permute-done | bytes 131104 | tf_op jit(solution)/shard_map/ppermute | solution.py:449
  75.3 0.1 fusion.1
  75.3 0.6 all-to-all-done.2.back_ref
  75.9 0.0 copy-start.1
  75.9 0.5 collective-permute-start.14
  76.4 1.2 %collective-permute-done.14 = f32[8,64,128]{2,1,0:T(8,128)S(1)} collective-permute-done((f32[8,64,128]{2,1,0:T(8,128)S(1)}, f32[8,64,128]{2,1,0:T(8,128)S(1)}, u32[]{:S(2)}, u32[]{:S(2)}) %collective-permute-start.14) | collective-permute-done | bytes 262176 | tf_op jit(solution)/shard_map/ppermute | solution.py:67
  77.6 0.7 add_convert_fusion.1
  78.3 4.2 %all-to-all-start.3 = ((bf16[8,64,128]{2,1,0:T(8,128)(2,1)}), bf16[8,64,128]{2,1,0:T(8,128)(2,1)S(1)}, u32[]{:S(2)}, u32[]{:S(2)}) async-start(bf16[8,64,128]{2,1,0:T(8,128)(2,1)} %add_convert_fusion.1), calls=%async_computation.3 | async-start | bytes 262144 | tf_op jit(solution)/shard_map/all_to_all | solution.py:71
  82.5 0.0 copy-done.1
  82.5 1.9 %unpack_q.1 = bf16[32,64,128]{2,1,0:T(8,128)(2,1)} custom-call(bf16[8,256,128]{2,1,0:T(8,128)(2,1)} %copy-done.1), custom_call_target="tpu_custom_call" | custom-call | bytes 6291456 | tf_op jit(solution)/shard_map/unpack_q/pallas_call | solution.py:365
  84.3 4.5 %all-to-all-done.3 = bf16[8,64,128]{2,1,0:T(8,128)(2,1)S(1)} async-done(((bf16[8,64,128]{2,1,0:T(8,128)(2,1)}), bf16[8,64,128]{2,1,0:T(8,128)(2,1)S(1)}, u32[]{:S(2)}, u32[]{:S(2)}) %all-to-all-start.3) | async-done | bytes 131104 | tf_op jit(solution)/shard_map/all_to_all | solution.py:71
  88.9 0.7 copy.17
  89.5 0.7 copy.16
  (7 shorter events, 0.2 us)
Async XLA Ops:
  2.2 11.8 %all-to-all-start = ((bf16[8,64,128]{2,1,0:T(8,128)(2,1)}), bf16[8,64,128]{2,1,0:T(8,128)(2,1)S(1)}, u32[]{:S(2)}, u32[]{:S(2)}) async-start(bf16[8,64,128]{2,1,0:T(8,128)(2,1)} %pad_maximum_fusion.1), calls=%async_computation | async-start | bytes 262144 | tf_op jit(solution)/shard_map/all_to_all | solution.py:71
  10.4 28.4 %copy-start.2 = (s32[4096]{0:T(1024)S(1)}, s32[4096]{0:T(1024)}, u32[]{:S(2)}) copy-start(s32[4096]{0:T(1024)} %param.12) | copy-start | bytes 49156
  10.4 29.7 %copy-start = (s32[128]{0:T(128)S(1)}, s32[128]{0:T(128)}, u32[]{:S(2)}) copy-start(s32[128]{0:T(128)} %span_ref.1) | copy-start | bytes 1540
  14.0 1.3 %collective-permute-start = (bf16[8,64,128]{2,1,0:T(8,128)(2,1)S(1)}, bf16[8,64,128]{2,1,0:T(8,128)(2,1)S(1)}, u32[]{:S(2)}, u32[]{:S(2)}) collective-permute-start(bf16[8,64,128]{2,1,0:T(8,128)(2,1)S(1)} %all-to-all-done.kv0_ref), channel_id=1, source_target_pairs={{0,16},{1,17},{2,18},{3,19},{4,20},{5,21},{6,22},{7,23},{8,24},{9,... | collective-permute-start | bytes 393224 | tf_op jit(solution)/shard_map/ppermute | solution.py:67
  15.3 24.7 %all-to-all-start.1 = ((bf16[8,528,128]{2,1,0:T(8,128)(2,1)}), bf16[8,528,128]{2,1,0:T(8,128)(2,1)S(1)}, u32[]{:S(2)}, u32[]{:S(2)}) async-start(bf16[8,528,128]{2,1,0:T(8,128)(2,1)} %pack_q.1), calls=%async_computation.1 | async-start | bytes 2162688 | tf_op jit(solution)/shard_map/all_to_all | solution.py:71
  18.9 13.3 %collective-permute-start.3 = (bf16[2,8,64,128]{3,2,1,0:T(8,128)(2,1)S(1)}, bf16[2,8,64,128]{3,2,1,0:T(8,128)(2,1)S(1)}, u32[]{:S(2)}, u32[]{:S(2)}) collective-permute-start(bf16[2,8,64,128]{3,2,1,0:T(8,128)(2,1)S(1)} %pad_maximum_fusion), channel_id=1, source_target_pairs={{0,12},{2,14},{1,13},{3,15},{4,8},{6,10},{5,9},{7,11},{8,4},{10,6}... | collective-permute-start | bytes 786440 | tf_op jit(solution)/shard_map/ppermute | solution.py:439
  23.1 10.4 %collective-permute-start.2 = (bf16[2,8,64,128]{3,2,1,0:T(8,128)(2,1)S(1)}, bf16[2,8,64,128]{3,2,1,0:T(8,128)(2,1)S(1)}, u32[]{:S(2)}, u32[]{:S(2)}) collective-permute-start(bf16[2,8,64,128]{3,2,1,0:T(8,128)(2,1)S(1)} %pad_maximum_fusion), channel_id=1, source_target_pairs={{0,3},{2,1},{1,2},{3,0},{4,7},{6,5},{5,6},{7,4},{8,11},{10,9},{9,1... | collective-permute-start | bytes 786440 | tf_op jit(solution)/shard_map/ppermute | solution.py:439
  25.2 11.7 %collective-permute-start.1 = (bf16[2,8,64,128]{3,2,1,0:T(8,128)(2,1)S(1)}, bf16[2,8,64,128]{3,2,1,0:T(8,128)(2,1)S(1)}, u32[]{:S(2)}, u32[]{:S(2)}) collective-permute-start(bf16[2,8,64,128]{3,2,1,0:T(8,128)(2,1)S(1)} %pad_maximum_fusion), channel_id=1, source_target_pairs={{0,7},{2,5},{1,6},{3,4},{4,3},{6,1},{5,2},{7,0},{8,15},{10,13},{9,... | collective-permute-start | bytes 786440 | tf_op jit(solution)/shard_map/ppermute | solution.py:439
  25.5 13.2 %collective-permute-start.4 = (bf16[8,64,128]{2,1,0:T(8,128)(2,1)S(1)}, bf16[8,64,128]{2,1,0:T(8,128)(2,1)S(1)}, u32[]{:S(2)}, u32[]{:S(2)}) collective-permute-start(bf16[8,64,128]{2,1,0:T(8,128)(2,1)S(1)} %all-to-all-done.kv0_ref), channel_id=1, source_target_pairs={{0,15},{2,13},{1,14},{3,12},{4,11},{6,9},{5,10},{7,8},{8,7},{10,5}... | collective-permute-start | bytes 393224 | tf_op jit(solution)/shard_map/ppermute | solution.py:440
  32.2 7.9 %collective-permute-start.7 = (bf16[2,8,64,128]{3,2,1,0:T(8,128)(2,1)S(1)}, bf16[2,8,64,128]{3,2,1,0:T(8,128)(2,1)S(1)}, u32[]{:S(2)}, u32[]{:S(2)}) collective-permute-start(bf16[2,8,64,128]{3,2,1,0:T(8,128)(2,1)S(1)} %collective-permute-done.3.mine2_ref), channel_id=1, source_target_pairs={{0,16},{1,17},{2,18},{3,19},{4,20},{5,21},{6,22},{7,23},{8,24},{9,... | collective-permute-start | bytes 786440 | tf_op jit(solution)/shard_map/ppermute | solution.py:67
  33.5 6.6 %collective-permute-start.6 = (bf16[2,8,64,128]{3,2,1,0:T(8,128)(2,1)S(1)}, bf16[2,8,64,128]{3,2,1,0:T(8,128)(2,1)S(1)}, u32[]{:S(2)}, u32[]{:S(2)}) collective-permute-start(bf16[2,8,64,128]{3,2,1,0:T(8,128)(2,1)S(1)} %collective-permute-done.2.mine1_ref), channel_id=1, source_target_pairs={{0,16},{1,17},{2,18},{3,19},{4,20},{5,21},{6,22},{7,23},{8,24},{9,... | collective-permute-start | bytes 786440 | tf_op jit(solution)/shard_map/ppermute | solution.py:67
  36.9 3.2 %collective-permute-start.5 = (bf16[2,8,64,128]{3,2,1,0:T(8,128)(2,1)S(1)}, bf16[2,8,64,128]{3,2,1,0:T(8,128)(2,1)S(1)}, u32[]{:S(2)}, u32[]{:S(2)}) collective-permute-start(bf16[2,8,64,128]{3,2,1,0:T(8,128)(2,1)S(1)} %collective-permute-done.1.mine0_ref), channel_id=1, source_target_pairs={{0,16},{1,17},{2,18},{3,19},{4,20},{5,21},{6,22},{7,23},{8,24},{9,... | collective-permute-start | bytes 786440 | tf_op jit(solution)/shard_map/ppermute | solution.py:67
  38.7 1.3 %collective-permute-start.8 = (bf16[8,64,128]{2,1,0:T(8,128)(2,1)S(1)}, bf16[8,64,128]{2,1,0:T(8,128)(2,1)S(1)}, u32[]{:S(2)}, u32[]{:S(2)}) collective-permute-start(bf16[8,64,128]{2,1,0:T(8,128)(2,1)S(1)} %collective-permute-done.4.mine3_ref), channel_id=1, source_target_pairs={{0,16},{1,17},{2,18},{3,19},{4,20},{5,21},{6,22},{7,23},{8,24},{9,... | collective-permute-start | bytes 393224 | tf_op jit(solution)/shard_map/ppermute | solution.py:67
  50.2 3.5 %collective-permute-start.9 = (bf16[8,8,64,128]{3,2,1,0:T(8,128)(2,1)S(1)}, bf16[8,8,64,128]{3,2,1,0:T(8,128)(2,1)S(1)}, u32[]{:S(2)}, u32[]{:S(2)}) collective-permute-start(bf16[8,8,64,128]{3,2,1,0:T(8,128)(2,1)S(1)} %get-tuple-element.18), channel_id=1, source_target_pairs={{0,16},{1,17},{2,18},{3,19},{4,20},{5,21},{6,22},{7,23},{8,24},{9,... | collective-permute-start | bytes 3145736 | tf_op jit(solution)/shard_map/ppermute | solution.py:67
  54.2 15.9 %collective-permute-start.11 = (bf16[2,8,64,128]{3,2,1,0:T(8,128)(2,1)S(1)}, bf16[2,8,64,128]{3,2,1,0:T(8,128)(2,1)S(1)}, u32[]{:S(2)}, u32[]{:S(2)}) collective-permute-start(bf16[2,8,64,128]{3,2,1,0:T(8,128)(2,1)S(1)} %get-tuple-element.29), channel_id=1, source_target_pairs={{0,7},{2,5},{1,6},{3,4},{4,3},{6,1},{5,2},{7,0},{8,15},{10,13},{9,... | collective-permute-start | bytes 786440 | tf_op jit(solution)/shard_map/ppermute | solution.py:446
  59.6 10.5 %collective-permute-start.13 = (bf16[2,8,64,128]{3,2,1,0:T(8,128)(2,1)S(1)}, bf16[2,8,64,128]{3,2,1,0:T(8,128)(2,1)S(1)}, u32[]{:S(2)}, u32[]{:S(2)}) collective-permute-start(bf16[2,8,64,128]{3,2,1,0:T(8,128)(2,1)S(1)} %get-tuple-element.30), channel_id=1, source_target_pairs={{0,12},{2,14},{1,13},{3,15},{4,8},{6,10},{5,9},{7,11},{8,4},{10,6}... | collective-permute-start | bytes 786440 | tf_op jit(solution)/shard_map/ppermute | solution.py:446
  61.2 9.1 %collective-permute-start.12 = (bf16[2,8,64,128]{3,2,1,0:T(8,128)(2,1)S(1)}, bf16[2,8,64,128]{3,2,1,0:T(8,128)(2,1)S(1)}, u32[]{:S(2)}, u32[]{:S(2)}) collective-permute-start(bf16[2,8,64,128]{3,2,1,0:T(8,128)(2,1)S(1)} %get-tuple-element.31), channel_id=1, source_target_pairs={{0,3},{2,1},{1,2},{3,0},{4,7},{6,5},{5,6},{7,4},{8,11},{10,9},{9,1... | collective-permute-start | bytes 786440 | tf_op jit(solution)/shard_map/ppermute | solution.py:446
  61.3 14.7 %all-to-all-start.2 = ((bf16[8,256,128]{2,1,0:T(8,128)(2,1)}), bf16[8,256,128]{2,1,0:T(8,128)(2,1)S(1)}, u32[]{:S(2)}, u32[]{:S(2)}) async-start(bf16[8,256,128]{2,1,0:T(8,128)(2,1)} %get-tuple-element.19), calls=%async_computation.2 | async-start | bytes 1048576 | tf_op jit(solution)/shard_map/all_to_all | solution.py:71
  65.7 9.5 %collective-permute-start.10 = (bf16[8,64,128]{2,1,0:T(8,128)(2,1)S(1)}, bf16[8,64,128]{2,1,0:T(8,128)(2,1)S(1)}, u32[]{:S(2)}, u32[]{:S(2)}) collective-permute-start(bf16[8,64,128]{2,1,0:T(8,128)(2,1)S(1)} %slice_bitcast_fusion.3), channel_id=1, source_target_pairs={{0,15},{2,13},{1,14},{3,12},{4,11},{6,9},{5,10},{7,8},{8,7},{10,5}... | collective-permute-start | bytes 393224 | tf_op jit(solution)/shard_map/ppermute | solution.py:449
  75.9 6.5 %copy-start.1 = (bf16[8,256,128]{2,1,0:T(8,128)(2,1)}, bf16[8,256,128]{2,1,0:T(8,128)(2,1)S(1)}, u32[]{:S(2)}) copy-start(bf16[8,256,128]{2,1,0:T(8,128)(2,1)S(1)} %all-to-all-done.2.back_ref) | copy-start | bytes 1572868
  75.9 1.7 %collective-permute-start.14 = (f32[8,64,128]{2,1,0:T(8,128)S(1)}, f32[8,64,128]{2,1,0:T(8,128)S(1)}, u32[]{:S(2)}, u32[]{:S(2)}) collective-permute-start(f32[8,64,128]{2,1,0:T(8,128)S(1)} %fusion), channel_id=1, source_target_pairs={{0,16},{1,17},{2,18},{3,19},{4,20},{5,21},{6,22},{7,23},{8,24},{9,... | collective-permute-start | bytes 786440 | tf_op jit(solution)/shard_map/ppermute | solution.py:67
  78.3 10.6 %all-to-all-start.3 = ((bf16[8,64,128]{2,1,0:T(8,128)(2,1)}), bf16[8,64,128]{2,1,0:T(8,128)(2,1)S(1)}, u32[]{:S(2)}, u32[]{:S(2)}) async-start(bf16[8,64,128]{2,1,0:T(8,128)(2,1)} %add_convert_fusion.1), calls=%async_computation.3 | async-start | bytes 262144 | tf_op jit(solution)/shard_map/all_to_all | solution.py:71

commit v7 on v6

--- a/solution.py
+++ b/solution.py
@@ -17,7 +17,7 @@
 DEL0 = 2 * ROWS
 MSG = DEL0 + 16
 PART = 2 * TOK
-SHARE = ((3, 1, 6), (5, 4, 2))
+SHARE = ((2, 6, 1), (5, 3, 4))
 LAST = 7
 TK = 256
 LENGTH = 4096

time: 91.4 us -> 88.6 us (0.969)
  starting transfers between devices: 42.8 us -> 38.1 us
  Pallas kernels: 14.7 us -> 16.9 us
    ppermute x3, starting transfers between devices: 7.07 us -> 3.53 us  [shards(): lax.ppermute(part[2 * n:2 * n + 2], AXES, seq_pairs(flips)).astype(F32)]
    ppermute x3, waiting for transfers between devices: 0.14 us -> 3.21 us  [shards(): lax.ppermute(part[2 * n:2 * n + 2], AXES, seq_pairs(flips)).astype(F32)]
    pallas_call x1, Pallas kernels: 10.1 us -> 12.2 us  [attention(): pl.pallas_call(attn_kernel, out_shape=(jax.ShapeDtypeStruct((8, ROWS, 128...]
    ppermute x1, waiting for transfers between devices: 1.8 us -> 0.01 us  [shards(): got.append(lax.ppermute(kv, AXES, seq_pairs((LAST, LAST))))]
    ppermute x7, starting transfers between devices: 4.88 us -> 6.64 us  [to_core(): return lax.ppermute(array, AXES, core_pairs())]
    ppermute x1, starting transfers between devices: 4.31 us -> 2.55 us  [shards(): last = lax.ppermute(part[6], AXES, seq_pairs((LAST, LAST)))]
    ppermute x1, waiting for transfers between devices: 4.86 us -> 3.42 us  [shards(): last = lax.ppermute(part[6], AXES, seq_pairs((LAST, LAST)))]
    ppermute x1, starting transfers between devices: 2.33 us -> 1 us  [shards(): got.append(lax.ppermute(kv, AXES, seq_pairs((LAST, LAST))))]
  transfers between devices with their start and end apart: 19 -> 19, of which waited for: 13 -> 12; matrix products, arithmetic and copies ran while one was open for 1% -> 1% of each run, Pallas kernels for 5% -> 5%
where the time goes in v7:
time: 88.6 us; the launch traced here: 87.7 us
  starting transfers between devices  38.1 us (43%)
  waiting for transfers between devices  27.4 us (31%)
  Pallas kernels  16.9 us (19%)
  local copies, waits for them, and re-layouts  2.32 us (3%)
  other arithmetic  2.24 us (3%)
    all_to_all x4, starting transfers between devices, exchange(): lax.all_to_all(array, AXES, split_axis=0, concat_axis=0, axis_index_group...  18 us
    pallas_call x1, Pallas kernels, attention(): pl.pallas_call(attn_kernel, out_shape=(jax.ShapeDtypeStruct((8, ROWS, 128...  12.2 us
    all_to_all x4, waiting for transfers between devices, exchange(): lax.all_to_all(array, AXES, split_axis=0, concat_axis=0, axis_index_group...  9.16 us
    ppermute x7, starting transfers between devices, to_core(): return lax.ppermute(array, AXES, core_pairs())  6.64 us
    ppermute x3, starting transfers between devices, shards(): got = [lax.ppermute(both, AXES, seq_pairs(flips)) for flips in zip(*SHARE)]  6.3 us
    ppermute x7, waiting for transfers between devices, to_core(): return lax.ppermute(array, AXES, core_pairs())  6.1 us
    ppermute x3, waiting for transfers between devices, shards(): got = [lax.ppermute(both, AXES, seq_pairs(flips)) for flips in zip(*SHARE)]  5.48 us
    ppermute x3, starting transfers between devices, shards(): lax.ppermute(part[2 * n:2 * n + 2], AXES, seq_pairs(flips)).astype(F32)  3.53 us
  transfers between devices with their start and end apart: 19, of which 12 were waited for; matrix products, arithmetic and copies ran while one was open for 1% of the time, Pallas kernels for 5%

profile of v7, /device:TPU:0, one launch (start us, length us, event | category | flops | bytes accessed | tf_op | source)
XLA Modules:
  0.0 87.7 jit_solution(29758679603565392)
XLA Ops:
  0.6 0.9 %copy_bitcast_fusion = (bf16[8,32,128]{2,1,0:T(8,128)(2,1)S(1)}, bf16[8,32,128]{2,1,0:T(8,128)(2,1)S(1)}) fusion(bf16[32,8,128]{2,1,0:T(8,128)(2,1)} %param.9, bf16[32,8,128]{2,1,0:T(8,128)(2,1)} %param.8), kind=kLoop, calls=%fused_computation.20 | loop fusion | bytes 262144 | tf_op jit(solution)/shard_map/transpose | solution.py:431
  1.5 0.7 pad_maximum_fusion.1
  2.2 5.4 %all-to-all-start = ((bf16[8,64,128]{2,1,0:T(8,128)(2,1)}), bf16[8,64,128]{2,1,0:T(8,128)(2,1)S(1)}, u32[]{:S(2)}, u32[]{:S(2)}) async-start(bf16[8,64,128]{2,1,0:T(8,128)(2,1)} %pad_maximum_fusion.1), calls=%async_computation | async-start | bytes 262144 | tf_op jit(solution)/shard_map/all_to_all | solution.py:71
  7.6 2.8 %pack_q.1 = bf16[8,528,128]{2,1,0:T(8,128)(2,1)} custom-call(bf16[32,64,128]{2,1,0:T(8,128)(2,1)} %q_hbm.1, bf16[32,64,128]{2,1,0:T(8,128)(2,1)} %g_hbm.1, bf16[32,64,128]{2,1,0:T(8,128)(2,1)} %o_hbm.1), custom_call_target="tpu_custom_call" | custom-call | bytes 8388608 | tf_op jit(solution)/shard_map/pack_q/pallas_call | solution.py:352
  10.4 0.0 copy-start.2
  10.4 0.0 copy-start
  10.4 3.6 %all-to-all-done.kv0_ref = bf16[8,64,128]{2,1,0:T(8,128)(2,1)S(1)} async-done(((bf16[8,64,128]{2,1,0:T(8,128)(2,1)}), bf16[8,64,128]{2,1,0:T(8,128)(2,1)S(1)}, u32[]{:S(2)}, u32[]{:S(2)}) %all-to-all-start) | async-done | bytes 131104 | tf_op jit(solution)/shard_map/all_to_all | solution.py:71
  14.0 0.0 collective-permute-start
  14.0 1.3 %collective-permute-done.kv1_ref = bf16[8,64,128]{2,1,0:T(8,128)(2,1)S(1)} collective-permute-done((bf16[8,64,128]{2,1,0:T(8,128)(2,1)S(1)}, bf16[8,64,128]{2,1,0:T(8,128)(2,1)S(1)}, u32[]{:S(2)}, u32[]{:S(2)}) %collective-permute-start) | collective-permute-done | bytes 131104 | tf_op jit(solution)/shard_map/ppermute | solution.py:67
  15.3 3.6 %all-to-all-start.1 = ((bf16[8,528,128]{2,1,0:T(8,128)(2,1)}), bf16[8,528,128]{2,1,0:T(8,128)(2,1)S(1)}, u32[]{:S(2)}, u32[]{:S(2)}) async-start(bf16[8,528,128]{2,1,0:T(8,128)(2,1)} %pack_q.1), calls=%async_computation.1 | async-start | bytes 2162688 | tf_op jit(solution)/shard_map/all_to_all | solution.py:71
  18.9 2.3 %collective-permute-start.3 = (bf16[2,8,64,128]{3,2,1,0:T(8,128)(2,1)S(1)}, bf16[2,8,64,128]{3,2,1,0:T(8,128)(2,1)S(1)}, u32[]{:S(2)}, u32[]{:S(2)}) collective-permute-start(bf16[2,8,64,128]{3,2,1,0:T(8,128)(2,1)S(1)} %pad_maximum_fusion), channel_id=1, source_target_pairs={{0,3},{2,1},{1,2},{3,0},{4,7},{6,5},{5,6},{7,4},{8,11},{10,9},{9,1... | collective-permute-start | bytes 786440 | tf_op jit(solution)/shard_map/ppermute | solution.py:439
  21.2 4.0 %collective-permute-start.2 = (bf16[2,8,64,128]{3,2,1,0:T(8,128)(2,1)S(1)}, bf16[2,8,64,128]{3,2,1,0:T(8,128)(2,1)S(1)}, u32[]{:S(2)}, u32[]{:S(2)}) collective-permute-start(bf16[2,8,64,128]{3,2,1,0:T(8,128)(2,1)S(1)} %pad_maximum_fusion), channel_id=1, source_target_pairs={{0,12},{2,14},{1,13},{3,15},{4,8},{6,10},{5,9},{7,11},{8,4},{10,6}... | collective-permute-start | bytes 786440 | tf_op jit(solution)/shard_map/ppermute | solution.py:439
  25.2 0.0 collective-permute-start.1
  25.2 1.0 %collective-permute-start.4 = (bf16[8,64,128]{2,1,0:T(8,128)(2,1)S(1)}, bf16[8,64,128]{2,1,0:T(8,128)(2,1)S(1)}, u32[]{:S(2)}, u32[]{:S(2)}) collective-permute-start(bf16[8,64,128]{2,1,0:T(8,128)(2,1)S(1)} %all-to-all-done.kv0_ref), channel_id=1, source_target_pairs={{0,15},{2,13},{1,14},{3,12},{4,11},{6,9},{5,10},{7,8},{8,7},{10,5}... | collective-permute-start | bytes 393224 | tf_op jit(solution)/shard_map/ppermute | solution.py:440
  26.2 0.4 collective-permute-done.3.mine2_ref
  26.6 3.8 %collective-permute-start.7 = (bf16[2,8,64,128]{3,2,1,0:T(8,128)(2,1)S(1)}, bf16[2,8,64,128]{3,2,1,0:T(8,128)(2,1)S(1)}, u32[]{:S(2)}, u32[]{:S(2)}) collective-permute-start(bf16[2,8,64,128]{3,2,1,0:T(8,128)(2,1)S(1)} %collective-permute-done.3.mine2_ref), channel_id=1, source_target_pairs={{0,16},{1,17},{2,18},{3,19},{4,20},{5,21},{6,22},{7,23},{8,24},{9,... | collective-permute-start | bytes 786440 | tf_op jit(solution)/shard_map/ppermute | solution.py:67
  30.4 0.0 collective-permute-done.2.mine1_ref
  30.4 0.9 %collective-permute-start.6 = (bf16[2,8,64,128]{3,2,1,0:T(8,128)(2,1)S(1)}, bf16[2,8,64,128]{3,2,1,0:T(8,128)(2,1)S(1)}, u32[]{:S(2)}, u32[]{:S(2)}) collective-permute-start(bf16[2,8,64,128]{3,2,1,0:T(8,128)(2,1)S(1)} %collective-permute-done.2.mine1_ref), channel_id=1, source_target_pairs={{0,16},{1,17},{2,18},{3,19},{4,20},{5,21},{6,22},{7,23},{8,24},{9,... | collective-permute-start | bytes 786440 | tf_op jit(solution)/shard_map/ppermute | solution.py:67
  31.3 5.1 %collective-permute-done.1.mine0_ref = bf16[2,8,64,128]{3,2,1,0:T(8,128)(2,1)S(1)} collective-permute-done((bf16[2,8,64,128]{3,2,1,0:T(8,128)(2,1)S(1)}, bf16[2,8,64,128]{3,2,1,0:T(8,128)(2,1)S(1)}, u32[]{:S(2)}, u32[]{:S(2)}) %collective-permute-start.1) | collective-permute-done | bytes 262176 | tf_op jit(solution)/shard_map/ppermute | solution.py:439
  36.4 1.1 %collective-permute-start.5 = (bf16[2,8,64,128]{3,2,1,0:T(8,128)(2,1)S(1)}, bf16[2,8,64,128]{3,2,1,0:T(8,128)(2,1)S(1)}, u32[]{:S(2)}, u32[]{:S(2)}) collective-permute-start(bf16[2,8,64,128]{3,2,1,0:T(8,128)(2,1)S(1)} %collective-permute-done.1.mine0_ref), channel_id=1, source_target_pairs={{0,16},{1,17},{2,18},{3,19},{4,20},{5,21},{6,22},{7,23},{8,24},{9,... | collective-permute-start | bytes 786440 | tf_op jit(solution)/shard_map/ppermute | solution.py:67
  37.5 0.0 collective-permute-done.4.mine3_ref
  37.5 0.7 collective-permute-start.8
  38.2 0.1 pad_add_fusion.me_ref
  38.2 0.0 copy-done.2
  38.2 0.1 convert_reduce_fusion.start_ref
  38.4 0.8 collective-permute-done.8.theirs3_ref
  39.2 0.0 collective-permute-done.7.theirs2_ref
  39.2 0.0 collective-permute-done.6.theirs1_ref
  39.2 0.0 collective-permute-done.5.theirs0_ref
  39.2 0.0 all-to-all-done.1.msg_ref
  39.2 0.0 copy-done
  39.2 12.2 %attention.1 = (bf16[8,256,128]{2,1,0:T(8,128)(2,1)}, bf16[8,8,64,128]{3,2,1,0:T(8,128)(2,1)S(1)}, bf16[8,8,64,128]{3,2,1,0:T(8,128)(2,1)S(1)}) custom-call(s32[128]{0:T(128)S(1)} %copy-done, s32[8]{0:T(128)S(1)} %convert_reduce_fusion.start_ref, s32[2]{0:T(128)S(1)} %pad_add_fusion.me_ref, bf16[8,528,128]{2,1,0:T(8,128)(2,1)S(1)} %all-to-all-done.1.msg_ref, ...), custom_call_target="tpu_custom_call" | custom-call | tf_op jit(solution)/shard_map/attention/pallas_call | solution.py:393
  51.4 0.0 collective-permute-start.9
  51.4 2.7 %collective-permute-done.9 = bf16[8,8,64,128]{3,2,1,0:T(8,128)(2,1)S(1)} collective-permute-done((bf16[8,8,64,128]{3,2,1,0:T(8,128)(2,1)S(1)}, bf16[8,8,64,128]{3,2,1,0:T(8,128)(2,1)S(1)}, u32[]{:S(2)}, u32[]{:S(2)}) %collective-permute-start.9) | collective-permute-done | bytes 1048608 | tf_op jit(solution)/shard_map/ppermute | solution.py:67
  54.1 0.4 add_convert_fusion
  54.5 0.1 fusion.4
  54.6 0.1 collective-permute-start.11
  54.7 3.4 %collective-permute-start.13 = (bf16[2,8,64,128]{3,2,1,0:T(8,128)(2,1)S(1)}, bf16[2,8,64,128]{3,2,1,0:T(8,128)(2,1)S(1)}, u32[]{:S(2)}, u32[]{:S(2)}) collective-permute-start(bf16[2,8,64,128]{3,2,1,0:T(8,128)(2,1)S(1)} %get-tuple-element.30), channel_id=1, source_target_pairs={{0,3},{2,1},{1,2},{3,0},{4,7},{6,5},{5,6},{7,4},{8,11},{10,9},{9,1... | collective-permute-start | bytes 786440 | tf_op jit(solution)/shard_map/ppermute | solution.py:446
  58.1 0.0 collective-permute-start.12
  58.1 4.8 %all-to-all-start.2 = ((bf16[8,256,128]{2,1,0:T(8,128)(2,1)}), bf16[8,256,128]{2,1,0:T(8,128)(2,1)S(1)}, u32[]{:S(2)}, u32[]{:S(2)}) async-start(bf16[8,256,128]{2,1,0:T(8,128)(2,1)} %get-tuple-element.19), calls=%async_computation.2 | async-start | bytes 1048576 | tf_op jit(solution)/shard_map/all_to_all | solution.py:71
  62.9 2.6 %collective-permute-start.10 = (bf16[8,64,128]{2,1,0:T(8,128)(2,1)S(1)}, bf16[8,64,128]{2,1,0:T(8,128)(2,1)S(1)}, u32[]{:S(2)}, u32[]{:S(2)}) collective-permute-start(bf16[8,64,128]{2,1,0:T(8,128)(2,1)S(1)} %slice_bitcast_fusion.3), channel_id=1, source_target_pairs={{0,15},{2,13},{1,14},{3,12},{4,11},{6,9},{5,10},{7,8},{8,7},{10,5}... | collective-permute-start | bytes 393224 | tf_op jit(solution)/shard_map/ppermute | solution.py:449
  65.5 3.0 %collective-permute-done.11 = bf16[2,8,64,128]{3,2,1,0:T(8,128)(2,1)S(1)} collective-permute-done((bf16[2,8,64,128]{3,2,1,0:T(8,128)(2,1)S(1)}, bf16[2,8,64,128]{3,2,1,0:T(8,128)(2,1)S(1)}, u32[]{:S(2)}, u32[]{:S(2)}) %collective-permute-start.11) | collective-permute-done | bytes 262176 | tf_op jit(solution)/shard_map/ppermute | solution.py:446
  68.5 0.0 collective-permute-done.13
  68.5 0.3 collective-permute-done.12
  68.9 3.4 %collective-permute-done.10 = bf16[8,64,128]{2,1,0:T(8,128)(2,1)S(1)} collective-permute-done((bf16[8,64,128]{2,1,0:T(8,128)(2,1)S(1)}, bf16[8,64,128]{2,1,0:T(8,128)(2,1)S(1)}, u32[]{:S(2)}, u32[]{:S(2)}) %collective-permute-start.10) | collective-permute-done | bytes 131104 | tf_op jit(solution)/shard_map/ppermute | solution.py:449
  72.3 0.1 fusion.1
  72.4 1.0 %all-to-all-done.2.back_ref = bf16[8,256,128]{2,1,0:T(8,128)(2,1)S(1)} async-done(((bf16[8,256,128]{2,1,0:T(8,128)(2,1)}), bf16[8,256,128]{2,1,0:T(8,128)(2,1)S(1)}, u32[]{:S(2)}, u32[]{:S(2)}) %all-to-all-start.2) | async-done | bytes 524320 | tf_op jit(solution)/shard_map/all_to_all | solution.py:71
  73.4 0.0 copy-start.1
  73.4 0.2 collective-permute-start.14
  73.6 1.3 %collective-permute-done.14 = f32[8,64,128]{2,1,0:T(8,128)S(1)} collective-permute-done((f32[8,64,128]{2,1,0:T(8,128)S(1)}, f32[8,64,128]{2,1,0:T(8,128)S(1)}, u32[]{:S(2)}, u32[]{:S(2)}) %collective-permute-start.14) | collective-permute-done | bytes 262176 | tf_op jit(solution)/shard_map/ppermute | solution.py:67
  74.9 0.7 add_convert_fusion.1
  75.6 4.3 %all-to-all-start.3 = ((bf16[8,64,128]{2,1,0:T(8,128)(2,1)}), bf16[8,64,128]{2,1,0:T(8,128)(2,1)S(1)}, u32[]{:S(2)}, u32[]{:S(2)}) async-start(bf16[8,64,128]{2,1,0:T(8,128)(2,1)} %add_convert_fusion.1), calls=%async_computation.3 | async-start | bytes 262144 | tf_op jit(solution)/shard_map/all_to_all | solution.py:71
  79.9 0.0 copy-done.1
  79.9 1.9 %unpack_q.1 = bf16[32,64,128]{2,1,0:T(8,128)(2,1)} custom-call(bf16[8,256,128]{2,1,0:T(8,128)(2,1)} %copy-done.1), custom_call_target="tpu_custom_call" | custom-call | bytes 6291456 | tf_op jit(solution)/shard_map/unpack_q/pallas_call | solution.py:365
  81.8 4.5 %all-to-all-done.3 = bf16[8,64,128]{2,1,0:T(8,128)(2,1)S(1)} async-done(((bf16[8,64,128]{2,1,0:T(8,128)(2,1)}), bf16[8,64,128]{2,1,0:T(8,128)(2,1)S(1)}, u32[]{:S(2)}, u32[]{:S(2)}) %all-to-all-start.3) | async-done | bytes 131104 | tf_op jit(solution)/shard_map/all_to_all | solution.py:71
  86.3 0.7 copy.17
  87.0 0.7 copy.16
  (7 shorter events, 0.2 us)
Async XLA Ops:
  2.2 11.8 %all-to-all-start = ((bf16[8,64,128]{2,1,0:T(8,128)(2,1)}), bf16[8,64,128]{2,1,0:T(8,128)(2,1)S(1)}, u32[]{:S(2)}, u32[]{:S(2)}) async-start(bf16[8,64,128]{2,1,0:T(8,128)(2,1)} %pad_maximum_fusion.1), calls=%async_computation | async-start | bytes 262144 | tf_op jit(solution)/shard_map/all_to_all | solution.py:71
  10.4 27.9 %copy-start.2 = (s32[4096]{0:T(1024)S(1)}, s32[4096]{0:T(1024)}, u32[]{:S(2)}) copy-start(s32[4096]{0:T(1024)} %param.12) | copy-start | bytes 49156
  10.4 28.8 %copy-start = (s32[128]{0:T(128)S(1)}, s32[128]{0:T(128)}, u32[]{:S(2)}) copy-start(s32[128]{0:T(128)} %span_ref.1) | copy-start | bytes 1540
  14.0 1.3 %collective-permute-start = (bf16[8,64,128]{2,1,0:T(8,128)(2,1)S(1)}, bf16[8,64,128]{2,1,0:T(8,128)(2,1)S(1)}, u32[]{:S(2)}, u32[]{:S(2)}) collective-permute-start(bf16[8,64,128]{2,1,0:T(8,128)(2,1)S(1)} %all-to-all-done.kv0_ref), channel_id=1, source_target_pairs={{0,16},{1,17},{2,18},{3,19},{4,20},{5,21},{6,22},{7,23},{8,24},{9,... | collective-permute-start | bytes 393224 | tf_op jit(solution)/shard_map/ppermute | solution.py:67
  15.3 23.8 %all-to-all-start.1 = ((bf16[8,528,128]{2,1,0:T(8,128)(2,1)}), bf16[8,528,128]{2,1,0:T(8,128)(2,1)S(1)}, u32[]{:S(2)}, u32[]{:S(2)}) async-start(bf16[8,528,128]{2,1,0:T(8,128)(2,1)} %pack_q.1), calls=%async_computation.1 | async-start | bytes 2162688 | tf_op jit(solution)/shard_map/all_to_all | solution.py:71
  18.9 7.7 %collective-permute-start.3 = (bf16[2,8,64,128]{3,2,1,0:T(8,128)(2,1)S(1)}, bf16[2,8,64,128]{3,2,1,0:T(8,128)(2,1)S(1)}, u32[]{:S(2)}, u32[]{:S(2)}) collective-permute-start(bf16[2,8,64,128]{3,2,1,0:T(8,128)(2,1)S(1)} %pad_maximum_fusion), channel_id=1, source_target_pairs={{0,3},{2,1},{1,2},{3,0},{4,7},{6,5},{5,6},{7,4},{8,11},{10,9},{9,1... | collective-permute-start | bytes 786440 | tf_op jit(solution)/shard_map/ppermute | solution.py:439
  21.2 9.2 %collective-permute-start.2 = (bf16[2,8,64,128]{3,2,1,0:T(8,128)(2,1)S(1)}, bf16[2,8,64,128]{3,2,1,0:T(8,128)(2,1)S(1)}, u32[]{:S(2)}, u32[]{:S(2)}) collective-permute-start(bf16[2,8,64,128]{3,2,1,0:T(8,128)(2,1)S(1)} %pad_maximum_fusion), channel_id=1, source_target_pairs={{0,12},{2,14},{1,13},{3,15},{4,8},{6,10},{5,9},{7,11},{8,4},{10,6}... | collective-permute-start | bytes 786440 | tf_op jit(solution)/shard_map/ppermute | solution.py:439
  25.2 11.1 %collective-permute-start.1 = (bf16[2,8,64,128]{3,2,1,0:T(8,128)(2,1)S(1)}, bf16[2,8,64,128]{3,2,1,0:T(8,128)(2,1)S(1)}, u32[]{:S(2)}, u32[]{:S(2)}) collective-permute-start(bf16[2,8,64,128]{3,2,1,0:T(8,128)(2,1)S(1)} %pad_maximum_fusion), channel_id=1, source_target_pairs={{0,4},{2,6},{1,5},{3,7},{4,0},{6,2},{5,1},{7,3},{8,12},{10,14},{9,... | collective-permute-start | bytes 786440 | tf_op jit(solution)/shard_map/ppermute | solution.py:439
  25.2 12.2 %collective-permute-start.4 = (bf16[8,64,128]{2,1,0:T(8,128)(2,1)S(1)}, bf16[8,64,128]{2,1,0:T(8,128)(2,1)S(1)}, u32[]{:S(2)}, u32[]{:S(2)}) collective-permute-start(bf16[8,64,128]{2,1,0:T(8,128)(2,1)S(1)} %all-to-all-done.kv0_ref), channel_id=1, source_target_pairs={{0,15},{2,13},{1,14},{3,12},{4,11},{6,9},{5,10},{7,8},{8,7},{10,5}... | collective-permute-start | bytes 393224 | tf_op jit(solution)/shard_map/ppermute | solution.py:440
  26.6 12.6 %collective-permute-start.7 = (bf16[2,8,64,128]{3,2,1,0:T(8,128)(2,1)S(1)}, bf16[2,8,64,128]{3,2,1,0:T(8,128)(2,1)S(1)}, u32[]{:S(2)}, u32[]{:S(2)}) collective-permute-start(bf16[2,8,64,128]{3,2,1,0:T(8,128)(2,1)S(1)} %collective-permute-done.3.mine2_ref), channel_id=1, source_target_pairs={{0,16},{1,17},{2,18},{3,19},{4,20},{5,21},{6,22},{7,23},{8,24},{9,... | collective-permute-start | bytes 786440 | tf_op jit(solution)/shard_map/ppermute | solution.py:67
  30.4 8.8 %collective-permute-start.6 = (bf16[2,8,64,128]{3,2,1,0:T(8,128)(2,1)S(1)}, bf16[2,8,64,128]{3,2,1,0:T(8,128)(2,1)S(1)}, u32[]{:S(2)}, u32[]{:S(2)}) collective-permute-start(bf16[2,8,64,128]{3,2,1,0:T(8,128)(2,1)S(1)} %collective-permute-done.2.mine1_ref), channel_id=1, source_target_pairs={{0,16},{1,17},{2,18},{3,19},{4,20},{5,21},{6,22},{7,23},{8,24},{9,... | collective-permute-start | bytes 786440 | tf_op jit(solution)/shard_map/ppermute | solution.py:67
  36.4 2.8 %collective-permute-start.5 = (bf16[2,8,64,128]{3,2,1,0:T(8,128)(2,1)S(1)}, bf16[2,8,64,128]{3,2,1,0:T(8,128)(2,1)S(1)}, u32[]{:S(2)}, u32[]{:S(2)}) collective-permute-start(bf16[2,8,64,128]{3,2,1,0:T(8,128)(2,1)S(1)} %collective-permute-done.1.mine0_ref), channel_id=1, source_target_pairs={{0,16},{1,17},{2,18},{3,19},{4,20},{5,21},{6,22},{7,23},{8,24},{9,... | collective-permute-start | bytes 786440 | tf_op jit(solution)/shard_map/ppermute | solution.py:67
  37.5 1.7 %collective-permute-start.8 = (bf16[8,64,128]{2,1,0:T(8,128)(2,1)S(1)}, bf16[8,64,128]{2,1,0:T(8,128)(2,1)S(1)}, u32[]{:S(2)}, u32[]{:S(2)}) collective-permute-start(bf16[8,64,128]{2,1,0:T(8,128)(2,1)S(1)} %collective-permute-done.4.mine3_ref), channel_id=1, source_target_pairs={{0,16},{1,17},{2,18},{3,19},{4,20},{5,21},{6,22},{7,23},{8,24},{9,... | collective-permute-start | bytes 393224 | tf_op jit(solution)/shard_map/ppermute | solution.py:67
  51.4 2.7 %collective-permute-start.9 = (bf16[8,8,64,128]{3,2,1,0:T(8,128)(2,1)S(1)}, bf16[8,8,64,128]{3,2,1,0:T(8,128)(2,1)S(1)}, u32[]{:S(2)}, u32[]{:S(2)}) collective-permute-start(bf16[8,8,64,128]{3,2,1,0:T(8,128)(2,1)S(1)} %get-tuple-element.18), channel_id=1, source_target_pairs={{0,16},{1,17},{2,18},{3,19},{4,20},{5,21},{6,22},{7,23},{8,24},{9,... | collective-permute-start | bytes 3145736 | tf_op jit(solution)/shard_map/ppermute | solution.py:67
  54.6 13.8 %collective-permute-start.11 = (bf16[2,8,64,128]{3,2,1,0:T(8,128)(2,1)S(1)}, bf16[2,8,64,128]{3,2,1,0:T(8,128)(2,1)S(1)}, u32[]{:S(2)}, u32[]{:S(2)}) collective-permute-start(bf16[2,8,64,128]{3,2,1,0:T(8,128)(2,1)S(1)} %get-tuple-element.29), channel_id=1, source_target_pairs={{0,4},{2,6},{1,5},{3,7},{4,0},{6,2},{5,1},{7,3},{8,12},{10,14},{9,... | collective-permute-start | bytes 786440 | tf_op jit(solution)/shard_map/ppermute | solution.py:446
  54.7 13.8 %collective-permute-start.13 = (bf16[2,8,64,128]{3,2,1,0:T(8,128)(2,1)S(1)}, bf16[2,8,64,128]{3,2,1,0:T(8,128)(2,1)S(1)}, u32[]{:S(2)}, u32[]{:S(2)}) collective-permute-start(bf16[2,8,64,128]{3,2,1,0:T(8,128)(2,1)S(1)} %get-tuple-element.30), channel_id=1, source_target_pairs={{0,3},{2,1},{1,2},{3,0},{4,7},{6,5},{5,6},{7,4},{8,11},{10,9},{9,1... | collective-permute-start | bytes 786440 | tf_op jit(solution)/shard_map/ppermute | solution.py:446
  58.1 10.7 %collective-permute-start.12 = (bf16[2,8,64,128]{3,2,1,0:T(8,128)(2,1)S(1)}, bf16[2,8,64,128]{3,2,1,0:T(8,128)(2,1)S(1)}, u32[]{:S(2)}, u32[]{:S(2)}) collective-permute-start(bf16[2,8,64,128]{3,2,1,0:T(8,128)(2,1)S(1)} %get-tuple-element.31), channel_id=1, source_target_pairs={{0,12},{2,14},{1,13},{3,15},{4,8},{6,10},{5,9},{7,11},{8,4},{10,6}... | collective-permute-start | bytes 786440 | tf_op jit(solution)/shard_map/ppermute | solution.py:446
  58.1 15.3 %all-to-all-start.2 = ((bf16[8,256,128]{2,1,0:T(8,128)(2,1)}), bf16[8,256,128]{2,1,0:T(8,128)(2,1)S(1)}, u32[]{:S(2)}, u32[]{:S(2)}) async-start(bf16[8,256,128]{2,1,0:T(8,128)(2,1)} %get-tuple-element.19), calls=%async_computation.2 | async-start | bytes 1048576 | tf_op jit(solution)/shard_map/all_to_all | solution.py:71
  62.9 9.4 %collective-permute-start.10 = (bf16[8,64,128]{2,1,0:T(8,128)(2,1)S(1)}, bf16[8,64,128]{2,1,0:T(8,128)(2,1)S(1)}, u32[]{:S(2)}, u32[]{:S(2)}) collective-permute-start(bf16[8,64,128]{2,1,0:T(8,128)(2,1)S(1)} %slice_bitcast_fusion.3), channel_id=1, source_target_pairs={{0,15},{2,13},{1,14},{3,12},{4,11},{6,9},{5,10},{7,8},{8,7},{10,5}... | collective-permute-start | bytes 393224 | tf_op jit(solution)/shard_map/ppermute | solution.py:449
  73.4 6.5 %copy-start.1 = (bf16[8,256,128]{2,1,0:T(8,128)(2,1)}, bf16[8,256,128]{2,1,0:T(8,128)(2,1)S(1)}, u32[]{:S(2)}) copy-start(bf16[8,256,128]{2,1,0:T(8,128)(2,1)S(1)} %all-to-all-done.2.back_ref) | copy-start | bytes 1572868
  73.4 1.5 %collective-permute-start.14 = (f32[8,64,128]{2,1,0:T(8,128)S(1)}, f32[8,64,128]{2,1,0:T(8,128)S(1)}, u32[]{:S(2)}, u32[]{:S(2)}) collective-permute-start(f32[8,64,128]{2,1,0:T(8,128)S(1)} %fusion), channel_id=1, source_target_pairs={{0,16},{1,17},{2,18},{3,19},{4,20},{5,21},{6,22},{7,23},{8,24},{9,... | collective-permute-start | bytes 786440 | tf_op jit(solution)/shard_map/ppermute | solution.py:67
  75.6 10.7 %all-to-all-start.3 = ((bf16[8,64,128]{2,1,0:T(8,128)(2,1)}), bf16[8,64,128]{2,1,0:T(8,128)(2,1)S(1)}, u32[]{:S(2)}, u32[]{:S(2)}) async-start(bf16[8,64,128]{2,1,0:T(8,128)(2,1)} %add_convert_fusion.1), calls=%async_computation.3 | async-start | bytes 262144 | tf_op jit(solution)/shard_map/all_to_all | solution.py:71

commit v8 on v7

--- a/solution.py
+++ b/solution.py
@@ -17,7 +17,7 @@
 DEL0 = 2 * ROWS
 MSG = DEL0 + 16
 PART = 2 * TOK
-SHARE = ((2, 6, 1), (5, 3, 4))
+SHARE = ((2, 6, 3), (5, 1, 4))
 LAST = 7
 TK = 256
 LENGTH = 4096
@@ -451,10 +451,11 @@
     give = got[0][1] + got[1][1] + got[2][1]
     total, give, dq = lax.optimization_barrier((total, give, dq))
     back = exchange((total + to_core(give)).astype(BF16))
+    key_value = back.reshape(8, 2, TOK, 128).transpose(1, 2, 0, 3)
     return (
         unpack_q(dq),
-        back[:, :TOK].transpose(1, 0, 2),
-        back[:, TOK:].transpose(1, 0, 2),
+        key_value[0],
+        key_value[1],
     )
 
 

time: 88.6 us -> 90.4 us (1.020)
  waiting for transfers between devices: 27.4 us -> 30.9 us
  Pallas kernels: 16.9 us -> 15.8 us
    ppermute x3, starting transfers between devices: 3.53 us -> 6.52 us  [shards(): lax.ppermute(part[2 * n:2 * n + 2], AXES, seq_pairs(flips)).astype(F32)]
    ppermute x7, starting transfers between devices: 6.64 us -> 3.73 us  [to_core(): return lax.ppermute(array, AXES, core_pairs())]
    ppermute x3, waiting for transfers between devices: 5.48 us -> 8.13 us  [shards(): got = [lax.ppermute(both, AXES, seq_pairs(flips)) for flips in zip(*SHARE)]]
    ppermute x1, waiting for transfers between devices: 3.42 us -> 5.5 us  [shards(): last = lax.ppermute(part[6], AXES, seq_pairs((LAST, LAST)))]
    ppermute x3, waiting for transfers between devices: 3.21 us -> 1.35 us  [shards(): lax.ppermute(part[2 * n:2 * n + 2], AXES, seq_pairs(flips)).astype(F32)]
    unnamed x8 -> x6, local copies, waits for them, and re-layouts: 1.33 us -> 0.02 us
    all_to_all x4, starting transfers between devices: 18 us -> 16.8 us  [exchange(): lax.all_to_all(array, AXES, split_axis=0, concat_axis=0, axis_index_group...]
    pallas_call x1, Pallas kernels: 12.2 us -> 11.1 us  [attention(): pl.pallas_call(attn_kernel, out_shape=(jax.ShapeDtypeStruct((8, ROWS, 128...]
  transfers between devices with their start and end apart: 19 -> 19, of which waited for: 12 -> 11; matrix products, arithmetic and copies ran while one was open for 1% -> 1% of each run, Pallas kernels for 5% -> 5%
where the time goes in v8:
time: 90.4 us; the launch traced here: 89.4 us
  starting transfers between devices  37.9 us (42%)
  waiting for transfers between devices  30.9 us (34%)
  Pallas kernels  15.8 us (17%)
  other arithmetic  2.24 us (2%)
  local copies, waits for them, and re-layouts  1.74 us (2%)
    all_to_all x4, starting transfers between devices, exchange(): lax.all_to_all(array, AXES, split_axis=0, concat_axis=0, axis_index_group...  16.8 us
    pallas_call x1, Pallas kernels, attention(): pl.pallas_call(attn_kernel, out_shape=(jax.ShapeDtypeStruct((8, ROWS, 128...  11.1 us
    all_to_all x4, waiting for transfers between devices, exchange(): lax.all_to_all(array, AXES, split_axis=0, concat_axis=0, axis_index_group...  9.47 us
    ppermute x3, waiting for transfers between devices, shards(): got = [lax.ppermute(both, AXES, seq_pairs(flips)) for flips in zip(*SHARE)]  8.13 us
    ppermute x3, starting transfers between devices, shards(): got = [lax.ppermute(both, AXES, seq_pairs(flips)) for flips in zip(*SHARE)]  7.16 us
    ppermute x3, starting transfers between devices, shards(): lax.ppermute(part[2 * n:2 * n + 2], AXES, seq_pairs(flips)).astype(F32)  6.52 us
    ppermute x7, waiting for transfers between devices, to_core(): return lax.ppermute(array, AXES, core_pairs())  6.44 us
    ppermute x1, waiting for transfers between devices, shards(): last = lax.ppermute(part[6], AXES, seq_pairs((LAST, LAST)))  5.5 us
  transfers between devices with their start and end apart: 19, of which 11 were waited for; matrix products, arithmetic and copies ran while one was open for 1% of the time, Pallas kernels for 5%

profile of v8, /device:TPU:0, one launch (start us, length us, event | category | flops | bytes accessed | tf_op | source)
XLA Modules:
  0.0 89.4 jit_solution(13559614600802586570)
XLA Ops:
  0.6 0.9 copy_bitcast_fusion.1
  1.5 0.7 pad_maximum_fusion.1
  2.2 5.4 %all-to-all-start = ((bf16[8,64,128]{2,1,0:T(8,128)(2,1)}), bf16[8,64,128]{2,1,0:T(8,128)(2,1)S(1)}, u32[]{:S(2)}, u32[]{:S(2)}) async-start(bf16[8,64,128]{2,1,0:T(8,128)(2,1)} %pad_maximum_fusion.1), calls=%async_computation | async-start | bytes 262144 | tf_op jit(solution)/shard_map/all_to_all | solution.py:71
  7.6 2.8 %pack_q.1 = bf16[8,528,128]{2,1,0:T(8,128)(2,1)} custom-call(bf16[32,64,128]{2,1,0:T(8,128)(2,1)} %q_hbm.1, bf16[32,64,128]{2,1,0:T(8,128)(2,1)} %g_hbm.1, bf16[32,64,128]{2,1,0:T(8,128)(2,1)} %o_hbm.1), custom_call_target="tpu_custom_call" | custom-call | bytes 8388608 | tf_op jit(solution)/shard_map/pack_q/pallas_call | solution.py:352
  10.4 0.0 copy-start.2
  10.4 0.0 copy-start
  10.4 3.6 %all-to-all-done.kv0_ref = bf16[8,64,128]{2,1,0:T(8,128)(2,1)S(1)} async-done(((bf16[8,64,128]{2,1,0:T(8,128)(2,1)}), bf16[8,64,128]{2,1,0:T(8,128)(2,1)S(1)}, u32[]{:S(2)}, u32[]{:S(2)}) %all-to-all-start) | async-done | bytes 131104 | tf_op jit(solution)/shard_map/all_to_all | solution.py:71
  14.0 0.0 collective-permute-start
  14.0 1.3 %collective-permute-done.kv1_ref = bf16[8,64,128]{2,1,0:T(8,128)(2,1)S(1)} collective-permute-done((bf16[8,64,128]{2,1,0:T(8,128)(2,1)S(1)}, bf16[8,64,128]{2,1,0:T(8,128)(2,1)S(1)}, u32[]{:S(2)}, u32[]{:S(2)}) %collective-permute-start) | collective-permute-done | bytes 131104 | tf_op jit(solution)/shard_map/ppermute | solution.py:67
  15.3 3.6 %all-to-all-start.1 = ((bf16[8,528,128]{2,1,0:T(8,128)(2,1)}), bf16[8,528,128]{2,1,0:T(8,128)(2,1)S(1)}, u32[]{:S(2)}, u32[]{:S(2)}) async-start(bf16[8,528,128]{2,1,0:T(8,128)(2,1)} %pack_q.1), calls=%async_computation.1 | async-start | bytes 2162688 | tf_op jit(solution)/shard_map/all_to_all | solution.py:71
  18.9 3.6 %collective-permute-start.3 = (bf16[2,8,64,128]{3,2,1,0:T(8,128)(2,1)S(1)}, bf16[2,8,64,128]{3,2,1,0:T(8,128)(2,1)S(1)}, u32[]{:S(2)}, u32[]{:S(2)}) collective-permute-start(bf16[2,8,64,128]{3,2,1,0:T(8,128)(2,1)S(1)} %pad_maximum_fusion), channel_id=1, source_target_pairs={{0,7},{2,5},{1,6},{3,4},{4,3},{6,1},{5,2},{7,0},{8,15},{10,13},{9,... | collective-permute-start | bytes 786440 | tf_op jit(solution)/shard_map/ppermute | solution.py:439
  22.6 2.5 %collective-permute-start.2 = (bf16[2,8,64,128]{3,2,1,0:T(8,128)(2,1)S(1)}, bf16[2,8,64,128]{3,2,1,0:T(8,128)(2,1)S(1)}, u32[]{:S(2)}, u32[]{:S(2)}) collective-permute-start(bf16[2,8,64,128]{3,2,1,0:T(8,128)(2,1)S(1)} %pad_maximum_fusion), channel_id=1, source_target_pairs={{0,12},{2,14},{1,13},{3,15},{4,8},{6,10},{5,9},{7,11},{8,4},{10,6}... | collective-permute-start | bytes 786440 | tf_op jit(solution)/shard_map/ppermute | solution.py:439
  25.1 1.0 %collective-permute-start.1 = (bf16[2,8,64,128]{3,2,1,0:T(8,128)(2,1)S(1)}, bf16[2,8,64,128]{3,2,1,0:T(8,128)(2,1)S(1)}, u32[]{:S(2)}, u32[]{:S(2)}) collective-permute-start(bf16[2,8,64,128]{3,2,1,0:T(8,128)(2,1)S(1)} %pad_maximum_fusion), channel_id=1, source_target_pairs={{0,4},{2,6},{1,5},{3,7},{4,0},{6,2},{5,1},{7,3},{8,12},{10,14},{9,... | collective-permute-start | bytes 786440 | tf_op jit(solution)/shard_map/ppermute | solution.py:439
  26.1 1.1 %collective-permute-start.4 = (bf16[8,64,128]{2,1,0:T(8,128)(2,1)S(1)}, bf16[8,64,128]{2,1,0:T(8,128)(2,1)S(1)}, u32[]{:S(2)}, u32[]{:S(2)}) collective-permute-start(bf16[8,64,128]{2,1,0:T(8,128)(2,1)S(1)} %all-to-all-done.kv0_ref), channel_id=1, source_target_pairs={{0,15},{2,13},{1,14},{3,12},{4,11},{6,9},{5,10},{7,8},{8,7},{10,5}... | collective-permute-start | bytes 393224 | tf_op jit(solution)/shard_map/ppermute | solution.py:440
  27.2 0.8 collective-permute-done.3.mine2_ref
  28.0 1.9 %collective-permute-start.7 = (bf16[2,8,64,128]{3,2,1,0:T(8,128)(2,1)S(1)}, bf16[2,8,64,128]{3,2,1,0:T(8,128)(2,1)S(1)}, u32[]{:S(2)}, u32[]{:S(2)}) collective-permute-start(bf16[2,8,64,128]{3,2,1,0:T(8,128)(2,1)S(1)} %collective-permute-done.3.mine2_ref), channel_id=1, source_target_pairs={{0,16},{1,17},{2,18},{3,19},{4,20},{5,21},{6,22},{7,23},{8,24},{9,... | collective-permute-start | bytes 786440 | tf_op jit(solution)/shard_map/ppermute | solution.py:67
  29.9 7.3 %collective-permute-done.2.mine1_ref = bf16[2,8,64,128]{3,2,1,0:T(8,128)(2,1)S(1)} collective-permute-done((bf16[2,8,64,128]{3,2,1,0:T(8,128)(2,1)S(1)}, bf16[2,8,64,128]{3,2,1,0:T(8,128)(2,1)S(1)}, u32[]{:S(2)}, u32[]{:S(2)}) %collective-permute-start.2) | collective-permute-done | bytes 262176 | tf_op jit(solution)/shard_map/ppermute | solution.py:439
  37.2 0.0 collective-permute-start.6
  37.2 0.0 collective-permute-done.1.mine0_ref
  37.2 0.5 collective-permute-start.5
  37.8 0.0 collective-permute-done.4.mine3_ref
  37.8 0.1 collective-permute-start.8
  37.8 0.1 pad_add_fusion.me_ref
  37.9 0.0 copy-done.2
  37.9 0.1 convert_reduce_fusion.start_ref
  38.1 1.3 %collective-permute-done.8.theirs3_ref = bf16[8,64,128]{2,1,0:T(8,128)(2,1)S(1)} collective-permute-done((bf16[8,64,128]{2,1,0:T(8,128)(2,1)S(1)}, bf16[8,64,128]{2,1,0:T(8,128)(2,1)S(1)}, u32[]{:S(2)}, u32[]{:S(2)}) %collective-permute-start.8) | collective-permute-done | bytes 131104 | tf_op jit(solution)/shard_map/ppermute | solution.py:67
  39.3 0.0 collective-permute-done.7.theirs2_ref
  39.3 0.0 collective-permute-done.6.theirs1_ref
  39.3 0.0 collective-permute-done.5.theirs0_ref
  39.3 0.0 all-to-all-done.1.msg_ref
  39.4 0.0 copy-done
  39.4 11.1 %attention.1 = (bf16[8,256,128]{2,1,0:T(8,128)(2,1)}, bf16[8,8,64,128]{3,2,1,0:T(8,128)(2,1)S(1)}, bf16[8,8,64,128]{3,2,1,0:T(8,128)(2,1)S(1)}) custom-call(s32[128]{0:T(128)S(1)} %copy-done, s32[8]{0:T(128)S(1)} %convert_reduce_fusion.start_ref, s32[2]{0:T(128)S(1)} %pad_add_fusion.me_ref, bf16[8,528,128]{2,1,0:T(8,128)(2,1)S(1)} %all-to-all-done.1.msg_ref, ...), custom_call_target="tpu_custom_call" | custom-call | tf_op jit(solution)/shard_map/attention/pallas_call | solution.py:393
  50.5 1.2 %collective-permute-start.9 = (bf16[8,8,64,128]{3,2,1,0:T(8,128)(2,1)S(1)}, bf16[8,8,64,128]{3,2,1,0:T(8,128)(2,1)S(1)}, u32[]{:S(2)}, u32[]{:S(2)}) collective-permute-start(bf16[8,8,64,128]{3,2,1,0:T(8,128)(2,1)S(1)} %get-tuple-element.18), channel_id=1, source_target_pairs={{0,16},{1,17},{2,18},{3,19},{4,20},{5,21},{6,22},{7,23},{8,24},{9,... | collective-permute-start | bytes 3145736 | tf_op jit(solution)/shard_map/ppermute | solution.py:67
  51.7 2.3 %collective-permute-done.9 = bf16[8,8,64,128]{3,2,1,0:T(8,128)(2,1)S(1)} collective-permute-done((bf16[8,8,64,128]{3,2,1,0:T(8,128)(2,1)S(1)}, bf16[8,8,64,128]{3,2,1,0:T(8,128)(2,1)S(1)}, u32[]{:S(2)}, u32[]{:S(2)}) %collective-permute-start.9) | collective-permute-done | bytes 1048608 | tf_op jit(solution)/shard_map/ppermute | solution.py:67
  54.0 0.4 add_convert_fusion
  54.4 0.1 fusion.4
  54.5 0.1 collective-permute-start.11
  54.6 6.4 %collective-permute-start.13 = (bf16[2,8,64,128]{3,2,1,0:T(8,128)(2,1)S(1)}, bf16[2,8,64,128]{3,2,1,0:T(8,128)(2,1)S(1)}, u32[]{:S(2)}, u32[]{:S(2)}) collective-permute-start(bf16[2,8,64,128]{3,2,1,0:T(8,128)(2,1)S(1)} %get-tuple-element.24), channel_id=1, source_target_pairs={{0,7},{2,5},{1,6},{3,4},{4,3},{6,1},{5,2},{7,0},{8,15},{10,13},{9,... | collective-permute-start | bytes 786440 | tf_op jit(solution)/shard_map/ppermute | solution.py:446
  61.0 0.0 collective-permute-start.12
  61.0 4.4 %all-to-all-start.2 = ((bf16[8,256,128]{2,1,0:T(8,128)(2,1)}), bf16[8,256,128]{2,1,0:T(8,128)(2,1)S(1)}, u32[]{:S(2)}, u32[]{:S(2)}) async-start(bf16[8,256,128]{2,1,0:T(8,128)(2,1)} %get-tuple-element.19), calls=%async_computation.2 | async-start | bytes 1048576 | tf_op jit(solution)/shard_map/all_to_all | solution.py:71
  65.5 2.6 %collective-permute-start.10 = (bf16[8,64,128]{2,1,0:T(8,128)(2,1)S(1)}, bf16[8,64,128]{2,1,0:T(8,128)(2,1)S(1)}, u32[]{:S(2)}, u32[]{:S(2)}) collective-permute-start(bf16[8,64,128]{2,1,0:T(8,128)(2,1)S(1)} %slice_bitcast_fusion.3), channel_id=1, source_target_pairs={{0,15},{2,13},{1,14},{3,12},{4,11},{6,9},{5,10},{7,8},{8,7},{10,5}... | collective-permute-start | bytes 393224 | tf_op jit(solution)/shard_map/ppermute | solution.py:449
  68.1 0.0 collective-permute-done.11
  68.2 0.0 collective-permute-done.13
  68.2 1.3 %collective-permute-done.12 = bf16[2,8,64,128]{3,2,1,0:T(8,128)(2,1)S(1)} collective-permute-done((bf16[2,8,64,128]{3,2,1,0:T(8,128)(2,1)S(1)}, bf16[2,8,64,128]{3,2,1,0:T(8,128)(2,1)S(1)}, u32[]{:S(2)}, u32[]{:S(2)}) %collective-permute-start.12) | collective-permute-done | bytes 262176 | tf_op jit(solution)/shard_map/ppermute | solution.py:446
  69.7 5.5 %collective-permute-done.10 = bf16[8,64,128]{2,1,0:T(8,128)(2,1)S(1)} collective-permute-done((bf16[8,64,128]{2,1,0:T(8,128)(2,1)S(1)}, bf16[8,64,128]{2,1,0:T(8,128)(2,1)S(1)}, u32[]{:S(2)}, u32[]{:S(2)}) %collective-permute-start.10) | collective-permute-done | bytes 131104 | tf_op jit(solution)/shard_map/ppermute | solution.py:449
  75.2 0.1 fusion.1
  75.3 1.3 %all-to-all-done.2.back_ref = bf16[8,256,128]{2,1,0:T(8,128)(2,1)S(1)} async-done(((bf16[8,256,128]{2,1,0:T(8,128)(2,1)}), bf16[8,256,128]{2,1,0:T(8,128)(2,1)S(1)}, u32[]{:S(2)}, u32[]{:S(2)}) %all-to-all-start.2) | async-done | bytes 524320 | tf_op jit(solution)/shard_map/all_to_all | solution.py:71
  76.5 0.0 copy-start.1
  76.5 0.0 collective-permute-start.14
  76.5 1.5 %collective-permute-done.14 = f32[8,64,128]{2,1,0:T(8,128)S(1)} collective-permute-done((f32[8,64,128]{2,1,0:T(8,128)S(1)}, f32[8,64,128]{2,1,0:T(8,128)S(1)}, u32[]{:S(2)}, u32[]{:S(2)}) %collective-permute-start.14) | collective-permute-done | bytes 262176 | tf_op jit(solution)/shard_map/ppermute | solution.py:67
  78.1 0.7 add_convert_fusion.1
  78.8 3.4 %all-to-all-start.3 = ((bf16[8,64,128]{2,1,0:T(8,128)(2,1)}), bf16[8,64,128]{2,1,0:T(8,128)(2,1)S(1)}, u32[]{:S(2)}, u32[]{:S(2)}) async-start(bf16[8,64,128]{2,1,0:T(8,128)(2,1)} %add_convert_fusion.1), calls=%async_computation.3 | async-start | bytes 262144 | tf_op jit(solution)/shard_map/all_to_all | solution.py:71
  82.1 0.0 copy-done.1
  82.1 1.9 %unpack_q.1 = bf16[32,64,128]{2,1,0:T(8,128)(2,1)} custom-call(bf16[8,256,128]{2,1,0:T(8,128)(2,1)} %copy-done.1), custom_call_target="tpu_custom_call" | custom-call | bytes 6291456 | tf_op jit(solution)/shard_map/unpack_q/pallas_call | solution.py:365
  84.0 4.6 %all-to-all-done.3 = bf16[8,64,128]{2,1,0:T(8,128)(2,1)S(1)} async-done(((bf16[8,64,128]{2,1,0:T(8,128)(2,1)}), bf16[8,64,128]{2,1,0:T(8,128)(2,1)S(1)}, u32[]{:S(2)}, u32[]{:S(2)}) %all-to-all-start.3) | async-done | bytes 131104 | tf_op jit(solution)/shard_map/all_to_all | solution.py:71
  88.6 0.1 copy.19
  88.7 0.7 slice_bitcast_fusion.5
  (6 shorter events, 0.2 us)
Async XLA Ops:
  2.2 11.8 %all-to-all-start = ((bf16[8,64,128]{2,1,0:T(8,128)(2,1)}), bf16[8,64,128]{2,1,0:T(8,128)(2,1)S(1)}, u32[]{:S(2)}, u32[]{:S(2)}) async-start(bf16[8,64,128]{2,1,0:T(8,128)(2,1)} %pad_maximum_fusion.1), calls=%async_computation | async-start | bytes 262144 | tf_op jit(solution)/shard_map/all_to_all | solution.py:71
  10.4 27.6 %copy-start.2 = (s32[4096]{0:T(1024)S(1)}, s32[4096]{0:T(1024)}, u32[]{:S(2)}) copy-start(s32[4096]{0:T(1024)} %param.12) | copy-start | bytes 49156
  10.4 29.0 %copy-start = (s32[128]{0:T(128)S(1)}, s32[128]{0:T(128)}, u32[]{:S(2)}) copy-start(s32[128]{0:T(128)} %span_ref.1) | copy-start | bytes 1540
  14.0 1.3 %collective-permute-start = (bf16[8,64,128]{2,1,0:T(8,128)(2,1)S(1)}, bf16[8,64,128]{2,1,0:T(8,128)(2,1)S(1)}, u32[]{:S(2)}, u32[]{:S(2)}) collective-permute-start(bf16[8,64,128]{2,1,0:T(8,128)(2,1)S(1)} %all-to-all-done.kv0_ref), channel_id=1, source_target_pairs={{0,16},{1,17},{2,18},{3,19},{4,20},{5,21},{6,22},{7,23},{8,24},{9,... | collective-permute-start | bytes 393224 | tf_op jit(solution)/shard_map/ppermute | solution.py:67
  15.3 24.0 %all-to-all-start.1 = ((bf16[8,528,128]{2,1,0:T(8,128)(2,1)}), bf16[8,528,128]{2,1,0:T(8,128)(2,1)S(1)}, u32[]{:S(2)}, u32[]{:S(2)}) async-start(bf16[8,528,128]{2,1,0:T(8,128)(2,1)} %pack_q.1), calls=%async_computation.1 | async-start | bytes 2162688 | tf_op jit(solution)/shard_map/all_to_all | solution.py:71
  18.9 9.1 %collective-permute-start.3 = (bf16[2,8,64,128]{3,2,1,0:T(8,128)(2,1)S(1)}, bf16[2,8,64,128]{3,2,1,0:T(8,128)(2,1)S(1)}, u32[]{:S(2)}, u32[]{:S(2)}) collective-permute-start(bf16[2,8,64,128]{3,2,1,0:T(8,128)(2,1)S(1)} %pad_maximum_fusion), channel_id=1, source_target_pairs={{0,7},{2,5},{1,6},{3,4},{4,3},{6,1},{5,2},{7,0},{8,15},{10,13},{9,... | collective-permute-start | bytes 786440 | tf_op jit(solution)/shard_map/ppermute | solution.py:439
  22.6 14.7 %collective-permute-start.2 = (bf16[2,8,64,128]{3,2,1,0:T(8,128)(2,1)S(1)}, bf16[2,8,64,128]{3,2,1,0:T(8,128)(2,1)S(1)}, u32[]{:S(2)}, u32[]{:S(2)}) collective-permute-start(bf16[2,8,64,128]{3,2,1,0:T(8,128)(2,1)S(1)} %pad_maximum_fusion), channel_id=1, source_target_pairs={{0,12},{2,14},{1,13},{3,15},{4,8},{6,10},{5,9},{7,11},{8,4},{10,6}... | collective-permute-start | bytes 786440 | tf_op jit(solution)/shard_map/ppermute | solution.py:439
  25.1 12.2 %collective-permute-start.1 = (bf16[2,8,64,128]{3,2,1,0:T(8,128)(2,1)S(1)}, bf16[2,8,64,128]{3,2,1,0:T(8,128)(2,1)S(1)}, u32[]{:S(2)}, u32[]{:S(2)}) collective-permute-start(bf16[2,8,64,128]{3,2,1,0:T(8,128)(2,1)S(1)} %pad_maximum_fusion), channel_id=1, source_target_pairs={{0,4},{2,6},{1,5},{3,7},{4,0},{6,2},{5,1},{7,3},{8,12},{10,14},{9,... | collective-permute-start | bytes 786440 | tf_op jit(solution)/shard_map/ppermute | solution.py:439
  26.1 11.7 %collective-permute-start.4 = (bf16[8,64,128]{2,1,0:T(8,128)(2,1)S(1)}, bf16[8,64,128]{2,1,0:T(8,128)(2,1)S(1)}, u32[]{:S(2)}, u32[]{:S(2)}) collective-permute-start(bf16[8,64,128]{2,1,0:T(8,128)(2,1)S(1)} %all-to-all-done.kv0_ref), channel_id=1, source_target_pairs={{0,15},{2,13},{1,14},{3,12},{4,11},{6,9},{5,10},{7,8},{8,7},{10,5}... | collective-permute-start | bytes 393224 | tf_op jit(solution)/shard_map/ppermute | solution.py:440
  28.0 11.3 %collective-permute-start.7 = (bf16[2,8,64,128]{3,2,1,0:T(8,128)(2,1)S(1)}, bf16[2,8,64,128]{3,2,1,0:T(8,128)(2,1)S(1)}, u32[]{:S(2)}, u32[]{:S(2)}) collective-permute-start(bf16[2,8,64,128]{3,2,1,0:T(8,128)(2,1)S(1)} %collective-permute-done.3.mine2_ref), channel_id=1, source_target_pairs={{0,16},{1,17},{2,18},{3,19},{4,20},{5,21},{6,22},{7,23},{8,24},{9,... | collective-permute-start | bytes 786440 | tf_op jit(solution)/shard_map/ppermute | solution.py:67
  37.2 2.1 %collective-permute-start.6 = (bf16[2,8,64,128]{3,2,1,0:T(8,128)(2,1)S(1)}, bf16[2,8,64,128]{3,2,1,0:T(8,128)(2,1)S(1)}, u32[]{:S(2)}, u32[]{:S(2)}) collective-permute-start(bf16[2,8,64,128]{3,2,1,0:T(8,128)(2,1)S(1)} %collective-permute-done.2.mine1_ref), channel_id=1, source_target_pairs={{0,16},{1,17},{2,18},{3,19},{4,20},{5,21},{6,22},{7,23},{8,24},{9,... | collective-permute-start | bytes 786440 | tf_op jit(solution)/shard_map/ppermute | solution.py:67
  37.2 2.1 %collective-permute-start.5 = (bf16[2,8,64,128]{3,2,1,0:T(8,128)(2,1)S(1)}, bf16[2,8,64,128]{3,2,1,0:T(8,128)(2,1)S(1)}, u32[]{:S(2)}, u32[]{:S(2)}) collective-permute-start(bf16[2,8,64,128]{3,2,1,0:T(8,128)(2,1)S(1)} %collective-permute-done.1.mine0_ref), channel_id=1, source_target_pairs={{0,16},{1,17},{2,18},{3,19},{4,20},{5,21},{6,22},{7,23},{8,24},{9,... | collective-permute-start | bytes 786440 | tf_op jit(solution)/shard_map/ppermute | solution.py:67
  37.8 1.6 %collective-permute-start.8 = (bf16[8,64,128]{2,1,0:T(8,128)(2,1)S(1)}, bf16[8,64,128]{2,1,0:T(8,128)(2,1)S(1)}, u32[]{:S(2)}, u32[]{:S(2)}) collective-permute-start(bf16[8,64,128]{2,1,0:T(8,128)(2,1)S(1)} %collective-permute-done.4.mine3_ref), channel_id=1, source_target_pairs={{0,16},{1,17},{2,18},{3,19},{4,20},{5,21},{6,22},{7,23},{8,24},{9,... | collective-permute-start | bytes 393224 | tf_op jit(solution)/shard_map/ppermute | solution.py:67
  50.5 3.5 %collective-permute-start.9 = (bf16[8,8,64,128]{3,2,1,0:T(8,128)(2,1)S(1)}, bf16[8,8,64,128]{3,2,1,0:T(8,128)(2,1)S(1)}, u32[]{:S(2)}, u32[]{:S(2)}) collective-permute-start(bf16[8,8,64,128]{3,2,1,0:T(8,128)(2,1)S(1)} %get-tuple-element.18), channel_id=1, source_target_pairs={{0,16},{1,17},{2,18},{3,19},{4,20},{5,21},{6,22},{7,23},{8,24},{9,... | collective-permute-start | bytes 3145736 | tf_op jit(solution)/shard_map/ppermute | solution.py:67
  54.5 13.6 %collective-permute-start.11 = (bf16[2,8,64,128]{3,2,1,0:T(8,128)(2,1)S(1)}, bf16[2,8,64,128]{3,2,1,0:T(8,128)(2,1)S(1)}, u32[]{:S(2)}, u32[]{:S(2)}) collective-permute-start(bf16[2,8,64,128]{3,2,1,0:T(8,128)(2,1)S(1)} %get-tuple-element.23), channel_id=1, source_target_pairs={{0,4},{2,6},{1,5},{3,7},{4,0},{6,2},{5,1},{7,3},{8,12},{10,14},{9,... | collective-permute-start | bytes 786440 | tf_op jit(solution)/shard_map/ppermute | solution.py:446
  54.6 13.6 %collective-permute-start.13 = (bf16[2,8,64,128]{3,2,1,0:T(8,128)(2,1)S(1)}, bf16[2,8,64,128]{3,2,1,0:T(8,128)(2,1)S(1)}, u32[]{:S(2)}, u32[]{:S(2)}) collective-permute-start(bf16[2,8,64,128]{3,2,1,0:T(8,128)(2,1)S(1)} %get-tuple-element.24), channel_id=1, source_target_pairs={{0,7},{2,5},{1,6},{3,4},{4,3},{6,1},{5,2},{7,0},{8,15},{10,13},{9,... | collective-permute-start | bytes 786440 | tf_op jit(solution)/shard_map/ppermute | solution.py:446
  61.0 8.5 %collective-permute-start.12 = (bf16[2,8,64,128]{3,2,1,0:T(8,128)(2,1)S(1)}, bf16[2,8,64,128]{3,2,1,0:T(8,128)(2,1)S(1)}, u32[]{:S(2)}, u32[]{:S(2)}) collective-permute-start(bf16[2,8,64,128]{3,2,1,0:T(8,128)(2,1)S(1)} %get-tuple-element.25), channel_id=1, source_target_pairs={{0,12},{2,14},{1,13},{3,15},{4,8},{6,10},{5,9},{7,11},{8,4},{10,6}... | collective-permute-start | bytes 786440 | tf_op jit(solution)/shard_map/ppermute | solution.py:446
  61.0 15.5 %all-to-all-start.2 = ((bf16[8,256,128]{2,1,0:T(8,128)(2,1)}), bf16[8,256,128]{2,1,0:T(8,128)(2,1)S(1)}, u32[]{:S(2)}, u32[]{:S(2)}) async-start(bf16[8,256,128]{2,1,0:T(8,128)(2,1)} %get-tuple-element.19), calls=%async_computation.2 | async-start | bytes 1048576 | tf_op jit(solution)/shard_map/all_to_all | solution.py:71
  65.5 9.7 %collective-permute-start.10 = (bf16[8,64,128]{2,1,0:T(8,128)(2,1)S(1)}, bf16[8,64,128]{2,1,0:T(8,128)(2,1)S(1)}, u32[]{:S(2)}, u32[]{:S(2)}) collective-permute-start(bf16[8,64,128]{2,1,0:T(8,128)(2,1)S(1)} %slice_bitcast_fusion.3), channel_id=1, source_target_pairs={{0,15},{2,13},{1,14},{3,12},{4,11},{6,9},{5,10},{7,8},{8,7},{10,5}... | collective-permute-start | bytes 393224 | tf_op jit(solution)/shard_map/ppermute | solution.py:449
  76.5 5.6 %copy-start.1 = (bf16[8,256,128]{2,1,0:T(8,128)(2,1)}, bf16[8,256,128]{2,1,0:T(8,128)(2,1)S(1)}, u32[]{:S(2)}) copy-start(bf16[8,256,128]{2,1,0:T(8,128)(2,1)S(1)} %all-to-all-done.2.back_ref) | copy-start | bytes 1572868
  76.5 1.5 %collective-permute-start.14 = (f32[8,64,128]{2,1,0:T(8,128)S(1)}, f32[8,64,128]{2,1,0:T(8,128)S(1)}, u32[]{:S(2)}, u32[]{:S(2)}) collective-permute-start(f32[8,64,128]{2,1,0:T(8,128)S(1)} %fusion), channel_id=1, source_target_pairs={{0,16},{1,17},{2,18},{3,19},{4,20},{5,21},{6,22},{7,23},{8,24},{9,... | collective-permute-start | bytes 786440 | tf_op jit(solution)/shard_map/ppermute | solution.py:67
  78.8 9.9 %all-to-all-start.3 = ((bf16[8,64,128]{2,1,0:T(8,128)(2,1)}), bf16[8,64,128]{2,1,0:T(8,128)(2,1)S(1)}, u32[]{:S(2)}, u32[]{:S(2)}) async-start(bf16[8,64,128]{2,1,0:T(8,128)(2,1)} %add_convert_fusion.1), calls=%async_computation.3 | async-start | bytes 262144 | tf_op jit(solution)/shard_map/all_to_all | solution.py:71
